TPU v7x, 32 devices: a whole 2x2x4 slice. The times are simulated.
32 devices in a mesh: batch: 8 (over z, y), seq: 4 (over x, core).
Axes of the slice: x: 2, y: 2, z: 4, core: 2. Of those that a mesh axis runs over, the one named last changes fastest.
Arguments:
- tokens: bfloat16 [16, 2048, 512], P('batch', 'seq'), may hold values from -6 to 6
- memory: bfloat16 [16, 64, 512], P('batch', 'seq'), may hold values from -6 to 6
- lengths: int32 [16, 8], P('batch'), may hold values from 1 to 1538, 2048 in all within a row
- resets: int32 [16, 4], P('batch'), may hold values 0 or 1
- attn_in: bfloat16 [786432], P(('batch', 'seq')), may hold values from -0.25 to 0.25
- attn_out: bfloat16 [262144], P(('batch', 'seq')), may hold values from -1 to 1
- ffn_in: bfloat16 [1048576], P(('batch', 'seq')), may hold values from -0.25 to 0.25
- ffn_out: bfloat16 [1048576], P(('batch', 'seq')), may hold values from -0.125 to 0.125
- writer_in: bfloat16 [524288], P(('batch', 'seq')), may hold values from -0.1875 to 0.1875
- writer_value: bfloat16 [262144], P(('batch', 'seq')), may hold values from -2 to 2
- norm_gains: bfloat16 [1024], P(('batch', 'seq')), may hold values from 0.5 to 1.5
- memory_init: bfloat16 [32768], P(('batch', 'seq')), may hold values from -6 to 6
- out_cotangent: bfloat16 [16, 2048, 512], P('batch', 'seq'), may hold values from -6 to 6
- memory_cotangent: bfloat16 [16, 64, 512], P('batch', 'seq'), may hold values from -6 to 6
Outputs:
- output: bfloat16 [16, 2048, 512], P('batch', 'seq')
- new_memory: bfloat16 [16, 64, 512], P('batch', 'seq')
- tokens_grad: bfloat16 [16, 2048, 512], P('batch', 'seq')
- memory_grad: bfloat16 [16, 64, 512], P('batch', 'seq')
- attn_in_grad: float32 [786432], P(('batch', 'seq'))
- attn_out_grad: float32 [262144], P(('batch', 'seq'))
- ffn_in_grad: float32 [1048576], P(('batch', 'seq'))
- ffn_out_grad: float32 [1048576], P(('batch', 'seq'))
- writer_in_grad: float32 [524288], P(('batch', 'seq'))
- writer_value_grad: float32 [262144], P(('batch', 'seq'))
- norm_gains_grad: float32 [1024], P(('batch', 'seq'))
- memory_init_grad: float32 [32768], P(('batch', 'seq'))
Inputs may be any that keep to these rules, and one draw needn't show every extreme that they name: `lengths`: each row sums to 2048; its longest document is exactly 1538 tokens.
All inputs are finite; a program needn't handle non-finite values. No bound on the sum of `resets` on one device may be relied on, other than what follows from the above.
Results may differ from a plain program's by a relative error of at most 0.028.
Values may be sent and summed in bfloat16 or wider, within the bound.
No kernel may reach another device: no remote copies, remote signals or barrier semaphores. Data moves between devices by JAX's collectives and lax.ppermute only.
A program may use at most 256 MiB of HBM per device.

v0:
```python
import jax
import jax.numpy as jnp
from jax import lax
from jax.sharding import PartitionSpec as P

HEADS = 8
HEAD_DIM = 64
FF = 2048
SEGMENT = 512


MASKED = -1e30


def joined(array, axis, combine):
    everything = jax.tree.map(
        lambda part, kind: lax.all_gather(part.astype(kind), axis),
        array,
        (jnp.bfloat16, jnp.bfloat16, jnp.bfloat16),
    )

    def take(k):
        return jax.tree.map(lambda part, own: part[k].astype(own.dtype), everything, array)

    return lax.fori_loop(
        1, lax.axis_size(axis), lambda k, so_far: combine(so_far, take(k)), take(0)
    )


def normalize(values, gain):
    centred = values - jnp.mean(values, axis=-1, keepdims=True)
    spread = jnp.mean(centred * centred, axis=-1, keepdims=True)
    return centred * lax.rsqrt(spread + 1e-05) * gain


def split_into_heads(values):
    return values.reshape(values.shape[0], HEADS, -1).transpose(1, 0, 2)


def merge_head_axis(values):
    return values.transpose(1, 0, 2).reshape(values.shape[1], -1)


def doc_numbers(positions, doc_ends):
    return jnp.sum((positions[:, None] >= doc_ends[None, :]).astype(jnp.int32), axis=1)


def unite(former, latter):
    highest = jnp.maximum(former[0], latter[0])
    former_scale = jnp.exp(former[0] - highest)
    latter_scale = jnp.exp(latter[0] - highest)
    return (
        highest,
        former[1] * former_scale + latter[1] * latter_scale,
        former[2] * former_scale[..., None] + latter[2] * latter_scale[..., None],
    )


def product(inputs, weight):
    return jnp.dot(inputs, weight, preferred_element_type=jnp.float32)


def product_back(inputs, weight):
    return lax.dot_general(
        inputs, weight, (((1,), (1,)), ((), ())), preferred_element_type=jnp.float32
    )


def outer_sum(inputs, grads):
    return lax.dot_general(
        inputs, grads, (((0,), (0,)), ((), ())), preferred_element_type=jnp.float32
    )


def unpack(pieces, width):
    return (
        pieces[0].reshape(3, width, width),
        pieces[1].reshape(width, width),
        pieces[2].reshape(width, -1),
        pieces[3].reshape(-1, width),
        pieces[4].reshape(2, width, width),
        pieces[5].reshape(width, width),
        pieces[6].reshape(2, width),
        pieces[7].reshape(-1, width),
    )


def per_device(
    tokens,
    memory,
    lengths,
    resets,
    attn_in,
    attn_out,
    ffn_in,
    ffn_out,
    writer_in,
    writer_value,
    norm_gains,
    memory_init,
    out_cotangent,
    memory_cotangent,
):
    micro_count, tok_rows, width = tokens.shape
    seq_count = lax.axis_size("seq")
    seq_rank = lax.axis_index("seq")
    slot_part = memory.shape[1]
    slots = slot_part * seq_count
    seq_len = tok_rows * seq_count
    logit_scale_factor = HEAD_DIM ** (-0.5)
    positions = seq_rank * tok_rows + jnp.arange(tok_rows, dtype=jnp.int32)
    segment_of = positions // SEGMENT
    segment_ids = jnp.arange(resets.shape[1], dtype=jnp.int32)
    slot_half = (jnp.arange(2 * slots, dtype=jnp.int32) >= slots).astype(jnp.int32)
    slot_start = seq_rank * slot_part
    grad_qkv = jnp.zeros((3, width, width), jnp.float32)
    grad_out = jnp.zeros((width, width), jnp.float32)
    grad_up = jnp.zeros((width, FF), jnp.float32)
    grad_down = jnp.zeros((FF, width), jnp.float32)
    grad_write = jnp.zeros((2, width, width), jnp.float32)
    grad_value = jnp.zeros((width, width), jnp.float32)
    grad_gains = jnp.zeros((2, width), jnp.float32)
    grad_init = jnp.zeros((slots, width), jnp.float32)
    outputs, new_rows, token_grads, memory_grads = ([], [], [], [])
    for micro_index in range(micro_count):
        weights = unpack(
            (
                lax.all_gather(attn_in, ("batch", "seq"), axis=0, tiled=True),
                lax.all_gather(attn_out, ("batch", "seq"), axis=0, tiled=True),
                lax.all_gather(ffn_in, ("batch", "seq"), axis=0, tiled=True),
                lax.all_gather(ffn_out, ("batch", "seq"), axis=0, tiled=True),
                lax.all_gather(writer_in, ("batch", "seq"), axis=0, tiled=True),
                lax.all_gather(writer_value, ("batch", "seq"), axis=0, tiled=True),
                lax.all_gather(norm_gains, ("batch", "seq"), axis=0, tiled=True),
                lax.all_gather(memory_init, ("batch", "seq"), axis=0, tiled=True),
            ),
            width,
        )
        w_qkv, w_out, w_up, w_down, w_write, w_value, gains, init_rows = weights
        gain_one = gains[0].astype(jnp.float32)
        gain_two = gains[1].astype(jnp.float32)
        doc_ends = jnp.cumsum(lengths[micro_index])
        my_docs = doc_numbers(positions, doc_ends)
        token_reset = jnp.sum(
            jnp.where(segment_of[:, None] == segment_ids[None, :], resets[micro_index][None, :], 0),
            axis=1,
        )
        slot_allowed = (slot_half[None, :] == token_reset[:, None])[None]
        inputs = tokens[micro_index].astype(jnp.float32)
        mem_rows, mem_cot = (
            lax.all_gather(memory[micro_index], "seq", axis=0, tiled=True),
            lax.all_gather(memory_cotangent[micro_index], "seq", axis=0, tiled=True),
        )
        normed = normalize(inputs, gain_one)
        normed_low = normed.astype(jnp.bfloat16)
        qkv_rows = jnp.einsum(
            "td,cde->cte", normed_low, w_qkv, preferred_element_type=jnp.float32
        ).astype(jnp.bfloat16)
        queries, keys, values = (qkv_rows[0], qkv_rows[1], qkv_rows[2])
        slot_source = jnp.concatenate([mem_rows, init_rows], axis=0)
        slot_kv = jnp.einsum(
            "sd,cde->cse", slot_source, w_qkv[1:], preferred_element_type=jnp.float32
        ).astype(jnp.bfloat16)
        query_heads = split_into_heads(queries)
        slot_keys = split_into_heads(slot_kv[0])
        slot_values = split_into_heads(slot_kv[1])
        slot_scores = (
            jnp.einsum("htd,hsd->hts", query_heads, slot_keys, preferred_element_type=jnp.float32)
            * logit_scale_factor
        )
        slot_scores = jnp.where(slot_allowed, slot_scores, MASKED)
        start_max = jnp.max(slot_scores, axis=-1)
        start_exp = jnp.exp(slot_scores - start_max[..., None])
        start_total = jnp.sum(start_exp, axis=-1)
        start_acc = jnp.einsum(
            "hts,hsd->htd",
            start_exp.astype(jnp.bfloat16),
            slot_values,
            preferred_element_type=jnp.float32,
        )

        def token_mask(count):
            key_pos = jnp.arange(count, dtype=jnp.int32)
            key_docs = doc_numbers(key_pos, doc_ends)
            return (
                (my_docs[:, None] == key_docs[None, :]) & (key_pos[None, :] <= positions[:, None])
            )[None]

        run_max = start_max
        run_total = start_total
        run_acc = start_acc
        key_piece = lax.all_gather(keys, "seq", axis=0, tiled=True)
        value_piece = lax.all_gather(values, "seq", axis=0, tiled=True)
        attend_count = key_piece.shape[0]
        scores = (
            jnp.einsum(
                "htd,hkd->htk",
                query_heads,
                split_into_heads(key_piece),
                preferred_element_type=jnp.float32,
            )
            * logit_scale_factor
        )
        scores = jnp.where(token_mask(attend_count), scores, MASKED)
        new_max = jnp.maximum(run_max, jnp.max(scores, axis=-1))
        carried = jnp.exp(run_max - new_max)
        expo = jnp.exp(scores - new_max[..., None])
        run_total = run_total * carried + jnp.sum(expo, axis=-1)
        run_acc = run_acc * carried[..., None] + jnp.einsum(
            "htk,hkd->htd",
            expo.astype(jnp.bfloat16),
            split_into_heads(value_piece),
            preferred_element_type=jnp.float32,
        )
        run_max, run_total, run_acc = (new_max, run_total, run_acc)
        attn_full = run_acc / run_total[..., None]
        log_total = run_max + jnp.log(run_total)
        attended = merge_head_axis(attn_full).astype(jnp.bfloat16)
        middle = inputs + product(attended, w_out)
        normed_two = normalize(middle, gain_two)
        normed_two_low = normed_two.astype(jnp.bfloat16)
        hidden_pre = product(normed_two_low, w_up)
        activated = jax.nn.gelu(hidden_pre).astype(jnp.bfloat16)
        result = middle + product(activated, w_down)
        result_low = result.astype(jnp.bfloat16)
        outputs.append(result_low)
        write_keys = product(result_low, w_write[1]).astype(jnp.bfloat16)
        write_values = product(result_low, w_value).astype(jnp.bfloat16)
        slot_queries = product(mem_rows, w_write[0]).astype(jnp.bfloat16)
        token_self_keys = product(mem_rows, w_write[1]).astype(jnp.bfloat16)
        self_values = product(mem_rows, w_value).astype(jnp.bfloat16)
        wkey_heads = split_into_heads(write_keys)
        wvalue_heads = split_into_heads(write_values)
        slot_query_heads = split_into_heads(slot_queries)
        slot_key_heads = split_into_heads(token_self_keys)
        svalue_heads = split_into_heads(self_values)
        read_scores = (
            jnp.einsum(
                "hsd,htd->hst", slot_query_heads, wkey_heads, preferred_element_type=jnp.float32
            )
            * logit_scale_factor
        )
        local_max = jnp.max(read_scores, axis=-1)
        local_exp = jnp.exp(read_scores - local_max[..., None])
        local_total = jnp.sum(local_exp, axis=-1)
        local_sum = jnp.einsum(
            "hst,htd->hsd",
            local_exp.astype(jnp.bfloat16),
            wvalue_heads,
            preferred_element_type=jnp.float32,
        )
        merged_max, merged_total, merged_sum = joined(
            (local_max, local_total, local_sum), "seq", unite
        )
        self_scores = (
            jnp.sum(
                slot_query_heads.astype(jnp.float32) * slot_key_heads.astype(jnp.float32), axis=-1
            )
            * logit_scale_factor
        )
        highest = jnp.maximum(merged_max, self_scores)
        kept_share = jnp.exp(merged_max - highest)
        self_weight = jnp.exp(self_scores - highest)
        denominator = merged_total * kept_share + self_weight
        written = (
            merged_sum * kept_share[..., None]
            + self_weight.astype(jnp.bfloat16).astype(jnp.float32)[..., None]
            * svalue_heads.astype(jnp.float32)
        ) / denominator[..., None]
        new_full = mem_rows.astype(jnp.float32) + merge_head_axis(written)
        new_rows.append(
            lax.dynamic_slice_in_dim(new_full, slot_start, slot_part, 0).astype(jnp.bfloat16)
        )
        write_log = highest + jnp.log(denominator)
        read_probs = jnp.exp(read_scores - write_log[..., None])
        self_probs = jnp.exp(self_scores - write_log)
        cot_heads = split_into_heads(mem_cot)
        cot_full = cot_heads.astype(jnp.float32)
        write_delta = jnp.sum(cot_full * written, axis=-1)
        read_dp = jnp.einsum(
            "hsd,htd->hst", cot_heads, wvalue_heads, preferred_element_type=jnp.float32
        )
        read_ds = (read_probs * (read_dp - write_delta[..., None])).astype(jnp.bfloat16)
        self_dp = jnp.sum(cot_full * svalue_heads.astype(jnp.float32), axis=-1)
        self_score_grad = (
            (self_probs * (self_dp - write_delta)).astype(jnp.bfloat16).astype(jnp.float32)
        )
        d_wvalues = merge_head_axis(
            jnp.einsum(
                "hst,hsd->htd",
                read_probs.astype(jnp.bfloat16),
                cot_heads,
                preferred_element_type=jnp.float32,
            )
        ).astype(jnp.bfloat16)
        d_wkeys = merge_head_axis(
            jnp.einsum(
                "hst,hsd->htd", read_ds, slot_query_heads, preferred_element_type=jnp.float32
            )
            * logit_scale_factor
        ).astype(jnp.bfloat16)
        dquery_part = merge_head_axis(
            jnp.einsum("hst,htd->hsd", read_ds, wkey_heads, preferred_element_type=jnp.float32)
            * logit_scale_factor
        )
        query_self_grad = merge_head_axis(
            self_score_grad[..., None] * slot_key_heads.astype(jnp.float32) * logit_scale_factor
        )
        dskeys = merge_head_axis(
            self_score_grad[..., None] * slot_query_heads.astype(jnp.float32) * logit_scale_factor
        )
        dsvalues = merge_head_axis(
            self_probs.astype(jnp.bfloat16).astype(jnp.float32)[..., None] * cot_full
        )
        grad_write = grad_write.at[1].add(outer_sum(result_low, d_wkeys))
        grad_value = grad_value + outer_sum(result_low, d_wvalues)
        d_result = (
            out_cotangent[micro_index].astype(jnp.float32)
            + product_back(d_wkeys, w_write[1])
            + product_back(d_wvalues, w_value)
        )
        d_update = d_result.astype(jnp.bfloat16)
        grad_down = grad_down + outer_sum(activated, d_update)
        d_activated = product_back(d_update, w_down)
        gelu_pull = jax.vjp(jax.nn.gelu, hidden_pre)[1]
        d_hidden = gelu_pull(d_activated)[0].astype(jnp.bfloat16)
        grad_up = grad_up + outer_sum(normed_two_low, d_hidden)
        d_normed_two = product_back(d_hidden, w_up)
        norm_pull_two = jax.vjp(normalize, middle, gain_two)[1]
        d_middle_norm, d_gain_two = norm_pull_two(d_normed_two)
        d_middle = d_result + d_middle_norm
        grad_gains = grad_gains.at[1].add(d_gain_two)
        d_branch = d_middle.astype(jnp.bfloat16)
        grad_out = grad_out + outer_sum(attended, d_branch)
        d_attended = product_back(d_branch, w_out).astype(jnp.bfloat16)
        dattn_heads = split_into_heads(d_attended)
        attn_delta = jnp.sum(dattn_heads.astype(jnp.float32) * attn_full, axis=-1)
        slot_probs = jnp.exp(slot_scores - log_total[..., None])
        slot_dp = jnp.einsum(
            "htd,hsd->hts", dattn_heads, slot_values, preferred_element_type=jnp.float32
        )
        slot_ds = (slot_probs * (slot_dp - attn_delta[..., None])).astype(jnp.bfloat16)
        start_dq = (
            jnp.einsum("hts,hsd->htd", slot_ds, slot_keys, preferred_element_type=jnp.float32)
            * logit_scale_factor
        )
        d_slot_keys = merge_head_axis(
            jnp.einsum("hts,htd->hsd", slot_ds, query_heads, preferred_element_type=jnp.float32)
            * logit_scale_factor
        )
        d_slot_values = merge_head_axis(
            jnp.einsum(
                "hts,htd->hsd",
                slot_probs.astype(jnp.bfloat16),
                dattn_heads,
                preferred_element_type=jnp.float32,
            )
        )
        slot_terms = jnp.stack(
            [
                d_slot_keys[:slots],
                d_slot_keys[slots:],
                d_slot_values[:slots],
                d_slot_values[slots:],
                dquery_part,
            ]
        )

        def attend_back(carry, piece):
            run_dq, key_value_grads = carry
            key_piece, value_piece = piece
            count = key_piece.shape[0]
            kpiece_heads = split_into_heads(key_piece)
            scores = (
                jnp.einsum(
                    "htd,hkd->htk", query_heads, kpiece_heads, preferred_element_type=jnp.float32
                )
                * logit_scale_factor
            )
            scores = jnp.where(token_mask(count), scores, MASKED)
            probs = jnp.exp(scores - log_total[..., None])
            dprobs = jnp.einsum(
                "htd,hkd->htk",
                dattn_heads,
                split_into_heads(value_piece),
                preferred_element_type=jnp.float32,
            )
            dscores = (probs * (dprobs - attn_delta[..., None])).astype(jnp.bfloat16)
            run_dq = (
                run_dq
                + jnp.einsum(
                    "htk,hkd->htd", dscores, kpiece_heads, preferred_element_type=jnp.float32
                )
                * logit_scale_factor
            )
            dkey_piece = merge_head_axis(
                jnp.einsum("htk,htd->hkd", dscores, query_heads, preferred_element_type=jnp.float32)
                * logit_scale_factor
            )
            dvalue_piece = merge_head_axis(
                jnp.einsum(
                    "htk,htd->hkd",
                    probs.astype(jnp.bfloat16),
                    dattn_heads,
                    preferred_element_type=jnp.float32,
                )
            )
            key_value_grads = jnp.stack([dkey_piece, dvalue_piece])
            return (run_dq, key_value_grads)

        run_dq, key_value_grads = attend_back(
            (start_dq, jnp.zeros((2, seq_len, width), jnp.float32)),
            (
                lax.all_gather(keys, "seq", axis=0, tiled=True),
                lax.all_gather(values, "seq", axis=0, tiled=True),
            ),
        )
        my_kv_grads, my_slot_terms = (
            lax.psum_scatter(
                key_value_grads.astype(jnp.bfloat16), "seq", scatter_dimension=1, tiled=True
            ).astype(jnp.float32),
            lax.psum_scatter(
                slot_terms.astype(jnp.bfloat16), "seq", scatter_dimension=1, tiled=True
            ).astype(jnp.float32),
        )
        d_qkv = jnp.stack([merge_head_axis(run_dq), my_kv_grads[0], my_kv_grads[1]]).astype(
            jnp.bfloat16
        )
        grad_qkv = grad_qkv + jnp.einsum(
            "td,cte->cde", normed_low, d_qkv, preferred_element_type=jnp.float32
        )
        d_normed = jnp.einsum("cte,cde->td", d_qkv, w_qkv, preferred_element_type=jnp.float32)
        norm_pull_one = jax.vjp(normalize, inputs, gain_one)[1]
        d_inputs_norm, d_gain_one = norm_pull_one(d_normed)
        grad_gains = grad_gains.at[0].add(d_gain_one)
        token_grads.append((d_middle + d_inputs_norm).astype(jnp.bfloat16))
        mem_mine = memory[micro_index]
        init_mine = lax.dynamic_slice_in_dim(init_rows, slot_start, slot_part, 0)
        dkey_mem = my_slot_terms[0].astype(jnp.bfloat16)
        dkey_init = my_slot_terms[1].astype(jnp.bfloat16)
        dvalue_mem = my_slot_terms[2].astype(jnp.bfloat16)
        dvalue_init = my_slot_terms[3].astype(jnp.bfloat16)
        dquery_total = (
            my_slot_terms[4] + lax.dynamic_slice_in_dim(query_self_grad, slot_start, slot_part, 0)
        ).astype(jnp.bfloat16)
        dskey_mine = lax.dynamic_slice_in_dim(dskeys, slot_start, slot_part, 0).astype(jnp.bfloat16)
        dsvalue_mine = lax.dynamic_slice_in_dim(dsvalues, slot_start, slot_part, 0).astype(
            jnp.bfloat16
        )
        cot_mine = lax.dynamic_slice_in_dim(mem_cot, slot_start, slot_part, 0).astype(jnp.float32)
        d_memory = (
            cot_mine
            + product_back(dkey_mem, w_qkv[1])
            + product_back(dvalue_mem, w_qkv[2])
            + product_back(dquery_total, w_write[0])
            + product_back(dskey_mine, w_write[1])
            + product_back(dsvalue_mine, w_value)
        )
        memory_grads.append(d_memory.astype(jnp.bfloat16))
        d_init = product_back(dkey_init, w_qkv[1]) + product_back(dvalue_init, w_qkv[2])
        grad_init = lax.dynamic_update_slice_in_dim(
            grad_init,
            lax.dynamic_slice_in_dim(grad_init, slot_start, slot_part, 0) + d_init,
            slot_start,
            0,
        )
        grad_qkv = grad_qkv.at[1].add(
            outer_sum(mem_mine, dkey_mem) + outer_sum(init_mine, dkey_init)
        )
        grad_qkv = grad_qkv.at[2].add(
            outer_sum(mem_mine, dvalue_mem) + outer_sum(init_mine, dvalue_init)
        )
        grad_write = grad_write.at[0].add(outer_sum(mem_mine, dquery_total))
        grad_write = grad_write.at[1].add(outer_sum(mem_mine, dskey_mine))
        grad_value = grad_value + outer_sum(mem_mine, dsvalue_mine)
    summed = (
        lax.psum_scatter(grad_qkv.reshape(-1), ("batch", "seq"), scatter_dimension=0, tiled=True),
        lax.psum_scatter(grad_out.reshape(-1), ("batch", "seq"), scatter_dimension=0, tiled=True),
        lax.psum_scatter(grad_up.reshape(-1), ("batch", "seq"), scatter_dimension=0, tiled=True),
        lax.psum_scatter(grad_down.reshape(-1), ("batch", "seq"), scatter_dimension=0, tiled=True),
        lax.psum_scatter(grad_write.reshape(-1), ("batch", "seq"), scatter_dimension=0, tiled=True),
        lax.psum_scatter(grad_value.reshape(-1), ("batch", "seq"), scatter_dimension=0, tiled=True),
        lax.psum_scatter(grad_gains.reshape(-1), ("batch", "seq"), scatter_dimension=0, tiled=True),
        lax.psum_scatter(grad_init.reshape(-1), ("batch", "seq"), scatter_dimension=0, tiled=True),
    )
    return (
        jnp.stack(outputs),
        jnp.stack(new_rows),
        jnp.stack(token_grads),
        jnp.stack(memory_grads),
        summed[0],
        summed[1],
        summed[2],
        summed[3],
        summed[4],
        summed[5],
        summed[6],
        summed[7],
    )


def solution(mesh):
    placed = (
        P("batch", "seq", None),
        P("batch", "seq", None),
        P("batch", None),
        P("batch", None),
        P(("batch", "seq")),
        P(("batch", "seq")),
        P(("batch", "seq")),
        P(("batch", "seq")),
        P(("batch", "seq")),
        P(("batch", "seq")),
        P(("batch", "seq")),
        P(("batch", "seq")),
        P("batch", "seq", None),
        P("batch", "seq", None),
    )
    return jax.shard_map(
        per_device,
        mesh=mesh,
        in_specs=placed,
        out_specs=(
            P("batch", "seq", None),
            P("batch", "seq", None),
            P("batch", "seq", None),
            P("batch", "seq", None),
            P(("batch", "seq")),
            P(("batch", "seq")),
            P(("batch", "seq")),
            P(("batch", "seq")),
            P(("batch", "seq")),
            P(("batch", "seq")),
            P(("batch", "seq")),
            P(("batch", "seq")),
        ),
        check_vma=False,
    )
```

profile of v0, /device:TPU:8, one launch (start us, length us, event | category | flops | bytes accessed | tf_op | source)
XLA Modules:
  0.0 989.4 jit_solution(8292137692998214473)
XLA Ops:
  11.2 35.8 %all_gather.91 = bf16[32768]{0:T(1024)(128)(2,1)S(1)} all-gather(bf16[1024]{0:T(1024)(128)(2,1)} %param.57), channel_id=1, replica_groups=mesh['batch'=8,'seq'=4] {'batch','seq'}, dimensions={0}, use_global_device_ids=true | all-gather | bytes 67584 | tf_op jit(solution)/shard_map/all_gather | solution.py:135
  48.4 5.2 all-gather.13
  54.2 5.2 all-gather.12
  60.8 38.4 %all_gather.94 = bf16[262144]{0:T(1024)(128)(2,1)S(1)} all-gather(bf16[8192]{0:T(1024)(128)(2,1)} %param.51), channel_id=1, replica_groups=mesh['batch'=8,'seq'=4] {'batch','seq'}, dimensions={0}, use_global_device_ids=true | all-gather | bytes 540672 | tf_op jit(solution)/shard_map/all_gather | solution.py:129
  102.3 44.7 %all-reduce = bf16[1024]{0:T(1024)(128)(2,1)S(1)} all-reduce(bf16[1024]{0:T(1024)(128)(2,1)S(1)} %dynamic-update-slice.42), channel_id=1, replica_groups=mesh['batch'=8,'seq'=4] {'batch','seq'}, use_global_device_ids=true, to_apply=%add | all-reduce | flops 1024 | bytes 4096
  153.3 35.4 %all_gather.103 = bf16[262144]{0:T(1024)(128)(2,1)S(1)} all-gather(bf16[8192]{0:T(1024)(128)(2,1)S(1)} %copy-done.230), channel_id=1, replica_groups=mesh['batch'=8,'seq'=4] {'batch','seq'}, dimensions={0}, use_global_device_ids=true | all-gather | bytes 540672 | tf_op jit(solution)/shard_map/all_gather | solution.py:133
  189.1 5.2 all-gather.3
  195.4 5.2 all-gather
  249.4 13.3 %all-gather.31.cloned.1.call-done = bf16[1,2048,512]{1,2,0:T(8,128)(2,1)} async-done(((bf16[1,512,512]{1,2,0:T(8,128)(2,1)}), bf16[1,2048,512]{1,2,0:T(8,128)(2,1)}) %all-gather.31.cloned.1.call-update) | async-done | bytes 2097168 | tf_op jit(solution)/shard_map/all_gather | solution.py:192
  262.7 15.8 %fusion.332 = (f32[8,512]{1,0:T(8,128)S(1)}, f32[8,512,2048]{2,1,0:T(8,128)}) fusion(bf16[8,512,64]{1,2,0:T(8,128)(2,1)} %bitcast.739, bf16[8,2048,64]{1,2,0:T(8,128)(2,1)} %bitcast.734, pred[512,2048]{1,0:T(8,128)(4,1)} %get-tuple-element.715), kind=kOutput, calls=%fused_computation.566 | convolution fusion | flops 1098903552 | bytes 37240832 | tf_op jit(solution)/shard_map/htd,hkd->htk/dot_general | solution.py:196
  278.6 13.7 %fusion.6 = f32[8,512]{1,0:T(8,128)S(1)} fusion(f32[8,512,2048]{2,1,0:T(8,128)} %get-tuple-element.736, f32[8,512]{1,0:T(8,128)S(1)} %max.67), kind=kLoop, calls=%fused_computation.24 | loop fusion | flops 16773120 | bytes 33587200 | tf_op jit(solution)/shard_map/reduce_sum | solution.py:208
  292.3 16.6 %fusion.151 = (bf16[512,8,64]{0,2,1:T(8,128)(2,1)}, f32[8,512,64]{1,2,0:T(8,128)}) fusion(f32[8,512,64]{1,2,0:T(8,128)} %fusion.146, f32[512,8]{0,1:T(8,128)S(1)} %get-tuple-element.664, f32[512,8]{0,1:T(8,128)S(1)} %get-tuple-element.665, bf16[8,2048,64]{1,2,0:T(8,128)(2,1)} %bitcast.753, f32[8,512,2048]{2,1,0:T(8,128)} %get-tuple-element.736, ...), kind=kOutput, calls=%fused_computation.272 | convolution fusion | flops 1091567616 | bytes 38322176 | tf_op jit(solution)/shard_map/htk,hkd->htd/dot_general | solution.py:209
  323.4 5.2 all-gather.7
  329.5 7.8 all-gather.8
  338.1 7.7 while.52
  345.8 15.3 %fusion.329 = (f32[8,512]{1,0:T(8,128)S(1)}, f32[8,512,2048]{2,1,0:T(8,128)}) fusion(bf16[8,512,64]{1,2,0:T(8,128)(2,1)} %bitcast.743, bf16[8,2048,64]{1,2,0:T(8,128)(2,1)} %bitcast.736, pred[512,2048]{1,0:T(8,128)(4,1)} %get-tuple-element.716), kind=kOutput, calls=%fused_computation.563 | convolution fusion | flops 1098903552 | bytes 37240832 | tf_op jit(solution)/shard_map/htd,hkd->htk/dot_general | solution.py:196
  361.8 13.8 %fusion.8 = f32[8,512]{1,0:T(8,128)S(1)} fusion(f32[8,512,2048]{2,1,0:T(8,128)} %get-tuple-element.728, f32[8,512]{1,0:T(8,128)S(1)} %max.69), kind=kLoop, calls=%fused_computation.26 | loop fusion | flops 16773120 | bytes 33587200 | tf_op jit(solution)/shard_map/reduce_sum | solution.py:208
  382.3 15.5 %fusion.149 = (bf16[512,8,64]{0,2,1:T(8,128)(2,1)}, f32[8,512,64]{1,2,0:T(8,128)}) fusion(f32[8,512,64]{1,2,0:T(8,128)} %fusion.144, f32[512,8]{0,1:T(8,128)S(1)} %copy-done.184, f32[512,8]{0,1:T(8,128)S(1)} %copy-done.185, bf16[8,2048,64]{1,2,0:T(8,128)(2,1)} %bitcast.751, f32[8,512,2048]{2,1,0:T(8,128)} %get-tuple-element.728, f32[8,512]{1,0:T(8,128)S(1)} %copy-done.160), kind=kOutput, calls=%fused_computation.268 | convolution fusion | flops 1091567616 | bytes 38322176 | tf_op jit(solution)/shard_map/htk,hkd->htd/dot_general | solution.py:209
  407.4 5.2 all-gather.9
  419.3 7.3 all-gather.11
  427.4 8.0 while.53
  465.5 15.1 %fusion.40 = bf16[8,2048,64]{1,2,0:T(8,128)(2,1)} fusion(bf16[8,512,64]{1,2,0:T(8,128)(2,1)S(1)} %bitcast.727, f32[8,512,2048]{2,1,0:T(8,128)} %get-tuple-element.736, f32[8,512]{1,0:T(8,128)S(1)} %copy-done.108), kind=kOutput, calls=%fused_computation.68 | convolution fusion | flops 1091567616 | bytes 36192256 | tf_op jit(solution)/shard_map/htk,htd->hkd/dot_general | solution.py:401
  482.3 18.1 %multiply_convert_fusion.1 = bf16[8,512,2048]{2,1,0:T(8,128)(2,1)} fusion(f32[8,512,2048]{2,1,0:T(8,128)} %get-tuple-element.736, bf16[8,512,64]{1,2,0:T(8,128)(2,1)S(1)} %bitcast.729, bf16[8,2048,64]{1,2,0:T(8,128)(2,1)S(1)} %bitcast.754, f32[8,512]{1,0:T(8,128)S(1)} %get-tuple-element.748, f32[8,512]{1,0:T(8,128)S(1)} %copy-done.108), kind=kOutput, calls=%fused_computation.18 | convolution fusion | flops 1107296256 | bytes 52985856 | tf_op jit(solution)/shard_map/htd,hkd->htk/dot_general | solution.py:382
  514.9 10.3 %multiply_convert_fusion.3 = bf16[8,2048,64]{1,2,0:T(8,128)(2,1)} fusion(bf16[8,512,64]{1,2,0:T(8,128)(2,1)S(1)} %bitcast.741, bf16[8,512,2048]{2,1,0:T(8,128)(2,1)} %multiply_convert_fusion.1), kind=kOutput, calls=%fused_computation.61 | convolution fusion | flops 1075838976 | bytes 19398656 | tf_op jit(solution)/shard_map/htk,htd->hkd/dot_general | solution.py:397
  541.3 14.6 %multiply_convert_fusion = bf16[8,512,2048]{2,1,0:T(8,128)(2,1)S(1)} fusion(f32[8,512,2048]{2,1,0:T(8,128)} %get-tuple-element.728, bf16[8,512,64]{1,2,0:T(8,128)(2,1)S(1)} %bitcast.724, bf16[8,2048,64]{1,2,0:T(8,128)(2,1)} %bitcast.752, f32[8,512]{1,0:T(8,128)S(1)} %copy-done.135, f32[8,512]{1,0:T(8,128)S(1)} %get-tuple-element.659), kind=kOutput, calls=%fused_computation.16 | convolution fusion | flops 1107296256 | bytes 52985856 | tf_op jit(solution)/shard_map/htd,hkd->htk/dot_general | solution.py:382
  566.5 16.0 %fusion.43 = bf16[8,2048,64]{1,2,0:T(8,128)(2,1)} fusion(bf16[8,512,64]{1,2,0:T(8,128)(2,1)S(1)} %bitcast.725, f32[8,512,2048]{2,1,0:T(8,128)} %get-tuple-element.728, f32[8,512]{1,0:T(8,128)S(1)} %get-tuple-element.659), kind=kOutput, calls=%fused_computation.69 | convolution fusion | flops 1091567616 | bytes 36192256 | tf_op jit(solution)/shard_map/htk,htd->hkd/dot_general | solution.py:401
  611.6 5.9 copy.401
  622.8 9.7 fusion.340
  635.7 8.8 fusion.342
  677.6 5.3 bitcast_add_fusion
  731.4 41.1 %all-reduce.7 = f32[1024]{0:T(1024)S(1)} all-reduce(f32[1024]{0:T(1024)S(1)} %bitcast.823), channel_id=26, replica_groups=mesh['batch'=8,'seq'=4] {'batch','seq'}, use_global_device_ids=true, to_apply=%region_62.63.clone | all-reduce | flops 1024 | bytes 8192
  773.1 199.3 %all-reduce.12.cloned.1.call-done = (f32[786432]{0:T(1024)}, f32[262144]{0:T(1024)}, f32[1048576]{0:T(1024)}, f32[1048576]{0:T(1024)}, f32[524288]{0:T(1024)}, /*index=5*/f32[262144]{0:T(1024)}, f32[32768]{0:T(1024)}) async-done(((f32[786432]{0:T(1024)}, f32[262144]{0:T(1024)}, f32[1048576]{0:T(1024)}, f32[1048576]{0:T(1024)}, f32[524288]{0:T(1024)}, /*index=5*/f32[262144]{0:T(1024)}, f32[32768]{0:T(1024)}), ...) | async-done | bytes 15859728
  (817 shorter events, 322.4 us)
Async XLA Ops:
  7.2 94.9 %copy-start.238 = (bf16[32]{0:T(256)(128)(2,1)S(1)}, bf16[32]{0:T(256)(128)(2,1)}, u32[]{:S(2)}) copy-start(bf16[32]{0:T(256)(128)(2,1)} %param.56) | copy-start | bytes 196
  7.2 140.9 %all-gather.23.cloned.1.call-start = ((), (), s32[]{:S(2)}) async-start(), calls=%async_computation.4 | async-start | bytes 1622016 | tf_op jit(solution)/shard_map/all_gather | solution.py:128
  7.9 201.6 %all-gather.29.cloned.1.call-start = ((), (), s32[]{:S(2)}) async-start(), calls=%async_computation.7 | async-start | bytes 1081344 | tf_op jit(solution)/shard_map/all_gather | solution.py:132
  8.7 232.2 %all-gather.25.cloned.1.call-start = ((), (), s32[]{:S(2)}) async-start(), calls=%async_computation.5 | async-start | bytes 2162688 | tf_op jit(solution)/shard_map/all_gather | solution.py:130
  9.4 235.6 %all-gather.27.cloned.1.call-start = ((), (), s32[]{:S(2)}) async-start(), calls=%async_computation.6 | async-start | bytes 2162688 | tf_op jit(solution)/shard_map/all_gather | solution.py:131
  10.0 252.7 %all-gather.31.cloned.1.call-start = ((), (), s32[]{:S(2)}) async-start(), calls=%async_computation.12 | async-start | bytes 2621440 | tf_op jit(solution)/shard_map/all_gather | solution.py:192
  101.8 50.2 %copy-start.36 = (bf16[1,512,512]{1,2,0:T(8,128)(2,1)}, bf16[1,512,512]{1,2,0:T(8,128)(2,1)S(1)}, u32[]{:S(2)}) copy-start(bf16[1,512,512]{1,2,0:T(8,128)(2,1)S(1)} %copy.394) | copy-start | bytes 1572868
  102.0 113.6 %copy-start.17 = (bf16[1,512,512]{1,2,0:T(8,128)(2,1)}, bf16[1,512,512]{1,2,0:T(8,128)(2,1)S(1)}, u32[]{:S(2)}) copy-start(bf16[1,512,512]{1,2,0:T(8,128)(2,1)S(1)} %copy.395) | copy-start | bytes 1572868
  148.1 67.5 %copy-start.207 = (f32[512]{0:T(512)}, f32[512]{0:T(512)S(1)}, u32[]{:S(2)}) copy-start(f32[512]{0:T(512)S(1)} %get-tuple-element.718) | copy-start | bytes 6148
  148.1 67.5 %copy-start.193 = (f32[512]{0:T(512)}, f32[512]{0:T(512)S(1)}, u32[]{:S(2)}) copy-start(f32[512]{0:T(512)S(1)} %get-tuple-element.760) | copy-start | bytes 6148
  150.9 38.2 %copy-start.115 = (bf16[2,16,512]{2,1,0:T(8,128)(2,1)S(1)}, bf16[2,16,512]{2,1,0:T(8,128)(2,1)}, u32[]{:S(2)}) copy-start(bf16[2,16,512]{2,1,0:T(8,128)(2,1)} %param.47) | copy-start | bytes 98308
  153.2 139.1 %all-gather.33.cloned.1.call-start = ((), (), s32[]{:S(2)}) async-start(), calls=%async_computation.13 | async-start | bytes 2621440 | tf_op jit(solution)/shard_map/all_gather | solution.py:193
  153.3 51.8 %copy-start.236 = (s32[2,4]{1,0:T(2,128)S(1)}, s32[2,4]{1,0:T(2,128)}, u32[]{:S(2)}) copy-start(s32[2,4]{1,0:T(2,128)} %param.49) | copy-start | bytes 100
  189.1 262.0 %copy-start.5 = (bf16[512,512]{1,0:T(8,128)(2,1)}, bf16[512,512]{1,0:T(8,128)(2,1)S(1)}, u32[]{:S(2)}) copy-start(bf16[512,512]{1,0:T(8,128)(2,1)S(1)} %reshape.1180) | copy-start | bytes 1572868
  194.3 19.6 %copy-start.109 = (bf16[1,64,512]{2,1,0:T(8,128)(2,1)}, bf16[1,64,512]{2,1,0:T(8,128)(2,1)S(1)}, u32[]{:S(2)}) copy-start(bf16[1,64,512]{2,1,0:T(8,128)(2,1)S(1)} %all-gather.3) | copy-start | bytes 196612
  209.2 136.6 %all-gather.35.cloned.1.call-start = ((), (), s32[]{:S(2)}) async-start(), calls=%async_computation.14 | async-start | bytes 2621440 | tf_op jit(solution)/shard_map/all_gather | solution.py:192
  211.1 239.5 %copy-start.3 = (bf16[512,512]{1,0:T(8,128)(2,1)}, bf16[512,512]{1,0:T(8,128)(2,1)S(1)}, u32[]{:S(2)}) copy-start(bf16[512,512]{1,0:T(8,128)(2,1)S(1)} %slice.560) | copy-start | bytes 1572868
  213.9 102.1 %copy-start.102 = (bf16[64,512]{0,1:T(8,128)(2,1)}, bf16[64,512]{0,1:T(8,128)(2,1)S(1)}, u32[]{:S(2)}) copy-start(bf16[64,512]{0,1:T(8,128)(2,1)S(1)} %copy.376) | copy-start | bytes 196612
  219.4 162.9 %all-gather.37.cloned.1.call-start = ((), (), s32[]{:S(2)}) async-start(), calls=%async_computation.15 | async-start | bytes 2621440 | tf_op jit(solution)/shard_map/all_gather | solution.py:193
  236.3 139.4 %copy-start.136 = (f32[8,512]{1,0:T(8,128)}, f32[8,512]{1,0:T(8,128)S(1)}, u32[]{:S(2)}) copy-start(f32[8,512]{1,0:T(8,128)S(1)} %get-tuple-element.725) | copy-start | bytes 49156
  240.5 408.0 %reduce-scatter.11.cloned.1.call-start = ((), (), s32[]{:S(2)}) async-start(), calls=%async_computation.11 | async-start | bytes 409600 | tf_op jit(solution)/shard_map/reduce_scatter | solution.py:422
  292.3 18.9 %copy-start.150 = (f32[512]{0:T(512)S(1)}, f32[512]{0:T(512)}, u32[]{:S(2)}) copy-start(f32[512]{0:T(512)} %get-tuple-element.717) | copy-start | bytes 6148
  315.0 22.3 %copy-start.43 = (bf16[512,512]{0,1:T(8,128)(2,1)}, bf16[512,512]{0,1:T(8,128)(2,1)S(1)}, u32[]{:S(2)}) copy-start(bf16[512,512]{0,1:T(8,128)(2,1)S(1)} %fusion.97) | copy-start | bytes 1572868
  315.5 21.8 %copy-start.62 = (bf16[512,512]{0,1:T(8,128)(2,1)}, bf16[512,512]{0,1:T(8,128)(2,1)S(1)}, u32[]{:S(2)}) copy-start(bf16[512,512]{0,1:T(8,128)(2,1)S(1)} %convolution_convert_fusion.8) | copy-start | bytes 1572868
  382.3 19.1 %copy-start.151 = (f32[512]{0:T(512)S(1)}, f32[512]{0:T(512)}, u32[]{:S(2)}) copy-start(f32[512]{0:T(512)} %get-tuple-element.717) | copy-start | bytes 6148
  404.8 21.7 %copy-start.45 = (bf16[512,512]{0,1:T(8,128)(2,1)}, bf16[512,512]{0,1:T(8,128)(2,1)S(1)}, u32[]{:S(2)}) copy-start(bf16[512,512]{0,1:T(8,128)(2,1)S(1)} %fusion.98) | copy-start | bytes 1572868
  405.3 21.3 %copy-start.64 = (bf16[512,512]{0,1:T(8,128)(2,1)}, bf16[512,512]{0,1:T(8,128)(2,1)S(1)}, u32[]{:S(2)}) copy-start(bf16[512,512]{0,1:T(8,128)(2,1)S(1)} %convolution_convert_fusion.6) | copy-start | bytes 1572868
  511.3 138.2 %reduce-scatter.9.cloned.1.call-start = ((), (), s32[]{:S(2)}) async-start(), calls=%async_computation.10 | async-start | bytes 409600 | tf_op jit(solution)/shard_map/reduce_scatter | solution.py:422
  514.9 153.6 %reduce-scatter.5.cloned.1.call-start = ((), (), s32[]{:S(2)}) async-start(), calls=%async_computation.8 | async-start | bytes 5242880 | tf_op jit(solution)/shard_map/reduce_scatter | solution.py:419
  525.6 62.1 %copy-start.156 = (f32[64,512]{1,0:T(8,128)}, f32[64,512]{1,0:T(8,128)S(1)}, u32[]{:S(2)}) copy-start(f32[64,512]{1,0:T(8,128)S(1)} %mul.947) | copy-start | bytes 393220
  540.3 137.3 %reduce-scatter.7.cloned.1.call-start = ((), (), s32[]{:S(2)}) async-start(), calls=%async_computation.9 | async-start | bytes 5242880 | tf_op jit(solution)/shard_map/reduce_scatter | solution.py:419
  606.1 366.3 %all-reduce.12.cloned.1.call-start = ((), (), s32[]{:S(2)}) async-start(), calls=%async_computation.16 | async-start | bytes 31719424
  (221 other events, 1309.8 us)
Sparse Core Ops, SparseCore 0:
  10.9 55.1 all-gather.22
  68.9 52.8 all-gather.28
  124.7 56.1 all-gather.24
  183.6 55.1 all-gather.26
  240.3 22.3 all-gather.30
  264.1 22.5 all-gather.32
  288.3 22.5 all-gather.34
  312.5 23.1 all-gather.36
  511.4 20.4 reduce-scatter.10
  534.4 20.4 reduce-scatter.8
  557.4 44.4 reduce-scatter.4
  606.2 44.7 reduce-scatter.6
  696.4 276.0 all-reduce.11
where the time goes:
time: 1000 us; the launch traced here: 989 us
  matrix products  279 us (28%)
  blocking collectives  252 us (25%)
  waiting for transfers between devices  215 us (22%)
  local copies, waits for them, and re-layouts  132 us (13%)
  other arithmetic  91.5 us (9%)
  between operations  17.5 us (2%)
    unnamed x14, waiting for transfers between devices  202 us
    unnamed x2, blocking collectives  85.9 us
    unnamed x511, local copies, waits for them, and re-layouts  60 us
    all_gather x1, blocking collectives, per_device(): lax.all_gather(attn_out, ('batch', 'seq'), axis=0, tiled=True)  38.4 us
    dot_general x24, matrix products, outer_sum(): lax.dot_general(inputs, grads, (((0,), (0,)), ((), ())), preferred_elemen...  36.1 us
    all_gather x1, blocking collectives, per_device(): lax.all_gather(memory_init, ('batch', 'seq'), axis=0, tiled=True)  35.8 us
    all_gather x6, blocking collectives, joined(): lax.all_gather(part.astype(kind), axis)  35.7 us
    all_gather x1, blocking collectives, per_device(): lax.all_gather(writer_value, ('batch', 'seq'), axis=0, tiled=True)  35.4 us
  transfers between devices with their start and end apart: 13, of which 2 were waited for; matrix products, arithmetic and copies ran while one was open for 36% of the time, Pallas kernels for 0%

commit v1 on v0

v1 whole, which is shorter than its diff:
```python
import functools
import math

import jax
import jax.numpy as jnp
from jax import lax
from jax.experimental import pallas as pl
from jax.experimental.pallas import tpu as pltpu
from jax.sharding import PartitionSpec as P

HEADS = 8
HEAD_DIM = 64
FF = 2048
SEGMENT = 512
MASKED = -1e30
LANES = 128
CORE_HEADS = HEADS // 2
CORE_WIDTH = CORE_HEADS * HEAD_DIM
SCALE = HEAD_DIM ** (-0.5)
EXP = math.log2(math.e) * SCALE
LOG2E = math.log2(math.e)
RESET_COL = 8
LOG_COL = 10
NT = (((1,), (1,)), ((), ()))
NN = (((1,), (0,)), ((), ()))
TN = (((0,), (0,)), ((), ()))
GELU_A = math.sqrt(2.0 / math.pi)
GELU_B = 0.044715
BF16 = jnp.bfloat16
F32 = jnp.float32


def dot(left, right, dims=NN):
    return lax.dot_general(left, right, dims, preferred_element_type=F32)


def params():
    return pltpu.CompilerParams(vmem_limit_bytes=56 << 20)


def whole(*shape):
    return pl.BlockSpec(shape, lambda *_: (0,) * len(shape))


def norm_parts(values):
    centred = values - jnp.mean(values, axis=-1, keepdims=True)
    scale = lax.rsqrt(jnp.mean(centred * centred, axis=-1, keepdims=True) + 1e-05)
    return centred * scale, scale


def norm_back(unit, scale, grad, gain):
    back = grad * gain
    return scale * (
        back
        - jnp.mean(back, axis=-1, keepdims=True)
        - unit * jnp.mean(back * unit, axis=-1, keepdims=True)
    )


def in_three(values):
    high = values.astype(BF16).astype(F32)
    rest = values - high
    middle = rest.astype(BF16).astype(F32)
    return high, middle, rest - middle


def put_log(column, values, others):
    high, middle, low = in_three(values)
    out = jnp.where(column == LOG_COL, high, others)
    out = jnp.where(column == LOG_COL + 1, middle, out)
    return jnp.where(column == LOG_COL + 2, low, out)


def aux_column(shape, parity):
    lane = lax.broadcasted_iota(jnp.int32, shape, 1)
    return lane - (1 - parity) * HEAD_DIM


def project_kernel(
    info, own, other, mem_own, mem_other, weight, init, gain,
    q_out, k_out, v_out, normed_out, ks_out, vs_out, rows_out,
):
    rank = pl.program_id(0)
    core = info[0]
    rows = own.shape[1]

    values = jnp.where(rank % 2 == core, own[0], other[0]).astype(F32)
    unit, _ = norm_parts(values)
    normed = (unit * gain[0:1, :].astype(F32)).astype(BF16)
    normed_out[...] = normed
    shape = (rows, LANES)
    position = rank * rows + lax.broadcasted_iota(jnp.int32, shape, 0)
    doc = jnp.zeros(shape, jnp.int32)
    for k in range(8):
        doc = doc + (position >= info[2 + k]).astype(jnp.int32)
    reset = info[10 + (rank * rows) // SEGMENT]
    for which, out in ((0, q_out), (1, k_out), (2, v_out)):
        result = dot(normed, weight[which])
        for pair in range(2):
            mine = result[:, pair * LANES : (pair + 1) * LANES]
            for parity in range(2):
                column = aux_column(shape, parity)
                inside = (column >= 0) & (column < HEAD_DIM)
                if which == 0:
                    side = jnp.where(column == doc, 1.0, 0.0)
                    side = jnp.where(column == RESET_COL, reset.astype(F32), side)
                    side = jnp.where(column == RESET_COL + 1, 1.0 - reset.astype(F32), side)
                elif which == 1:
                    side = jnp.where((column < 8) & (column != doc), MASKED, 0.0)
                    side = jnp.where((column >= LOG_COL) & (column < LOG_COL + 3), 1.0, side)
                else:
                    side = jnp.ones(shape, F32)
                out[2 * pair + parity] = jnp.where(inside, side, mine).astype(BF16)

    @pl.when(rank == 0)
    def _():
        part = mem_own.shape[1]
        for k in range(4):
            rows_out[k * part : (k + 1) * part, :] = jnp.where(
                core == k % 2, mem_own[k // 2], mem_other[k // 2]
            )
        slots = rows_out.shape[0]
        source = jnp.concatenate([rows_out[...], init[...]], axis=0)
        shape = (2 * slots, LANES)
        start = (lax.broadcasted_iota(jnp.int32, shape, 0) >= slots).astype(jnp.int32)
        for which, out in ((1, ks_out), (2, vs_out)):
            result = dot(source, weight[which])
            for pair in range(2):
                mine = result[:, pair * LANES : (pair + 1) * LANES]
                for parity in range(2):
                    column = aux_column(shape, parity)
                    inside = (column >= 0) & (column < HEAD_DIM)
                    if which == 1:
                        side = jnp.where(column == RESET_COL + start, MASKED, 0.0)
                        side = jnp.where((column >= LOG_COL) & (column < LOG_COL + 3), 1.0, side)
                    else:
                        side = jnp.ones(shape, F32)
                    out[2 * pair + parity] = jnp.where(inside, side, mine).astype(BF16)


def project(info, own, other, weight, init, gains, rows, slot_part):
    width = own.shape[2]
    slots = 4 * slot_part
    length = 4 * rows
    at = rows // slot_part
    tokens = pl.BlockSpec((1, rows, width), lambda r, _: (r // 2, 0, 0))
    memory = pl.BlockSpec((2, slot_part, width), lambda r, _: (0, at, 0))
    heads = pl.BlockSpec((CORE_HEADS, rows, LANES), lambda r, _: (0, r, 0))
    return pl.pallas_call(
        project_kernel,
        grid_spec=pltpu.PrefetchScalarGridSpec(
            num_scalar_prefetch=1,
            grid=(4,),
            in_specs=[
                tokens, tokens, memory, memory,
                whole(3, width, CORE_WIDTH), whole(slots, width), whole(2, width),
            ],
            out_specs=[
                heads, heads, heads,
                pl.BlockSpec((rows, width), lambda r, _: (r, 0)),
                whole(CORE_HEADS, 2 * slots, LANES), whole(CORE_HEADS, 2 * slots, LANES),
                whole(slots, width),
            ],
        ),
        out_shape=[
            *[jax.ShapeDtypeStruct((CORE_HEADS, length, LANES), BF16)] * 3,
            jax.ShapeDtypeStruct((length, width), BF16),
            *[jax.ShapeDtypeStruct((CORE_HEADS, 2 * slots, LANES), BF16)] * 2,
            jax.ShapeDtypeStruct((slots, width), BF16),
        ],
        compiler_params=params(),
        name="project",
    )(info, own, other, own, other, weight, init, gains)


def attend_kernel(block, q_ref, k_ref, v_ref, ks_ref, vs_ref, o_ref, q_out):
    length = q_ref.shape[1]
    parity = pl.program_id(1)
    column = aux_column((block, LANES), parity)
    keep = (column < 0) | (column >= HEAD_DIM)
    row = lax.broadcasted_iota(jnp.int32, (block, block), 0)
    key = lax.broadcasted_iota(jnp.int32, (block, block), 1)
    for i in range(length // block):
        low, high = i * block, (i + 1) * block
        q = q_ref[0, low:high, :]
        slot = dot(q, ks_ref[0], NT)
        scores = dot(q, k_ref[0, :high, :], NT)
        last = jnp.where(row >= key, scores[:, low:], MASKED)
        scores = jnp.concatenate([scores[:, :low], last], axis=1) if i else last
        top = jnp.maximum(
            jnp.max(scores, axis=1, keepdims=True), jnp.max(slot, axis=1, keepdims=True)
        )
        share = jnp.exp2((scores - top) * EXP).astype(BF16)
        slot_share = jnp.exp2((slot - top) * EXP).astype(BF16)
        total = dot(share, v_ref[0, :high, :]) + dot(slot_share, vs_ref[0])
        count = jnp.where(parity == 0, total[:, HEAD_DIM : HEAD_DIM + 1], total[:, 0:1])
        o_ref[low:high, :] = jnp.where(keep, (total / count).astype(BF16), o_ref[low:high, :])
        log = top + jnp.log2(count) * (1.0 / EXP)
        q_out[0, low:high, :] = put_log(column, -log, q.astype(F32)).astype(BF16)


def attend(q, k, v, ks, vs):
    heads, length, _ = q.shape
    count = ks.shape[1]
    head = pl.BlockSpec((1, length, LANES), lambda p, e: (2 * p + e, 0, 0))
    slot = pl.BlockSpec((1, count, LANES), lambda p, e: (2 * p + e, 0, 0))
    return pl.pallas_call(
        functools.partial(attend_kernel, 256),
        grid=(heads // 2, 2),
        in_specs=[head, head, head, slot, slot],
        out_specs=[pl.BlockSpec((length, LANES), lambda p, e: (0, p)), head],
        out_shape=[
            jax.ShapeDtypeStruct((length, CORE_WIDTH), BF16),
            jax.ShapeDtypeStruct(q.shape, BF16),
        ],
        compiler_params=params(),
        name="attend",
    )(q, k, v, ks, vs)


def attend_back_kernel(
    kb, qb, info, q_ref, k_ref, v_ref, ks_ref, vs_ref, own_ref, other_ref, o_ref,
    dq_ref, dk_ref, dv_ref, dks_ref, dvs_ref, d_ref, acc_ref,
):
    length = q_ref.shape[1]
    parity = pl.program_id(1)
    core = info[0]
    rows = own_ref.shape[1]
    column = aux_column((rows, LANES), parity)
    inside = (column < 0) | (column >= HEAD_DIM)
    for r in range(length // rows):
        low, high = r * rows, (r + 1) * rows
        d = jnp.where(core == r % 2, own_ref[r // 2], other_ref[r // 2]).astype(F32)
        delta = jnp.sum(
            jnp.where(inside, d * o_ref[low:high, :].astype(F32), 0.0), axis=1, keepdims=True
        )
        d_ref[low:high, :] = jnp.where(
            inside, d, put_log(column, -delta, jnp.zeros_like(d))
        ).astype(BF16)
    acc_ref[...] = jnp.zeros_like(acc_ref)

    def merged(ref, low, high, value):
        column = aux_column(value.shape, parity)
        keep = (column < 0) | (column >= HEAD_DIM)
        ref[low:high, :] = jnp.where(keep, value.astype(BF16), ref[low:high, :])

    count = ks_ref.shape[1]
    pieces = [(ks_ref, vs_ref, dks_ref, dvs_ref, 0, count, None)]
    pieces += [(k_ref, v_ref, dk_ref, dv_ref, j, j + kb, j) for j in range(0, length, kb)]
    for keys, values, dk_out, dv_out, start, stop, first in pieces:
        k = keys[0, start:stop, :]
        v = values[0, start:stop, :]
        turned = k.astype(F32).T.astype(BF16)
        dk = jnp.zeros((stop - start, LANES), F32)
        dv = jnp.zeros((stop - start, LANES), F32)
        low = first or 0
        while low < length:
            high = min((low // qb + 1) * qb, length)
            q = q_ref[0, low:high, :]
            d = d_ref[low:high, :]
            scores = dot(k, q, NT)
            share = jnp.exp2(scores * EXP)
            if first is not None and low < stop:
                key = first + lax.broadcasted_iota(jnp.int32, scores.shape, 0)
                position = low + lax.broadcasted_iota(jnp.int32, scores.shape, 1)
                share = jnp.where(key <= position, share, 0.0)
            ds = (share * dot(v, d, NT)).astype(BF16)
            dv = dv + dot(share.astype(BF16), d)
            dk = dk + dot(ds, q)
            acc_ref[:, low:high] += dot(turned, ds)
            low = high
        merged(dk_out, start, stop, dk * SCALE)
        merged(dv_out, start, stop, dv)
    merged(dq_ref, 0, length, acc_ref[...].T * SCALE)


def attend_back(info, q, k, v, ks, vs, own, other, o):
    heads, length, _ = q.shape
    count = ks.shape[1]
    rows = own.shape[1]
    head = pl.BlockSpec((1, length, LANES), lambda p, e, _: (2 * p + e, 0, 0))
    slot = pl.BlockSpec((1, count, LANES), lambda p, e, _: (2 * p + e, 0, 0))
    grads = pl.BlockSpec((2, rows, LANES), lambda p, e, _: (0, 0, p))
    pair = pl.BlockSpec((length, LANES), lambda p, e, _: (0, p))
    slot_pair = pl.BlockSpec((count, LANES), lambda p, e, _: (0, p))
    return pl.pallas_call(
        functools.partial(attend_back_kernel, 256, 1024),
        grid_spec=pltpu.PrefetchScalarGridSpec(
            num_scalar_prefetch=1,
            grid=(heads // 2, 2),
            in_specs=[head, head, head, slot, slot, grads, grads, pair],
            out_specs=[pair, pair, pair, slot_pair, slot_pair],
            scratch_shapes=[pltpu.VMEM((length, LANES), BF16), pltpu.VMEM((LANES, length), F32)],
        ),
        out_shape=[
            *[jax.ShapeDtypeStruct((length, CORE_WIDTH), BF16)] * 3,
            *[jax.ShapeDtypeStruct((count, CORE_WIDTH), BF16)] * 2,
        ],
        compiler_params=params(),
        name="attend_back",
    )(info, q, k, v, ks, vs, own, other, o)


def forward_kernel(
    info, tokens, own, other, w_out, w_up, w_down, w_write, w_value, gains,
    middle_out, normed_out, act_out, slope_out, result_out, keys_out, values_out,
):
    core = info[0]
    mine = pl.multiple_of(core * CORE_WIDTH, CORE_WIDTH)
    rest = pl.multiple_of((1 - core) * CORE_WIDTH, CORE_WIDTH)
    middle = (
        tokens[0].astype(F32)
        + dot(own[...], w_out[pl.ds(mine, CORE_WIDTH), :])
        + dot(other[0], w_out[pl.ds(rest, CORE_WIDTH), :])
    )
    middle_out[0] = middle
    unit, _ = norm_parts(middle)
    normed = (unit * gains[1:2, :].astype(F32)).astype(BF16)
    normed_out[0] = normed
    chunk = w_up.shape[2]
    for k in range(w_up.shape[0]):
        pre = dot(normed, w_up[k])
        square = pre * pre
        bend = jnp.tanh(GELU_A * (pre + GELU_B * (square * pre)))
        half = 0.5 * (1.0 + bend)
        act = (pre * half).astype(BF16)
        slope = half + 0.5 * pre * (1.0 - bend * bend) * (
            GELU_A * (1.0 + (3.0 * GELU_B) * square)
        )
        act_out[0, :, k * chunk : (k + 1) * chunk] = act
        slope_out[0, :, k * chunk : (k + 1) * chunk] = slope.astype(BF16)
    low = (middle + dot(act_out[0], w_down[...])).astype(BF16)
    result_out[0] = low
    keys_out[0] = dot(low, w_write[1]).astype(BF16)
    values_out[0] = dot(low, w_value[...]).astype(BF16)


def forward(info, tokens, o, other, weights, gains, rows):
    width = tokens.shape[2]
    w_out, w_up, w_down, w_write, w_value = weights
    block = pl.BlockSpec((1, rows, width), lambda i, _: (i, 0, 0))
    wide = pl.BlockSpec((1, rows, FF), lambda i, _: (i, 0, 0))
    shape = (2, rows, width)
    return pl.pallas_call(
        forward_kernel,
        grid_spec=pltpu.PrefetchScalarGridSpec(
            num_scalar_prefetch=1,
            grid=(2,),
            in_specs=[
                block,
                pl.BlockSpec((rows, CORE_WIDTH), lambda i, info: (2 * i + info[0], 0)),
                pl.BlockSpec((1, rows, CORE_WIDTH), lambda i, _: (i, 0, 0)),
                *[whole(*w.shape) for w in weights],
                whole(*gains.shape),
            ],
            out_specs=[block, block, wide, wide, block, block, block],
        ),
        out_shape=[
            jax.ShapeDtypeStruct(shape, F32),
            jax.ShapeDtypeStruct(shape, BF16),
            *[jax.ShapeDtypeStruct((2, rows, FF), BF16)] * 2,
            *[jax.ShapeDtypeStruct(shape, BF16)] * 3,
        ],
        compiler_params=params(),
        name="feed_forward",
    )(info, tokens, o, other, *weights, gains)


def backward_kernel(
    info, cot, d_keys, d_values, result, middle, normed, act, slope, own_a, own_b, other,
    w_out, w_up, w_down, w_write, w_value, gains, rows_ref, d_query, d_self_key, d_self_value,
    mem_cot,
    g_up, g_down, g_out, g_write, g_value, d_middle_out, d_own, d_other, g_gain, d_memory,
    d_result_ref, d_update_ref, d_normed_ref,
):
    step = pl.program_id(0)
    core = info[0]
    count, rows, width = result.shape
    total = count * rows
    mine = pl.multiple_of(core * CORE_WIDTH, CORE_WIDTH)
    rest = pl.multiple_of((1 - core) * CORE_WIDTH, CORE_WIDTH)

    @pl.when(step == 0)
    def _():
        dk = d_keys[...].reshape(total, width)
        dv = d_values[...].reshape(total, width)
        d_result = (
            cot[...].reshape(total, width).astype(F32)
            + dot(dk, w_write[1], NT)
            + dot(dv, w_value[...], NT)
        )
        d_result_ref[...] = d_result
        d_update_ref[...] = d_result.astype(BF16)
        d_normed_ref[...] = jnp.zeros_like(d_normed_ref)
        out = result[...].reshape(total, width)
        memory = rows_ref[...]
        g_write[0] = dot(memory, d_query[...], TN).astype(BF16)
        g_write[1] = (dot(out, dk, TN) + dot(memory, d_self_key[...], TN)).astype(BF16)
        g_value[...] = (dot(out, dv, TN) + dot(memory, d_self_value[...], TN)).astype(BF16)
        d_memory[...] = (
            mem_cot[...]
            + dot(d_query[...], w_write[0], NT)
            + dot(d_self_key[...], w_write[1], NT)
            + dot(d_self_value[...], w_value[...], NT)
        )

    d_update = d_update_ref[...]
    d_act = dot(d_update, w_down[...], NT)
    d_hidden = (d_act * slope[...].reshape(total, -1).astype(F32)).astype(BF16)
    g_down[...] = dot(act[...].reshape(total, -1), d_update, TN).astype(BF16)
    g_up[0] = dot(normed[...].reshape(total, width), d_hidden, TN).astype(BF16)
    d_normed_ref[...] += dot(d_hidden, w_up[0], NT)

    @pl.when(step == pl.num_programs(0) - 1)
    def _():
        gain = gains[1:2, :].astype(F32)
        unit, scale = norm_parts(middle[...].reshape(total, width))
        d_normed = d_normed_ref[...]
        g_gain[...] = jnp.sum(d_normed * unit, axis=0, keepdims=True)
        d_middle = d_result_ref[...] + norm_back(unit, scale, d_normed, gain)
        d_middle_out[...] = d_middle.reshape(count, rows, width)
        d_branch = d_middle.astype(BF16)
        d_own[...] = (
            dot(d_branch, w_out[pl.ds(mine, CORE_WIDTH), :], NT)
            .astype(BF16)
            .reshape(count, rows, CORE_WIDTH)
        )
        d_other[...] = (
            dot(d_branch, w_out[pl.ds(rest, CORE_WIDTH), :], NT)
            .astype(BF16)
            .reshape(count, rows, CORE_WIDTH)
        )
        g_out[pl.ds(mine, CORE_WIDTH), :] = (
            dot(own_a[...], d_branch[:rows], TN) + dot(own_b[...], d_branch[rows:], TN)
        ).astype(BF16)
        g_out[pl.ds(rest, CORE_WIDTH), :] = dot(
            other[...].reshape(total, CORE_WIDTH), d_branch, TN
        ).astype(BF16)


def backward(info, cot, d_keys, d_values, result, middle, normed, act, slope, o, other, weights,
             gains, memory, slot_grads, mem_cot, rows):
    width = result.shape[2]
    w_out, w_up, w_down, w_write, w_value = weights
    steps = w_up.shape[0]
    chunk = FF // steps
    all_rows = whole(2, rows, width)
    wide = pl.BlockSpec((2, rows, chunk), lambda i, _: (0, 0, i))
    slots = whole(*memory.shape)
    up = pl.BlockSpec((1, width, chunk), lambda i, _: (i, 0, 0))
    down = pl.BlockSpec((chunk, width), lambda i, _: (i, 0))
    half = whole(2, rows, CORE_WIDTH)
    return pl.pallas_call(
        backward_kernel,
        grid_spec=pltpu.PrefetchScalarGridSpec(
            num_scalar_prefetch=1,
            grid=(steps,),
            in_specs=[
                all_rows, all_rows, all_rows, all_rows, all_rows, all_rows, wide, wide,
                pl.BlockSpec((rows, CORE_WIDTH), lambda i, info: (info[0], 0)),
                pl.BlockSpec((rows, CORE_WIDTH), lambda i, info: (2 + info[0], 0)),
                half, whole(*w_out.shape), up, down, whole(*w_write.shape), whole(*w_value.shape),
                whole(*gains.shape), slots, slots, slots, slots, slots,
            ],
            out_specs=[
                up, down, whole(width, width), whole(2, width, width), whole(width, width),
                all_rows, half, half, whole(1, width), slots,
            ],
            scratch_shapes=[
                pltpu.VMEM((2 * rows, width), F32),
                pltpu.VMEM((2 * rows, width), BF16),
                pltpu.VMEM((2 * rows, width), F32),
            ],
        ),
        out_shape=[
            jax.ShapeDtypeStruct(w_up.shape, BF16),
            jax.ShapeDtypeStruct(w_down.shape, BF16),
            jax.ShapeDtypeStruct((width, width), BF16),
            jax.ShapeDtypeStruct((2, width, width), BF16),
            jax.ShapeDtypeStruct((width, width), BF16),
            jax.ShapeDtypeStruct((2, rows, width), F32),
            *[jax.ShapeDtypeStruct((2, rows, CORE_WIDTH), BF16)] * 2,
            jax.ShapeDtypeStruct((1, width), F32),
            jax.ShapeDtypeStruct(memory.shape, F32),
        ],
        compiler_params=params(),
        name="feed_forward_back",
    )(info, cot, d_keys, d_values, result, middle, normed, act, slope, o, o, other, *weights,
      gains, memory, *slot_grads, mem_cot)


def head_mask(shape, head):
    lane = lax.broadcasted_iota(jnp.int32, shape, 1)
    return (lane >= head * HEAD_DIM) & (lane < (head + 1) * HEAD_DIM)


def stacked_heads(values):
    return jnp.concatenate(
        [jnp.where(head_mask(values.shape, h), values, 0.0) for h in range(HEADS)], axis=0
    )


def joined_heads(stacked, slots):
    out = None
    for h in range(HEADS):
        part = stacked[h * slots : (h + 1) * slots, :]
        shape = (slots, HEADS * HEAD_DIM)
        part = jnp.broadcast_to(part, shape)
        out = part if out is None else jnp.where(head_mask(shape, h), part, out)
    return out


def column_of_heads(values):
    return jnp.concatenate(
        [values[:, h * HEAD_DIM : h * HEAD_DIM + 1] for h in range(HEADS)], axis=0
    )


def head_sums(values):
    return jnp.concatenate(
        [
            jnp.sum(jnp.where(head_mask(values.shape, h), values, 0.0), axis=1, keepdims=True)
            for h in range(HEADS)
        ],
        axis=0,
    )


def write_kernel(keys, values, memory, w_write, w_value, query_out, key_out, value_out, stats):
    slots = memory.shape[0]
    total = keys.shape[0] * keys.shape[1]
    rows = memory[...]
    query = dot(rows, w_write[0]).astype(BF16)
    query_out[...] = query
    key_out[...] = dot(rows, w_write[1]).astype(BF16)
    value_out[...] = dot(rows, w_value[...]).astype(BF16)
    stacked = stacked_heads(query.astype(F32)).astype(BF16)
    scores = dot(stacked, keys[...].reshape(total, -1), NT)
    top = jnp.max(scores, axis=1, keepdims=True)
    share = jnp.exp2((scores - top) * EXP)
    stats[0] = joined_heads(top, slots)
    stats[1] = joined_heads(jnp.sum(share, axis=1, keepdims=True), slots)
    stats[2] = joined_heads(dot(share.astype(BF16), values[...].reshape(total, -1)), slots)


def write(keys, values, memory, w_write, w_value):
    slots, width = memory.shape
    small = jax.ShapeDtypeStruct((slots, width), BF16)
    return pl.pallas_call(
        write_kernel,
        out_shape=[small, small, small, jax.ShapeDtypeStruct((3, slots, width), F32)],
        compiler_params=params(),
        name="write",
    )(keys, values, memory, w_write, w_value)


def write_back_kernel(
    info, own, other, query, key, value, memory, cot_own, cot_other, keys, values,
    new_out, d_keys, d_values, d_query, d_key, d_value, cot_mine,
):
    core = info[0]
    slots, width = memory.shape
    part = cot_own.shape[1]
    total = keys.shape[0] * keys.shape[1]
    cot = jnp.concatenate(
        [jnp.where(core == k % 2, cot_own[k // 2], cot_other[k // 2]) for k in range(4)], axis=0
    ).astype(F32)
    q = query[...].astype(F32)
    sk = key[...].astype(F32)
    sv = value[...].astype(F32)
    self_column = head_sums(q * sk)
    self_scores = joined_heads(self_column, slots)
    top = jnp.maximum(jnp.maximum(own[0], other[0]), self_scores)
    own_share = jnp.exp2((own[0] - top) * EXP)
    other_share = jnp.exp2((other[0] - top) * EXP)
    self_share = jnp.exp2((self_scores - top) * EXP)
    count = own[1] * own_share + other[1] * other_share + self_share
    written = (
        own[2] * own_share + other[2] * other_share + self_share.astype(BF16).astype(F32) * sv
    ) / count
    new_out[...] = (memory[...].astype(F32) + written).astype(BF16)
    log = top + jnp.log2(count) * (1.0 / EXP)
    log_column = column_of_heads(log)
    delta_column = head_sums(cot * written)
    delta = joined_heads(delta_column, slots)
    stacked = stacked_heads(q).astype(BF16)
    stacked_cot = stacked_heads(cot).astype(BF16)
    flat_keys = keys[...].reshape(total, width)
    share = jnp.exp2((dot(stacked, flat_keys, NT) - log_column) * EXP)
    d_share = dot(stacked_cot, values[...].reshape(total, width), NT)
    d_scores = (share * (d_share - delta_column)).astype(BF16)
    d_values[...] = dot(share.astype(BF16), stacked_cot, TN).astype(BF16).reshape(d_values.shape)
    d_keys[...] = (dot(d_scores, stacked, TN) * SCALE).astype(BF16).reshape(d_keys.shape)
    d_query_part = joined_heads(dot(d_scores, flat_keys), slots) * SCALE
    mine = (lax.broadcasted_iota(jnp.int32, (slots, width), 0) // part) % 2 == core
    self_probs = jnp.exp2((self_scores - log) * EXP)
    self_dp = joined_heads(head_sums(cot * sv), slots)
    self_ds = (self_probs * (self_dp - delta)).astype(BF16).astype(F32) * SCALE
    self_ds = jnp.where(mine, self_ds, 0.0)
    d_query[...] = (d_query_part + self_ds * sk).astype(BF16)
    d_key[...] = (self_ds * q).astype(BF16)
    d_value[...] = jnp.where(mine, self_probs.astype(BF16).astype(F32) * cot, 0.0).astype(BF16)
    cot_mine[...] = jnp.where(mine, cot, 0.0)


def write_back(info, own, other, query, key, value, memory, cot_own, cot_other, keys, values, rows):
    slots, width = memory.shape
    part = slots // 4
    at = rows // part
    small = jax.ShapeDtypeStruct((slots, width), BF16)
    cots = pl.BlockSpec((2, part, width), lambda i, _: (0, at, 0))
    flat = whole(slots, width)
    stats = whole(3, slots, width)
    big = whole(2, rows, width)
    return pl.pallas_call(
        write_back_kernel,
        grid_spec=pltpu.PrefetchScalarGridSpec(
            num_scalar_prefetch=1,
            grid=(1,),
            in_specs=[stats, stats, flat, flat, flat, flat, cots, cots, big, big],
            out_specs=[flat, big, big, flat, flat, flat, flat],
        ),
        out_shape=[
            small,
            *[jax.ShapeDtypeStruct((2, rows, width), BF16)] * 2,
            small, small, small,
            jax.ShapeDtypeStruct((slots, width), F32),
        ],
        compiler_params=params(),
        name="write_back",
    )(info, own, other, query, key, value, memory, cot_own, cot_other, keys, values)


def project_back_kernel(
    normed, dq, dk, dv, weight, memory, init, dks, dvs, d_normed_out, g_out, d_slots, acc_ref
):
    rank = pl.program_id(0)

    @pl.when(rank == 0)
    def _():
        source = jnp.concatenate([memory[...], init[...]], axis=0)
        acc_ref[0] = jnp.zeros(acc_ref.shape[1:], F32)
        acc_ref[1] = dot(source, dks[...], TN)
        acc_ref[2] = dot(source, dvs[...], TN)
        d_slots[...] = dot(dks[...], weight[1], NT) + dot(dvs[...], weight[2], NT)

    rows = normed[...]
    grads = (dq[...], dk[...], dv[...])
    d_normed_out[...] = (
        dot(grads[0], weight[0], NT) + dot(grads[1], weight[1], NT) + dot(grads[2], weight[2], NT)
    ).astype(BF16)
    for k in range(3):
        acc_ref[k] += dot(rows, grads[k], TN)

    @pl.when(rank == pl.num_programs(0) - 1)
    def _():
        g_out[...] = acc_ref[...].astype(BF16)


def project_back(normed, dq, dk, dv, weight, memory, init, dks, dvs, rows):
    length, width = normed.shape
    slots = memory.shape[0]
    block = pl.BlockSpec((rows, width), lambda r: (r, 0))
    half = pl.BlockSpec((rows, CORE_WIDTH), lambda r: (r, 0))
    return pl.pallas_call(
        project_back_kernel,
        grid=(length // rows,),
        in_specs=[
            block, half, half, half, whole(*weight.shape), whole(slots, width),
            whole(slots, width), whole(*dks.shape), whole(*dvs.shape),
        ],
        out_specs=[block, whole(*weight.shape), whole(2 * slots, width)],
        out_shape=[
            jax.ShapeDtypeStruct((length, width), BF16),
            jax.ShapeDtypeStruct(weight.shape, BF16),
            jax.ShapeDtypeStruct((2 * slots, width), F32),
        ],
        scratch_shapes=[pltpu.VMEM(weight.shape, F32)],
        compiler_params=params(),
        name="project_back",
    )(normed, dq, dk, dv, weight, memory, init, dks, dvs)


def inputs_back_kernel(tokens, mine, other, d_middle, gains, d_out, g_gain):
    step = pl.program_id(0)
    unit, scale = norm_parts(tokens[0].astype(F32))
    d_normed = mine[...].astype(F32) + other[0].astype(F32)
    gain = gains[0:1, :].astype(F32)
    d_out[0] = (d_middle[0] + norm_back(unit, scale, d_normed, gain)).astype(BF16)
    part = jnp.sum(d_normed * unit, axis=0, keepdims=True)

    @pl.when(step == 0)
    def _():
        g_gain[...] = part

    @pl.when(step > 0)
    def _():
        g_gain[...] += part


def inputs_back(info, tokens, d_normed, other, d_middle, gains, rows):
    width = tokens.shape[2]
    block = pl.BlockSpec((1, rows, width), lambda i, _: (i, 0, 0))
    return pl.pallas_call(
        lambda info, *refs: inputs_back_kernel(*refs),
        grid_spec=pltpu.PrefetchScalarGridSpec(
            num_scalar_prefetch=1,
            grid=(2,),
            in_specs=[
                block,
                pl.BlockSpec((rows, width), lambda i, info: (2 * i + info[0], 0)),
                block, block, whole(*gains.shape),
            ],
            out_specs=[block, whole(1, width)],
        ),
        out_shape=[
            jax.ShapeDtypeStruct((2, rows, width), BF16),
            jax.ShapeDtypeStruct((1, width), F32),
        ],
        compiler_params=params(),
        name="inputs_back",
    )(info, tokens, d_normed, other, d_middle, gains)


def swap(value, over_batch, over_seq):
    batch, seq = lax.axis_size("batch"), lax.axis_size("seq")
    pairs = [
        (i * seq + j, (i ^ over_batch) * seq + (j ^ over_seq))
        for i in range(batch)
        for j in range(seq)
    ]
    return lax.ppermute(value, ("batch", "seq"), pairs)


def chip_groups():
    batch = lax.axis_index("batch")
    chip = lax.axis_index("seq") // 2
    stages = [(4, 2 * (batch & 1) + chip, lambda k: (k >> 1, 2 * (k & 1)))]
    bits = lax.axis_size("batch").bit_length() - 1
    at = 1
    while at < bits:
        count = min(2, bits - at)
        stages.append(
            (1 << count, (batch >> at) & ((1 << count) - 1), lambda k, at=at: (k << at, 0))
        )
        at += count
    return stages


def in_order(pieces, own):
    bit = 1
    while bit < len(pieces):
        turned = (own & bit) > 0
        pieces = [jnp.where(turned, pieces[k ^ bit], pieces[k]) for k in range(len(pieces))]
        bit *= 2
    return jnp.stack(pieces)


def gather_chips(piece):
    stages = chip_groups()
    shape = piece.shape
    for size, own, peer in reversed(stages):
        piece = in_order([piece] + [swap(piece, *peer(k)) for k in range(1, size)], own)
    count = len(stages)
    piece = piece.transpose(*reversed(range(count)), *range(count, piece.ndim))
    return piece.reshape(-1, *shape)


def sum_to_chips(pieces):
    shape = pieces.shape[1:]
    stages = chip_groups()
    for k, (size, own, peer) in enumerate(stages):
        pieces = pieces.reshape(-1, size, *shape)
        parts = [
            lax.dynamic_index_in_dim(pieces, own ^ j, 1, keepdims=False) for j in range(size)
        ]
        total = parts[0].astype(F32)
        for j in range(1, size):
            total = total + swap(parts[j], *peer(j)).astype(F32)
        pieces = total if k == len(stages) - 1 else total.astype(BF16)
    return pieces.reshape(shape)


def by_core(core, mine, other, axis=0):
    return jnp.where(
        core == 0,
        jnp.concatenate([mine, other], axis=axis),
        jnp.concatenate([other, mine], axis=axis),
    )


def by_chip(chip, mine, other):
    return jnp.where(chip == 0, jnp.stack([mine, other]), jnp.stack([other, mine]))


def pick(array, index, axis=0):
    return lax.dynamic_index_in_dim(array, index, axis, keepdims=False)


def per_device(
    tokens, memory, lengths, resets, attn_in, attn_out, ffn_in, ffn_out, writer_in, writer_value,
    norm_gains, memory_init, out_cotangent, memory_cotangent,
):
    _, rows, width = tokens.shape
    devices = lax.axis_size("batch") * lax.axis_size("seq")
    rank = lax.axis_index("seq")
    chip, core = rank // 2, rank % 2
    slot_part = memory.shape[1]
    slots = 4 * slot_part
    chunks = FF // width

    ends = jnp.cumsum(pick(lengths, chip))
    info = jnp.concatenate([jnp.stack([core, chip]), ends, pick(resets, chip)]).astype(jnp.int32)

    def to_chip(big, small):
        mine = jnp.concatenate([pick(big, chip), pick(small, chip)], axis=0)
        away = jnp.concatenate([pick(big, 1 - chip), pick(small, 1 - chip)], axis=0)
        return by_chip(chip, mine, swap(away, 0, 2))

    misc = jnp.concatenate([memory_init, norm_gains])
    misc_rows = -(-misc.shape[0] // CORE_WIDTH)
    misc = jnp.pad(misc, (0, misc_rows * CORE_WIDTH - misc.shape[0])).reshape(misc_rows, CORE_WIDTH)
    attn_rows = attn_in.reshape(-1, 2, CORE_WIDTH)
    own_rows = attn_rows.shape[0]
    mine = jnp.concatenate([pick(attn_rows, core, 1), misc], axis=0)
    theirs = swap(jnp.concatenate([pick(attn_rows, 1 - core, 1), misc], axis=0), 0, 1)
    piece = jnp.concatenate(
        [
            by_core(core, mine[:own_rows], theirs[:own_rows]),
            by_core(core, mine[own_rows:], theirs[own_rows:]),
        ],
        axis=0,
    )
    gathered = gather_chips(piece)
    w_qkv = gathered[:, : 2 * own_rows].reshape(3, width, CORE_WIDTH)
    misc = gathered[:, 2 * own_rows :].reshape(devices, -1)
    init = misc[:, : memory_init.shape[0]].reshape(slots, width)
    gains = misc[:, memory_init.shape[0] :][:, : norm_gains.shape[0]].reshape(2, width)

    def columns(flat):
        return flat.reshape(-1, chunks, width).transpose(1, 0, 2).reshape(-1, width)

    parts = [
        attn_out.reshape(-1, width), columns(ffn_in), ffn_out.reshape(-1, width),
        writer_in.reshape(-1, width), writer_value.reshape(-1, width),
    ]
    sizes = [part.shape[0] for part in parts]
    cuts = [sum(sizes[:k]) for k in range(len(sizes) + 1)]
    packed = lax.all_gather(jnp.concatenate(parts, axis=0), ("batch", "seq"), axis=0)
    fields = [packed[:, cuts[k] : cuts[k + 1]] for k in range(len(sizes))]
    weights = (
        fields[0].reshape(width, width),
        fields[1].reshape(devices, chunks, -1, width).transpose(1, 0, 2, 3).reshape(chunks, width, width),
        fields[2].reshape(FF, width),
        fields[3].reshape(2, width, width),
        fields[4].reshape(width, width),
    )
    w_out, w_up, w_down, w_write, w_value = weights

    own = to_chip(tokens, memory)
    other = swap(own, 0, 1)
    q, k, v, normed, ks, vs, mem_rows = project(
        info, own, other, w_qkv, init, gains, rows, slot_part
    )
    cots = to_chip(out_cotangent, memory_cotangent)
    cots_other = swap(cots[:, rows:], 0, 1)
    cots_other = jnp.concatenate([jnp.zeros((2, rows, width), BF16), cots_other], axis=1)
    o, q_log = attend(q, k, v, ks, vs)
    o_other = swap(pick(o.reshape(2, 2, rows, CORE_WIDTH), 1 - core, 1), 0, 1)
    middle, normed_two, act, slope, result, keys, values = forward(
        info, own, o, o_other, weights, gains, rows
    )
    wq, sk, sv, stats = write(keys, values, mem_rows, w_write, w_value)
    stats_other = swap(stats, 0, 1)
    new_rows, d_keys, d_values, *slot_grads, cot_mine = write_back(
        info, stats, stats_other, wq, sk, sv, mem_rows, cots, cots_other, keys, values, rows
    )
    g_up, g_down, g_out, g_write, g_value, d_middle, d_own, d_away, g_gain_two, d_memory = backward(
        info, cots, d_keys, d_values, result, middle, normed_two, act, slope, o, o_other, weights,
        gains, mem_rows, slot_grads, cot_mine, rows,
    )
    d_other = swap(d_away, 0, 1)

    grads = jnp.concatenate(
        [
            g_out.reshape(devices, -1, width),
            g_up.reshape(chunks, devices, -1, width).transpose(1, 0, 2, 3).reshape(devices, -1, width),
            g_down.reshape(devices, -1, width),
            g_write.reshape(devices, -1, width),
            g_value.reshape(devices, -1, width),
        ],
        axis=1,
    ).reshape(devices // 2, 2, -1, width)
    kept = pick(grads, core, 1)
    arrived = swap(pick(grads, 1 - core, 1), 0, 1)
    summed = sum_to_chips((kept.astype(F32) + arrived.astype(F32)).astype(BF16))
    big = [summed[cuts[k] : cuts[k + 1]] for k in range(len(sizes))]
    big[1] = big[1].reshape(chunks, -1, width).transpose(1, 0, 2)

    dq, dk, dv, dks, dvs = attend_back(info, q_log, k, v, ks, vs, d_own, d_other, o)
    d_normed, g_qkv, d_slots = project_back(
        normed, dq, dk, dv, w_qkv, mem_rows, init, dks, dvs, rows
    )
    d_memory = (d_memory + d_slots[:slots]).reshape(2, 2, slot_part, width)
    d_away = jnp.concatenate(
        [
            pick(d_normed.reshape(2, 2, rows, width), 1 - core, 1),
            pick(d_memory, 1 - core, 1).astype(BF16),
        ],
        axis=1,
    )
    d_back = swap(d_away, 0, 1)
    d_tokens, g_gain_one = inputs_back(info, own, d_normed, d_back, d_middle, gains, rows)
    d_mem_mine = (pick(d_memory, core, 1) + d_back[:, rows:].astype(F32)).astype(BF16)

    g_misc = jnp.concatenate(
        [
            d_slots[slots:].reshape(devices, -1),
            jnp.concatenate([g_gain_one, g_gain_two]).reshape(devices, -1),
        ],
        axis=1,
    )
    g_misc = jnp.pad(g_misc, ((0, 0), (0, misc_rows * CORE_WIDTH - g_misc.shape[1])))
    g_small = jnp.concatenate(
        [
            g_qkv.reshape(devices // 2, 2 * own_rows, CORE_WIDTH),
            g_misc.reshape(devices // 2, 2 * misc_rows, CORE_WIDTH).astype(BF16),
        ],
        axis=1,
    )
    small = sum_to_chips(g_small)
    small_attn = small[: 2 * own_rows].reshape(2, own_rows, CORE_WIDTH)
    small_misc = small[2 * own_rows :].reshape(2, misc_rows, CORE_WIDTH)
    sent = jnp.concatenate([pick(small_attn, 1 - core), pick(small_misc, 1 - core)], axis=0)
    back = swap(sent, 0, 1)
    attn_grad = by_core(core, pick(small_attn, core), back[:own_rows], axis=1)
    misc_grad = (pick(small_misc, core) + back[own_rows:]).reshape(-1)

    def to_rank(big, small):
        mine = jnp.concatenate([pick(big, chip), pick(small, chip)], axis=0)
        away = jnp.concatenate([pick(big, 1 - chip), pick(small, 1 - chip)], axis=0)
        both = by_chip(chip, mine, swap(away, 0, 2))
        return both[:, :rows], both[:, rows:]

    new_mine = pick(new_rows.reshape(2, 2, slot_part, width), core, 1)
    output, new_memory = to_rank(result, new_mine)
    tokens_grad, memory_grad = to_rank(d_tokens, d_mem_mine)
    return (
        output,
        new_memory,
        tokens_grad,
        memory_grad,
        attn_grad.reshape(-1),
        *[part.reshape(-1) for part in big],
        misc_grad[memory_init.shape[0] :][: norm_gains.shape[0]],
        misc_grad[: memory_init.shape[0]],
    )


def solution(mesh):
    rows = P("batch", "seq", None)
    table = P("batch", None)
    flat = P(("batch", "seq"))
    return jax.shard_map(
        per_device,
        mesh=mesh,
        in_specs=(rows, rows, table, table, *[flat] * 8, rows, rows),
        out_specs=(rows, rows, rows, rows, *[flat] * 8),
        check_vma=False,
    )
```

time: 1000 us -> 342 us (0.34)
  matrix products: 279 us -> 0 us
  blocking collectives: 252 us -> 0 us
  Pallas kernels: 0 us -> 132 us
  waiting for transfers between devices: 215 us -> 102 us
  local copies, waits for them, and re-layouts: 132 us -> 46.4 us
  other arithmetic: 91.5 us -> 12 us
  starting transfers between devices: 0.99 us -> 30.3 us
    dot_general x108 -> x0, matrix products: 279 us -> none  [the longest x24 36.1 us: outer_sum(): lax.dot_general(inputs, grads, (((0,), (0,)), ((), ())), preferred_elemen...]
    unnamed x14 -> x1, waiting for transfers between devices: 202 us -> 0.02 us
    all_gather x13 -> x0, blocking collectives: 166 us -> none  [the longest x1 38.4 us: per_device(): lax.all_gather(attn_out, ('batch', 'seq'), axis=0, tiled=True)]
    pallas_call x0 -> x9, Pallas kernels: none -> 132 us  [the longest x1 34.1 us: attend_back(): pl.pallas_call(functools.partial(attend_back_kernel, 256, 1024), grid_spe...]
    ppermute x0 -> x31, waiting for transfers between devices: none -> 102 us  [swap(): return lax.ppermute(value, ('batch', 'seq'), pairs)]
    unnamed x2 -> x0, blocking collectives: 85.9 us -> none
    unnamed x511 -> x85, local copies, waits for them, and re-layouts: 60 us -> 17.3 us
    reduce_sum x21 -> x0, other arithmetic: 42.6 us -> none  [the longest x2 27.5 us: per_device(): run_total = run_total * carried + jnp.sum(expo, axis=-1)]
  transfers between devices with their start and end apart: 13 -> 32, of which waited for: 2 -> 14; matrix products, arithmetic and copies ran while one was open for 36% -> 12% of each run, Pallas kernels for 0% -> 30%
where the time goes in v1:
time: 342 us; the launch traced here: 338 us
  Pallas kernels  132 us (39%)
  waiting for transfers between devices  102 us (30%)
  local copies, waits for them, and re-layouts  46.4 us (14%)
  starting transfers between devices  30.3 us (9%)
  between operations  15.3 us (4%)
  other arithmetic  12 us (4%)
    ppermute x31, waiting for transfers between devices, swap(): return lax.ppermute(value, ('batch', 'seq'), pairs)  102 us
    pallas_call x1, Pallas kernels, attend_back(): pl.pallas_call(functools.partial(attend_back_kernel, 256, 1024), grid_spe...  34.1 us
    ppermute x31, starting transfers between devices, swap(): return lax.ppermute(value, ('batch', 'seq'), pairs)  30.2 us
    pallas_call x1, Pallas kernels, attend(): pl.pallas_call(functools.partial(attend_kernel, 256), grid=(heads // 2, 2...  24 us
    pallas_call x1, Pallas kernels, backward(): pl.pallas_call(backward_kernel, grid_spec=pltpu.PrefetchScalarGridSpec(nu...  23.7 us
    unnamed x85, local copies, waits for them, and re-layouts  17.3 us
    pallas_call x1, Pallas kernels, forward(): pl.pallas_call(forward_kernel, grid_spec=pltpu.PrefetchScalarGridSpec(num...  16.4 us
    pallas_call x1, Pallas kernels, project(): pl.pallas_call(project_kernel, grid_spec=pltpu.PrefetchScalarGridSpec(num...  9.23 us
  transfers between devices with their start and end apart: 32, of which 14 were waited for; matrix products, arithmetic and copies ran while one was open for 12% of the time, Pallas kernels for 30%

profile of v1, /device:TPU:8, one launch (start us, length us, event | category | flops | bytes accessed | tf_op | source)
XLA Modules:
  0.0 337.8 jit_solution(8917166797675538421)
XLA Ops:
  16.0 1.6 collective-permute-start.3
  20.1 9.2 %collective-permute-done = bf16[528,512]{1,0:T(8,128)(2,1)S(1)} collective-permute-done((bf16[528,512]{1,0:T(8,128)(2,1)S(1)}, bf16[528,512]{1,0:T(8,128)(2,1)S(1)}, u32[]{:S(2)}, u32[]{:S(2)}) %collective-permute-start) | collective-permute-done | bytes 540704 | tf_op jit(solution)/shard_map/ppermute | solution.py:732
  31.9 2.5 collective-permute-start.6
  36.0 14.1 %collective-permute-done.6 = bf16[4,106,256]{2,1,0:T(8,128)(2,1)S(1)} collective-permute-done((bf16[4,106,256]{2,1,0:T(8,128)(2,1)S(1)}, bf16[4,106,256]{2,1,0:T(8,128)(2,1)S(1)}, u32[]{:S(2)}, u32[]{:S(2)}) %collective-permute-start.6) | collective-permute-done | bytes 217120 | tf_op jit(solution)/shard_map/ppermute | solution.py:732
  50.1 5.9 %collective-permute-done.8 = bf16[4,106,256]{2,1,0:T(8,128)(2,1)S(1)} collective-permute-done((bf16[4,106,256]{2,1,0:T(8,128)(2,1)S(1)}, bf16[4,106,256]{2,1,0:T(8,128)(2,1)S(1)}, u32[]{:S(2)}, u32[]{:S(2)}) %collective-permute-start.8) | collective-permute-done | bytes 217120 | tf_op jit(solution)/shard_map/ppermute | solution.py:732
  59.8 9.2 %project.1 = (bf16[4,2048,128]{2,1,0:T(8,128)(2,1)}, bf16[4,2048,128]{2,1,0:T(8,128)(2,1)}, bf16[4,2048,128]{2,1,0:T(8,128)(2,1)}, bf16[2048,512]{1,0:T(8,128)(2...) custom-call(s32[14]{0:T(128)} %pad_add_fusion.info, ...), custom_call_target="tpu_custom_call" | custom-call | tf_op jit(solution)/shard_map/project/pallas_call | solution.py:149
  69.0 24.0 %attend.1 = (bf16[2048,256]{1,0:T(8,128)(2,1)}, bf16[4,2048,128]{2,1,0:T(8,128)(2,1)}) custom-call(bf16[4,2048,128]{2,1,0:T(8,128)(2,1)} %get-tuple-element.59.q_ref, bf16[4,2048,128]{2,1,0:T(8,128)(2,1)} %get-tuple-element.60.k_ref, bf16[4,2048,128]{2,1,0:T(8,128)(2,1)} %get-tuple-element.61.v_ref, bf16[4,128,128]{2,1,0:T(8,128)(2,1)} %get-tuple-element.62.ks_ref, ...), custom_call_target="tpu_custom_call" | custom-call | tf_op jit(solution)/shard_map/attend/pallas_call | solution.py:207
  94.2 3.9 %fusion.30 = (bf16[32,64,512]{2,1,0:T(8,128)(2,1)}, bf16[32,64,512]{2,1,0:T(8,128)(2,1)S(1)}) fusion(bf16[32,192,512]{2,1,0:T(8,128)(2,1)} %bitcast.208), kind=kLoop, calls=%fused_computation.143 | loop fusion | bytes 8388608 | tf_op jit(solution)/shard_map/slice | solution.py:850
  98.2 2.3 slice.150
  100.5 1.6 copy.68
  102.1 2.2 fusion.29
  105.2 16.4 %feed_forward.1 = (f32[2,512,512]{2,1,0:T(8,128)}, bf16[2,512,512]{2,1,0:T(8,128)(2,1)}, bf16[2,512,2048]{2,1,0:T(8,128)(2,1)}, bf16[2,512,2048]{2,1,0:T(8,128)(...) custom-call(s32[14]{0:T(128)} %pad_add_fusion.info, ...), custom_call_target="tpu_custom_call" | custom-call | tf_op jit(solution)/shard_map/feed_forward/pallas_call | solution.py:344
  121.6 4.6 %write.1 = (bf16[64,512]{1,0:T(8,128)(2,1)}, bf16[64,512]{1,0:T(8,128)(2,1)}, bf16[64,512]{1,0:T(8,128)(2,1)}, f32[3,64,512]{2,1,0:T(8,128)}) custom-call(bf16[2,512,512]{2,1,0:T(8,128)(2,1)} %get-tuple-element.66.keys, bf16[2,512,512]{2,1,0:T(8,128)(2,1)} %get-tuple-element.67.values, bf16[64,512]{1,0:T(8,128)(2,1)} %get-tuple-element.68.memory.rows_ref, ...), custom_call_target="tpu_custom_call" | custom-call | tf_op jit(solution)/shard_map/write/pallas_call | solution.py:549
  131.2 6.4 %write_back.1 = (bf16[64,512]{1,0:T(8,128)(2,1)}, bf16[2,512,512]{2,1,0:T(8,128)(2,1)}, bf16[2,512,512]{2,1,0:T(8,128)(2,1)}, bf16[64,512]{1,0:T(8,128)(2,1)}, b...) custom-call(s32[14]{0:T(128)} %pad_add_fusion.info, f32[3,64,512]{2,1,0:T(8,128)} %get-tuple-element.69.own, ...), custom_call_target="tpu_custom_call" | custom-call | tf_op jit(solution)/shard_map/write_back/pallas_call | solution.py:615
  137.6 23.7 %feed_forward_back.1 = (bf16[4,512,512]{2,1,0:T(8,128)(2,1)}, bf16[2048,512]{1,0:T(8,128)(2,1)}, bf16[512,512]{1,0:T(8,128)(2,1)}, bf16[2,512,512]{2,1,0:T(8,128...) custom-call(s32[14]{0:T(128)} %pad_add_fusion.info, ...), custom_call_target="tpu_custom_call" | custom-call | tf_op jit(solution)/shard_map/feed_forward_back/pallas_call | solution.py:453
  162.7 1.8 copy.73
  167.6 2.2 dynamic-slice_bitcast_fusion
  172.3 34.1 %attend_back.1 = (bf16[2048,256]{1,0:T(8,128)(2,1)}, bf16[2048,256]{1,0:T(8,128)(2,1)}, bf16[2048,256]{1,0:T(8,128)(2,1)}, bf16[128,256]{1,0:T(8,128)(2,1)}, bf16[128,256]{1,0:T(8,128)(2,1)}) custom-call(s32[14]{0:T(128)} %pad_add_fusion.info, bf16[4,2048,128]{2,1,0:T(8,128)(2,1)} %get-tuple-element.75.q_ref, bf16[4,2048,128]{2,1,0:T(8,128)(2,1)} %get-tuple-element.60.k_ref, ...), custom_call_target="tpu_custom_call" | custom-call | tf_op jit(solution)/shard_map/attend_back/pallas_call | solution.py:286
  206.4 8.0 %project_back.1 = (bf16[2048,512]{1,0:T(8,128)(2,1)}, bf16[3,512,256]{2,1,0:T(8,128)(2,1)}, f32[128,512]{1,0:T(8,128)}) custom-call(bf16[2048,512]{1,0:T(8,128)(2,1)} %get-tuple-element.74.normed, bf16[2048,256]{1,0:T(8,128)(2,1)} %get-tuple-element.88.dq, bf16[2048,256]{1,0:T(8,128)(2,1)} %get-tuple-element.89.dk, bf16[2048,256]{1,0:T(8,128)(2,1)} %get-tuple-element.90.dv, ...), custom_call_target="tpu_custom_call" | custom-call | tf_op jit(solution)/shard_map/project_back/pallas_call | solution.py:665
  220.1 12.8 %collective-permute-done.13 = bf16[528,512]{1,0:T(8,128)(2,1)S(1)} collective-permute-done((bf16[528,512]{1,0:T(8,128)(2,1)S(1)}, bf16[528,512]{1,0:T(8,128)(2,1)S(1)}, u32[]{:S(2)}, u32[]{:S(2)}) %collective-permute-start.13) | collective-permute-done | bytes 540704 | tf_op jit(solution)/shard_map/ppermute | solution.py:732
  235.8 5.2 %inputs_back.1 = (bf16[2,512,512]{2,1,0:T(8,128)(2,1)}, f32[1,512]{1,0:T(1,128)}) custom-call(s32[14]{0:T(128)} %pad_add_fusion.info, bf16[2,528,512]{2,1,0:T(8,128)(2,1)} %copy-done.2, bf16[2048,512]{1,0:T(8,128)(2,1)} %get-tuple-element.93.refs_1_, bf16[2,528,512]{2,1,0:T(8,128)(2,1)} %copy-done.10, f32[2,512,512]{2,1,0:T(8,128)} %get-tuple-element.96.refs_3_, ...), custom_call_target="tpu_custom_call" | custom-call | tf_op jit(solution)/shard_map/inputs_back/pallas_call | solution.py:704
  246.4 4.2 %collective-permute-done.17 = bf16[4,106,256]{2,1,0:T(8,128)(2,1)S(1)} collective-permute-done((bf16[4,106,256]{2,1,0:T(8,128)(2,1)S(1)}, bf16[4,106,256]{2,1,0:T(8,128)(2,1)S(1)}, u32[]{:S(2)}, u32[]{:S(2)}) %collective-permute-start.17) | collective-permute-done | bytes 217120 | tf_op jit(solution)/shard_map/ppermute | solution.py:732
  250.6 4.4 %collective-permute-done.18 = bf16[4,106,256]{2,1,0:T(8,128)(2,1)S(1)} collective-permute-done((bf16[4,106,256]{2,1,0:T(8,128)(2,1)S(1)}, bf16[4,106,256]{2,1,0:T(8,128)(2,1)S(1)}, u32[]{:S(2)}, u32[]{:S(2)}) %collective-permute-start.18) | collective-permute-done | bytes 217120 | tf_op jit(solution)/shard_map/ppermute | solution.py:732
  255.6 2.6 collective-permute-start.21
  260.0 1.6 collective-permute-done.21
  262.9 3.9 %fusion = bf16[16,192,512]{2,1,0:T(8,128)(2,1)S(1)} fusion(bf16[16,192,512]{2,1,0:T(8,128)(2,1)} %collective-permute-done.24, bf16[16,2,192,512]{3,2,1,0:T(8,128)(2,1)} %copy-done.4, s32[]{:T(128)S(6)} %select_n.242), kind=kLoop, calls=%fused_computation.1 | loop fusion | flops 6291456 | bytes 9437188 | tf_op jit(solution)/shard_map/convert_element_type | solution.py:896
  271.1 16.3 %collective-permute-done.25 = bf16[4,192,512]{2,1,0:T(8,128)(2,1)S(1)} collective-permute-done((bf16[4,192,512]{2,1,0:T(8,128)(2,1)S(1)}, bf16[4,192,512]{2,1,0:T(8,128)(2,1)S(1)}, u32[]{:S(2)}, u32[]{:S(2)}) %collective-permute-start.25) | collective-permute-done | bytes 786464 | tf_op jit(solution)/shard_map/ppermute | solution.py:732
  287.4 17.3 %collective-permute-done.26 = bf16[4,192,512]{2,1,0:T(8,128)(2,1)S(1)} collective-permute-done((bf16[4,192,512]{2,1,0:T(8,128)(2,1)S(1)}, bf16[4,192,512]{2,1,0:T(8,128)(2,1)S(1)}, u32[]{:S(2)}, u32[]{:S(2)}) %collective-permute-start.26) | collective-permute-done | bytes 786464 | tf_op jit(solution)/shard_map/ppermute | solution.py:732
  305.3 3.2 collective-permute-start.28
  313.2 2.2 collective-permute-done.28
  315.3 6.9 %collective-permute-done.29 = bf16[1,192,512]{2,1,0:T(8,128)(2,1)S(1)} collective-permute-done((bf16[1,192,512]{2,1,0:T(8,128)(2,1)S(1)}, bf16[1,192,512]{2,1,0:T(8,128)(2,1)S(1)}, u32[]{:S(2)}, u32[]{:S(2)}) %collective-permute-start.29) | collective-permute-done | bytes 196640 | tf_op jit(solution)/shard_map/ppermute | solution.py:732
  322.3 4.9 %collective-permute-done.30 = bf16[1,192,512]{2,1,0:T(8,128)(2,1)S(1)} collective-permute-done((bf16[1,192,512]{2,1,0:T(8,128)(2,1)S(1)}, bf16[1,192,512]{2,1,0:T(8,128)(2,1)S(1)}, u32[]{:S(2)}, u32[]{:S(2)}) %collective-permute-start.30) | collective-permute-done | bytes 196640 | tf_op jit(solution)/shard_map/ppermute | solution.py:732
  (228 shorter events, 63.0 us)
Async XLA Ops:
  7.2 87.0 %all-gather.3.cloned.1.call-start = ((), (), s32[]{:S(2)}) async-start(), calls=%async_computation | async-start | bytes 6488064 | tf_op jit(solution)/shard_map/all_gather | solution.py:849
  12.5 3.4 %collective-permute-start.2 = (bf16[53,256]{1,0:T(8,128)(2,1)S(1)}, bf16[53,256]{1,0:T(8,128)(2,1)S(1)}, u32[]{:S(2)}, u32[]{:S(2)}) collective-permute-start(bf16[53,256]{1,0:T(8,128)(2,1)S(1)} %pad_maximum_fusion.8), channel_id=1, source_target_pairs={{0,1},{1,0},{2,3},{3,2},{4,5},{5,4},{6,7},{7,6},{8,9},{9,8},{10,11... | collective-permute-start | bytes 81416 | tf_op jit(solution)/shard_map/ppermute | solution.py:732
  12.8 16.5 %collective-permute-start = (bf16[528,512]{1,0:T(8,128)(2,1)S(1)}, bf16[528,512]{1,0:T(8,128)(2,1)S(1)}, u32[]{:S(2)}, u32[]{:S(2)}) collective-permute-start(bf16[528,512]{1,0:T(8,128)(2,1)S(1)} %pad_maximum_fusion.1), channel_id=1, source_target_pairs={{0,2},{1,3},{2,0},{3,1},{4,6},{5,7},{6,4},{7,5},{8,10},{9,11},{10,... | collective-permute-start | bytes 1622024 | tf_op jit(solution)/shard_map/ppermute | solution.py:732
  14.5 112.2 %collective-permute-start.11 = (bf16[528,512]{1,0:T(8,128)(2,1)S(1)}, bf16[528,512]{1,0:T(8,128)(2,1)}, u32[]{:S(2)}, u32[]{:S(2)}) collective-permute-start(bf16[528,512]{1,0:T(8,128)(2,1)S(1)} %pad_maximum_fusion.2), channel_id=1, source_target_pairs={{0,2},{1,3},{2,0},{3,1},{4,6},{5,7},{6,4},{7,5},{8,10},{9,11},{10,... | collective-permute-start | bytes 1622024 | tf_op jit(solution)/shard_map/ppermute | solution.py:732
  16.0 15.7 %collective-permute-start.3 = (bf16[106,256]{1,0:T(8,128)(2,1)S(1)}, bf16[106,256]{1,0:T(8,128)(2,1)S(1)}, u32[]{:S(2)}, u32[]{:S(2)}) collective-permute-start(bf16[106,256]{1,0:T(8,128)(2,1)S(1)} %pad_maximum_fusion.6), channel_id=1, source_target_pairs={{0,24},{1,25},{2,26},{3,27},{4,28},{5,29},{6,30},{7,31},{8,16},{9,... | collective-permute-start | bytes 162824 | tf_op jit(solution)/shard_map/ppermute | solution.py:732
  17.7 14.1 %collective-permute-start.4 = (bf16[106,256]{1,0:T(8,128)(2,1)S(1)}, bf16[106,256]{1,0:T(8,128)(2,1)S(1)}, u32[]{:S(2)}, u32[]{:S(2)}) collective-permute-start(bf16[106,256]{1,0:T(8,128)(2,1)S(1)} %pad_maximum_fusion.6), channel_id=1, source_target_pairs={{0,16},{1,17},{2,18},{3,19},{4,20},{5,21},{6,22},{7,23},{8,24},{9,... | collective-permute-start | bytes 162824 | tf_op jit(solution)/shard_map/ppermute | solution.py:732
  18.9 12.8 %collective-permute-start.5 = (bf16[106,256]{1,0:T(8,128)(2,1)S(1)}, bf16[106,256]{1,0:T(8,128)(2,1)S(1)}, u32[]{:S(2)}, u32[]{:S(2)}) collective-permute-start(bf16[106,256]{1,0:T(8,128)(2,1)S(1)} %pad_maximum_fusion.6), channel_id=1, source_target_pairs={{0,8},{1,9},{2,10},{3,11},{4,12},{5,13},{6,14},{7,15},{8,0},{9,1},... | collective-permute-start | bytes 162824 | tf_op jit(solution)/shard_map/ppermute | solution.py:732
  31.6 27.2 %collective-permute-start.1 = (bf16[2,528,512]{2,1,0:T(8,128)(2,1)S(1)}, bf16[2,528,512]{2,1,0:T(8,128)(2,1)S(1)}, u32[]{:S(2)}, u32[]{:S(2)}) collective-permute-start(bf16[2,528,512]{2,1,0:T(8,128)(2,1)S(1)} %maximum_select_fusion.own.mem_own.tokens.refs_0_), channel_id=1, source_target_pairs={{0,1},{1,0},{2,3},{3,2},{4,5},{5,4},{6,7},{7,6},{8,9},{9,8},{10,11... | collective-permute-start | bytes 3244040 | tf_op jit(solution)/shard_map/ppermute | solution.py:732
  31.9 18.3 %collective-permute-start.6 = (bf16[4,106,256]{2,1,0:T(8,128)(2,1)S(1)}, bf16[4,106,256]{2,1,0:T(8,128)(2,1)S(1)}, u32[]{:S(2)}, u32[]{:S(2)}) collective-permute-start(bf16[4,106,256]{2,1,0:T(8,128)(2,1)S(1)} %pad_maximum_fusion.5), channel_id=1, source_target_pairs={{0,6},{1,7},{2,4},{3,5},{4,2},{5,3},{6,0},{7,1},{8,14},{9,15},{10,... | collective-permute-start | bytes 651272 | tf_op jit(solution)/shard_map/ppermute | solution.py:732
  34.4 15.7 %collective-permute-start.7 = (bf16[4,106,256]{2,1,0:T(8,128)(2,1)S(1)}, bf16[4,106,256]{2,1,0:T(8,128)(2,1)S(1)}, u32[]{:S(2)}, u32[]{:S(2)}) collective-permute-start(bf16[4,106,256]{2,1,0:T(8,128)(2,1)S(1)} %pad_maximum_fusion.5), channel_id=1, source_target_pairs={{0,4},{1,5},{2,6},{3,7},{4,0},{5,1},{6,2},{7,3},{8,12},{9,13},{10,... | collective-permute-start | bytes 651272 | tf_op jit(solution)/shard_map/ppermute | solution.py:732
  34.9 21.1 %collective-permute-start.8 = (bf16[4,106,256]{2,1,0:T(8,128)(2,1)S(1)}, bf16[4,106,256]{2,1,0:T(8,128)(2,1)S(1)}, u32[]{:S(2)}, u32[]{:S(2)}) collective-permute-start(bf16[4,106,256]{2,1,0:T(8,128)(2,1)S(1)} %pad_maximum_fusion.5), channel_id=1, source_target_pairs={{0,2},{1,3},{2,0},{3,1},{4,6},{5,7},{6,4},{7,5},{8,10},{9,11},{10,... | collective-permute-start | bytes 651272 | tf_op jit(solution)/shard_map/ppermute | solution.py:732
  94.1 10.2 %collective-permute-start.9 = (bf16[2,512,256]{2,1,0:T(8,128)(2,1)S(1)}, bf16[2,512,256]{2,1,0:T(8,128)(2,1)S(1)}, u32[]{:S(2)}, u32[]{:S(2)}) collective-permute-start(bf16[2,512,256]{2,1,0:T(8,128)(2,1)S(1)} %dynamic-slice_bitcast_fusion.11), channel_id=1, source_target_pairs={{0,1},{1,0},{2,3},{3,2},{4,5},{5,4},{6,7},{7,6},{8,9},{9,8},{10,11... | collective-permute-start | bytes 1572872 | tf_op jit(solution)/shard_map/ppermute | solution.py:732
  126.2 4.3 %collective-permute-start.10 = (f32[3,64,512]{2,1,0:T(8,128)}, f32[3,64,512]{2,1,0:T(8,128)S(1)}, u32[]{:S(2)}, u32[]{:S(2)}) collective-permute-start(f32[3,64,512]{2,1,0:T(8,128)} %get-tuple-element.69.own), channel_id=1, source_target_pairs={{0,1},{1,0},{2,3},{3,2},{4,5},{5,4},{6,7},{7,6},{8,9},{9,8},{10,11... | collective-permute-start | bytes 1179656 | tf_op jit(solution)/shard_map/ppermute | solution.py:732
  128.1 1.3 collective-permute-start.12
  161.4 10.1 %collective-permute-start.14 = (bf16[2,512,256]{2,1,0:T(8,128)(2,1)}, bf16[2,512,256]{2,1,0:T(8,128)(2,1)S(1)}, u32[]{:S(2)}, u32[]{:S(2)}) collective-permute-start(bf16[2,512,256]{2,1,0:T(8,128)(2,1)} %get-tuple-element.87), channel_id=1, source_target_pairs={{0,1},{1,0},{2,3},{3,2},{4,5},{5,4},{6,7},{7,6},{8,9},{9,8},{10,11... | collective-permute-start | bytes 1572872 | tf_op jit(solution)/shard_map/ppermute | solution.py:732
  171.1 91.7 %collective-permute-start.24 = (bf16[16,192,512]{2,1,0:T(8,128)(2,1)}, bf16[16,192,512]{2,1,0:T(8,128)(2,1)}, u32[]{:S(2)}, u32[]{:S(2)}) collective-permute-start(bf16[16,192,512]{2,1,0:T(8,128)(2,1)} %dynamic-slice_bitcast_fusion), channel_id=1, source_target_pairs={{0,1},{1,0},{2,3},{3,2},{4,5},{5,4},{6,7},{7,6},{8,9},{9,8},{10,11... | collective-permute-start | bytes 9437192 | tf_op jit(solution)/shard_map/ppermute | solution.py:732
  217.6 17.2 %collective-permute-start.15 = (bf16[2,528,512]{2,1,0:T(8,128)(2,1)}, bf16[2,528,512]{2,1,0:T(8,128)(2,1)S(1)}, u32[]{:S(2)}, u32[]{:S(2)}) collective-permute-start(bf16[2,528,512]{2,1,0:T(8,128)(2,1)} %pad_maximum_fusion), channel_id=1, source_target_pairs={{0,1},{1,0},{2,3},{3,2},{4,5},{5,4},{6,7},{7,6},{8,9},{9,8},{10,11... | collective-permute-start | bytes 3244040 | tf_op jit(solution)/shard_map/ppermute | solution.py:732
  218.5 14.4 %collective-permute-start.13 = (bf16[528,512]{1,0:T(8,128)(2,1)S(1)}, bf16[528,512]{1,0:T(8,128)(2,1)S(1)}, u32[]{:S(2)}, u32[]{:S(2)}) collective-permute-start(bf16[528,512]{1,0:T(8,128)(2,1)S(1)} %pad_maximum_fusion.3), channel_id=1, source_target_pairs={{0,2},{1,3},{2,0},{3,1},{4,6},{5,7},{6,4},{7,5},{8,10},{9,11},{10,... | collective-permute-start | bytes 1622024 | tf_op jit(solution)/shard_map/ppermute | solution.py:732
  242.0 8.6 %collective-permute-start.17 = (bf16[4,106,256]{2,1,0:T(8,128)(2,1)S(1)}, bf16[4,106,256]{2,1,0:T(8,128)(2,1)S(1)}, u32[]{:S(2)}, u32[]{:S(2)}) collective-permute-start(bf16[4,106,256]{2,1,0:T(8,128)(2,1)S(1)} %get-tuple-element.121), channel_id=1, source_target_pairs={{0,2},{1,3},{2,0},{3,1},{4,6},{5,7},{6,4},{7,5},{8,10},{9,11},{10,... | collective-permute-start | bytes 651272 | tf_op jit(solution)/shard_map/ppermute | solution.py:732
  243.5 11.5 %collective-permute-start.18 = (bf16[4,106,256]{2,1,0:T(8,128)(2,1)S(1)}, bf16[4,106,256]{2,1,0:T(8,128)(2,1)S(1)}, u32[]{:S(2)}, u32[]{:S(2)}) collective-permute-start(bf16[4,106,256]{2,1,0:T(8,128)(2,1)S(1)} %get-tuple-element.122), channel_id=1, source_target_pairs={{0,4},{1,5},{2,6},{3,7},{4,0},{5,1},{6,2},{7,3},{8,12},{9,13},{10,... | collective-permute-start | bytes 651272 | tf_op jit(solution)/shard_map/ppermute | solution.py:732
  245.0 10.0 %collective-permute-start.19 = (bf16[4,106,256]{2,1,0:T(8,128)(2,1)S(1)}, bf16[4,106,256]{2,1,0:T(8,128)(2,1)S(1)}, u32[]{:S(2)}, u32[]{:S(2)}) collective-permute-start(bf16[4,106,256]{2,1,0:T(8,128)(2,1)S(1)} %get-tuple-element.123), channel_id=1, source_target_pairs={{0,6},{1,7},{2,4},{3,5},{4,2},{5,3},{6,0},{7,1},{8,14},{9,15},{10,... | collective-permute-start | bytes 651272 | tf_op jit(solution)/shard_map/ppermute | solution.py:732
  255.1 4.9 %collective-permute-start.20 = (bf16[1,106,256]{2,1,0:T(8,128)(2,1)S(1)}, bf16[1,106,256]{2,1,0:T(8,128)(2,1)S(1)}, u32[]{:S(2)}, u32[]{:S(2)}) collective-permute-start(bf16[1,106,256]{2,1,0:T(8,128)(2,1)S(1)} %get-tuple-element.134), channel_id=1, source_target_pairs={{0,8},{1,9},{2,10},{3,11},{4,12},{5,13},{6,14},{7,15},{8,0},{9,1},... | collective-permute-start | bytes 162824 | tf_op jit(solution)/shard_map/ppermute | solution.py:732
  255.6 6.0 %collective-permute-start.21 = (bf16[1,106,256]{2,1,0:T(8,128)(2,1)S(1)}, bf16[1,106,256]{2,1,0:T(8,128)(2,1)S(1)}, u32[]{:S(2)}, u32[]{:S(2)}) collective-permute-start(bf16[1,106,256]{2,1,0:T(8,128)(2,1)S(1)} %get-tuple-element.136), channel_id=1, source_target_pairs={{0,16},{1,17},{2,18},{3,19},{4,20},{5,21},{6,22},{7,23},{8,24},{9,... | collective-permute-start | bytes 162824 | tf_op jit(solution)/shard_map/ppermute | solution.py:732
  258.2 4.5 %collective-permute-start.22 = (bf16[1,106,256]{2,1,0:T(8,128)(2,1)S(1)}, bf16[1,106,256]{2,1,0:T(8,128)(2,1)S(1)}, u32[]{:S(2)}, u32[]{:S(2)}) collective-permute-start(bf16[1,106,256]{2,1,0:T(8,128)(2,1)S(1)} %get-tuple-element.135), channel_id=1, source_target_pairs={{0,24},{1,25},{2,26},{3,27},{4,28},{5,29},{6,30},{7,31},{8,16},{9,... | collective-permute-start | bytes 162824 | tf_op jit(solution)/shard_map/ppermute | solution.py:732
  258.7 52.6 %collective-permute-start.16 = (bf16[528,512]{1,0:T(8,128)(2,1)S(1)}, bf16[528,512]{1,0:T(8,128)(2,1)S(1)}, u32[]{:S(2)}, u32[]{:S(2)}) collective-permute-start(bf16[528,512]{1,0:T(8,128)(2,1)S(1)} %pad_maximum_fusion.4), channel_id=1, source_target_pairs={{0,2},{1,3},{2,0},{3,1},{4,6},{5,7},{6,4},{7,5},{8,10},{9,11},{10,... | collective-permute-start | bytes 1622024 | tf_op jit(solution)/shard_map/ppermute | solution.py:732
  262.8 7.8 %collective-permute-start.23 = (f32[53,256]{1,0:T(8,128)S(1)}, f32[53,256]{1,0:T(8,128)S(1)}, u32[]{:S(2)}, u32[]{:S(2)}) collective-permute-start(f32[53,256]{1,0:T(8,128)S(1)} %pad_maximum_fusion.7), channel_id=1, source_target_pairs={{0,1},{1,0},{2,3},{3,2},{4,5},{5,4},{6,7},{7,6},{8,9},{9,8},{10,11... | collective-permute-start | bytes 162824 | tf_op jit(solution)/shard_map/ppermute | solution.py:732
  266.9 20.5 %collective-permute-start.25 = (bf16[4,192,512]{2,1,0:T(8,128)(2,1)S(1)}, bf16[4,192,512]{2,1,0:T(8,128)(2,1)S(1)}, u32[]{:S(2)}, u32[]{:S(2)}) collective-permute-start(bf16[4,192,512]{2,1,0:T(8,128)(2,1)S(1)} %get-tuple-element.110), channel_id=1, source_target_pairs={{0,2},{1,3},{2,0},{3,1},{4,6},{5,7},{6,4},{7,5},{8,10},{9,11},{10,... | collective-permute-start | bytes 2359304 | tf_op jit(solution)/shard_map/ppermute | solution.py:732
  268.3 36.5 %collective-permute-start.26 = (bf16[4,192,512]{2,1,0:T(8,128)(2,1)S(1)}, bf16[4,192,512]{2,1,0:T(8,128)(2,1)S(1)}, u32[]{:S(2)}, u32[]{:S(2)}) collective-permute-start(bf16[4,192,512]{2,1,0:T(8,128)(2,1)S(1)} %get-tuple-element.112), channel_id=1, source_target_pairs={{0,4},{1,5},{2,6},{3,7},{4,0},{5,1},{6,2},{7,3},{8,12},{9,13},{10,... | collective-permute-start | bytes 2359304 | tf_op jit(solution)/shard_map/ppermute | solution.py:732
  269.1 35.6 %collective-permute-start.27 = (bf16[4,192,512]{2,1,0:T(8,128)(2,1)S(1)}, bf16[4,192,512]{2,1,0:T(8,128)(2,1)S(1)}, u32[]{:S(2)}, u32[]{:S(2)}) collective-permute-start(bf16[4,192,512]{2,1,0:T(8,128)(2,1)S(1)} %get-tuple-element.111), channel_id=1, source_target_pairs={{0,6},{1,7},{2,4},{3,5},{4,2},{5,3},{6,0},{7,1},{8,14},{9,15},{10,... | collective-permute-start | bytes 2359304 | tf_op jit(solution)/shard_map/ppermute | solution.py:732
  305.3 10.1 %collective-permute-start.28 = (bf16[1,192,512]{2,1,0:T(8,128)(2,1)S(1)}, bf16[1,192,512]{2,1,0:T(8,128)(2,1)S(1)}, u32[]{:S(2)}, u32[]{:S(2)}) collective-permute-start(bf16[1,192,512]{2,1,0:T(8,128)(2,1)S(1)} %get-tuple-element.127), channel_id=1, source_target_pairs={{0,8},{1,9},{2,10},{3,11},{4,12},{5,13},{6,14},{7,15},{8,0},{9,1},... | collective-permute-start | bytes 589832 | tf_op jit(solution)/shard_map/ppermute | solution.py:732
  308.5 13.8 %collective-permute-start.29 = (bf16[1,192,512]{2,1,0:T(8,128)(2,1)S(1)}, bf16[1,192,512]{2,1,0:T(8,128)(2,1)S(1)}, u32[]{:S(2)}, u32[]{:S(2)}) collective-permute-start(bf16[1,192,512]{2,1,0:T(8,128)(2,1)S(1)} %get-tuple-element.129), channel_id=1, source_target_pairs={{0,16},{1,17},{2,18},{3,19},{4,20},{5,21},{6,22},{7,23},{8,24},{9,... | collective-permute-start | bytes 589832 | tf_op jit(solution)/shard_map/ppermute | solution.py:732
  308.5 18.7 %collective-permute-start.30 = (bf16[1,192,512]{2,1,0:T(8,128)(2,1)S(1)}, bf16[1,192,512]{2,1,0:T(8,128)(2,1)S(1)}, u32[]{:S(2)}, u32[]{:S(2)}) collective-permute-start(bf16[1,192,512]{2,1,0:T(8,128)(2,1)S(1)} %get-tuple-element.128), channel_id=1, source_target_pairs={{0,24},{1,25},{2,26},{3,27},{4,28},{5,29},{6,30},{7,31},{8,16},{9,... | collective-permute-start | bytes 589832 | tf_op jit(solution)/shard_map/ppermute | solution.py:732
  (32 other events, 110.3 us)
Sparse Core Ops, SparseCore 0:
  12.3 76.4 all-gather.2

commit v2 on v1

v2 whole, which is shorter than its diff:
```python
import functools
import math

import jax
import jax.numpy as jnp
from jax import lax
from jax.experimental import pallas as pl
from jax.experimental.pallas import tpu as pltpu
from jax.sharding import PartitionSpec as P

HEADS = 8
HEAD_DIM = 64
FF = 2048
SEGMENT = 512
MASKED = -1e30
LANES = 128
CORE_HEADS = HEADS // 2
CORE_WIDTH = CORE_HEADS * HEAD_DIM
SCALE = HEAD_DIM ** (-0.5)
EXP = math.log2(math.e) * SCALE
LOG2E = math.log2(math.e)
RESET_COL = 8
LOG_COL = 10
NT = (((1,), (1,)), ((), ()))
NN = (((1,), (0,)), ((), ()))
TN = (((0,), (0,)), ((), ()))
GELU_A = math.sqrt(2.0 / math.pi)
GELU_B = 0.044715
BF16 = jnp.bfloat16
F32 = jnp.float32


def dot(left, right, dims=NN):
    return lax.dot_general(left, right, dims, preferred_element_type=F32)


def streamed(kernel, name, info, arrays, outs, scratch=(), grid=(1,)):
    arrays = [a if isinstance(a, tuple) else (a, a.shape, [((), ())]) for a in arrays]
    count = sum(len(pieces) for _, _, pieces in arrays)

    def at(ref, place):
        return ref.at[place] if place else ref

    def body(info, *refs):
        n, m = len(arrays), len(outs)
        far, far_out, refs = refs[:n], refs[n : n + m], refs[n + m :]
        near, near_out, refs = refs[:n], refs[n : n + m], refs[n + m :]
        own, sems, out_sems = refs[:-2], refs[-2], refs[-1]
        step = pl.program_id(0)
        copies = []
        for k, (_, _, pieces) in enumerate(arrays):
            first = sum(map(len, copies))
            copies.append(
                [
                    pltpu.make_async_copy(at(far[k], a), at(near[k], b), sems.at[first + j])
                    for j, (a, b) in enumerate(pieces)
                ]
            )

        @pl.when(step == 0)
        def _():
            for group in copies:
                for copy in group:
                    copy.start()

        def need(k, j=0, when=0):
            pl.when(step == when)(copies[k][j].wait)

        def give(k, *place):
            pltpu.make_async_copy(
                at(near_out[k], place), at(far_out[k], place), out_sems.at[k]
            ).start()

        kernel(need, give, info, *near, *near_out, *own)

        @pl.when(step == pl.num_programs(0) - 1)
        def _():
            for k in range(m):
                pltpu.make_async_copy(near_out[k], far_out[k], out_sems.at[k]).wait()

    space = pl.BlockSpec(memory_space=pl.ANY)
    return pl.pallas_call(
        body,
        grid_spec=pltpu.PrefetchScalarGridSpec(
            num_scalar_prefetch=1,
            grid=grid,
            in_specs=[space] * len(arrays),
            out_specs=[space] * len(outs),
            scratch_shapes=[
                *[pltpu.VMEM(shape, array.dtype) for array, shape, _ in arrays],
                *[pltpu.VMEM(shape, kind) for shape, kind in outs],
                *scratch,
                pltpu.SemaphoreType.DMA((count,)),
                pltpu.SemaphoreType.DMA((len(outs),)),
            ],
        ),
        out_shape=[jax.ShapeDtypeStruct(shape, kind) for shape, kind in outs],
        compiler_params=pltpu.CompilerParams(vmem_limit_bytes=58 << 20),
        name=name,
    )(info, *[array for array, _, _ in arrays])


def norm_parts(values):
    centred = values - jnp.mean(values, axis=-1, keepdims=True)
    scale = lax.rsqrt(jnp.mean(centred * centred, axis=-1, keepdims=True) + 1e-05)
    return centred * scale, scale


def norm_back(unit, scale, grad, gain):
    back = grad * gain
    return scale * (
        back
        - jnp.mean(back, axis=-1, keepdims=True)
        - unit * jnp.mean(back * unit, axis=-1, keepdims=True)
    )


def in_three(values):
    high = values.astype(BF16).astype(F32)
    rest = values - high
    middle = rest.astype(BF16).astype(F32)
    return high, middle, rest - middle


def put_log(column, values, others):
    high, middle, low = in_three(values)
    out = jnp.where(column == LOG_COL, high, others)
    out = jnp.where(column == LOG_COL + 1, middle, out)
    return jnp.where(column == LOG_COL + 2, low, out)


def aux_column(shape, parity):
    lane = lax.broadcasted_iota(jnp.int32, shape, 1)
    return lane - (1 - parity) * HEAD_DIM


OWNERS = 32
OUT, VALUE, WRITE, UP, DOWN = range(5)
FIELDS = (16, 16, 32, 64, 64)
CUTS = tuple(sum(FIELDS[:k]) for k in range(len(FIELDS) + 1))
PACKED = CUTS[-1]
CHUNKS = 4
PART = FIELDS[UP] // CHUNKS


def flat_rows(block):
    return block.reshape(-1, block.shape[-1])


def take(packed, field):
    return flat_rows(packed[:, CUTS[field] : CUTS[field + 1], :])


def take_up(packed, chunk):
    if isinstance(chunk, int):
        at = CUTS[UP] + chunk * PART
    else:
        at = pl.multiple_of(CUTS[UP] + chunk * PART, PART)
    return flat_rows(packed[:, pl.ds(at, PART), :])


def take_down(packed, chunk):
    count = OWNERS // CHUNKS
    return flat_rows(packed[pl.ds(chunk * count, count), CUTS[DOWN] : CUTS[DOWN + 1], :])


def put(core, kept, away, value, owner, owners, at, rows):
    split = value.reshape(owners // 2, 2, rows, value.shape[-1])
    place = (pl.ds(owner, owners // 2), pl.ds(at, rows), slice(None))
    kept[place] = jnp.where(core == 0, split[:, 0], split[:, 1]).astype(BF16)
    away[place] = jnp.where(core == 0, split[:, 1], split[:, 0]).astype(BF16)


def by_head(out, place, pair, mine, side):
    lane = lax.broadcasted_iota(jnp.int32, mine.shape, 1)
    out[2 * pair, place, :] = jnp.where(lane < HEAD_DIM, mine, side).astype(BF16)
    out[2 * pair + 1, place, :] = jnp.where(lane < HEAD_DIM, side, mine).astype(BF16)


def choose(rank, core, chip, mine, recv, mine_other, recv_other):
    here = jnp.where(rank // 2 == chip, mine, recv)
    there = jnp.where(rank // 2 == chip, mine_other, recv_other)
    return jnp.where(rank % 2 == core, here, there)


def qkv_weight(packed, which):
    pairs = packed.shape[0]
    width = 2 * CORE_WIDTH
    rows = 3 * width // pairs
    if width % rows == 0:
        return flat_rows(packed[which * width // rows : (which + 1) * width // rows, :rows, :])
    return flat_rows(packed[:, :rows, :])[which * width : (which + 1) * width]


def project_step(
    need, give, info, rank, packed, init, gain, sources,
    q_out, k_out, v_out, normed_out, ks_out, vs_out, rows_out, tokens_out, scale_out, w_ref,
):
    core, chip = info[0], info[1]
    rows = normed_out.shape[0] // 4
    shape = (rows, LANES)
    column = lax.broadcasted_iota(jnp.int32, (1, LANES), 1) % HEAD_DIM

    @pl.when(rank == 0)
    def _():
        need(0)
        for which in range(3):
            w_ref[which] = qkv_weight(packed, which)
        for k in range(1, 7):
            need(k)
        slots = rows_out.shape[0]
        part = slots // 4
        for k in range(4):
            rows_out[k * part : (k + 1) * part, :] = choose(
                k, core, chip, *[ref[rows:, :] for ref in sources]
            )
        source = jnp.concatenate([rows_out[...], init[...]], axis=0)
        shape = (2 * slots, LANES)
        start = (lax.broadcasted_iota(jnp.int32, shape, 0) >= slots).astype(jnp.int32)
        ones = jnp.where((column >= LOG_COL) & (column < LOG_COL + 3), 1.0, 0.0)
        side = jnp.where(column == RESET_COL + start, MASKED, ones)
        keys = dot(source, w_ref[1])
        values = dot(source, w_ref[2])
        whole = slice(0, 2 * slots)
        for pair in range(CORE_HEADS // 2):
            lanes = slice(pair * LANES, (pair + 1) * LANES)
            by_head(ks_out, whole, pair, keys[:, lanes], side)
            by_head(vs_out, whole, pair, values[:, lanes], jnp.ones(shape, F32))
        for k in (KS, VS, ROWS):
            give(k)

    values = choose(rank, core, chip, *[ref[:rows, :] for ref in sources])

    @pl.when(rank % 2 == core)
    def _():
        tokens_out[rank // 2] = values
        give(TOKENS, rank // 2)

    unit, scale = norm_parts(values.astype(F32))
    normed = (unit * gain[0:1, :].astype(F32)).astype(BF16)
    place = pl.ds(pl.multiple_of(rank * rows, rows), rows)
    normed_out[place, :] = normed
    give(NORMED, place)
    scale_out[place, :] = jnp.broadcast_to(scale, (rows, LANES))
    give(SCALES, place)
    low = jnp.zeros((1, LANES), jnp.int32)
    high = jnp.zeros((1, LANES), jnp.int32)
    for k in range(8):
        low = jnp.where(column == k, info[1 + k] if k else 0, low)
        high = jnp.where(column == k, info[2 + k], high)
    reset = info[10 + (rank * rows) // SEGMENT]
    position = rank * rows + lax.broadcasted_iota(jnp.int32, shape, 0)
    here = (position >= low) & (position < high)
    fixed = jnp.where(column == RESET_COL + 1 - reset, 1.0, 0.0)
    q_side = jnp.where(here, 1.0, jnp.broadcast_to(fixed, shape))
    ones = jnp.where((column >= LOG_COL) & (column < LOG_COL + 3), 1.0, 0.0)
    others = jnp.where(column < 8, MASKED, ones)
    k_side = jnp.where(here, 0.0, jnp.broadcast_to(others, shape))
    for which, out, side in ((0, q_out, q_side), (1, k_out, k_side), (2, v_out, jnp.ones(shape, F32))):
        result = dot(normed, w_ref[which])
        for pair in range(CORE_HEADS // 2):
            by_head(out, place, pair, result[:, pair * LANES : (pair + 1) * LANES], side)


    @pl.when(rank == 3)
    def _():
        give(K)
        give(V)


Q_LOG, K, V, KS, VS, NORMED, TOKENS, ROWS, O, O_AWAY, SCALES = range(11)


def attend_step(block, give, info, head, q_ref, k_ref, v_ref, ks_ref, vs_ref, q_out, o_ref, away):
    core = info[0]
    length = q_ref.shape[1]
    rows = away.shape[2]
    pair, parity = head // 2, head % 2
    column = aux_column((block, LANES), parity)
    keep = (column < 0) | (column >= HEAD_DIM)
    row = lax.broadcasted_iota(jnp.int32, (block, block), 0)
    key = lax.broadcasted_iota(jnp.int32, (block, block), 1)
    for i in range(length // block):
        low, high = i * block, (i + 1) * block
        q = q_ref[head, low:high, :]
        slot = dot(q, ks_ref[head], NT)
        scores = dot(q, k_ref[head, :high, :], NT)
        last = jnp.where(row >= key, scores[:, low:], MASKED)
        scores = jnp.concatenate([scores[:, :low], last], axis=1) if i else last
        top = jnp.maximum(
            jnp.max(scores, axis=1, keepdims=True), jnp.max(slot, axis=1, keepdims=True)
        )
        share = jnp.exp2((scores - top) * EXP).astype(BF16)
        slot_share = jnp.exp2((slot - top) * EXP).astype(BF16)
        total = dot(share, v_ref[head, :high, :]) + dot(slot_share, vs_ref[head])
        count = jnp.where(parity == 0, total[:, HEAD_DIM : HEAD_DIM + 1], total[:, 0:1])
        o_ref[pair, low:high, :] = jnp.where(
            keep, (total / count).astype(BF16), o_ref[pair, low:high, :]
        )
        log = top + jnp.log2(count) * (1.0 / EXP)
        q_out[head, low:high, :] = put_log(column, -log, q.astype(F32)).astype(BF16)
    give(Q_LOG, head)

    @pl.when(parity == 1)
    def _():
        for rank in range(4):

            @pl.when(core != rank % 2)
            def _():
                away[rank // 2, pair] = o_ref[pair, rank * rows : (rank + 1) * rows, :]

        give(O, pair)
        give(O_AWAY, slice(None), pair)


def read_kernel(
    need, give, info, packed, init, gain, mine, recv, mine_other, recv_other,
    q_log, k, v, ks, vs, normed, tokens, rows, o, o_away, scales, q, w_ref,
):
    step = pl.program_id(0)

    @pl.when(step < 4)
    def _():
        project_step(
            need, give, info, step, packed, init, gain, (mine, recv, mine_other, recv_other),
            q, k, v, normed, ks, vs, rows, tokens, scales, w_ref,
        )

    @pl.when(step >= 4)
    def _():
        attend_step(256, give, info, step - 4, q, k, v, ks, vs, q_log, o, o_away)


def read(info, sources, packed, init, gains, rows):
    total, width = sources[0].shape
    slots = 4 * (total - rows)
    length = 4 * rows
    heads = ((CORE_HEADS, length, LANES), BF16)
    slot = ((CORE_HEADS, 2 * slots, LANES), BF16)
    return streamed(
        read_kernel, "read", info, (packed, init, gains, *sources),
        (heads, heads, heads, slot, slot, ((length, width), BF16), ((2, rows, width), BF16),
         ((slots, width), BF16), ((2, length, LANES), BF16), ((2, 2, rows, LANES), BF16), ((length, LANES), F32)),
        [pltpu.VMEM((CORE_HEADS, length, LANES), BF16), pltpu.VMEM((3, width, CORE_WIDTH), BF16)],
        grid=(4 + CORE_HEADS,),
    )


def attend_back_kernel(
    kb, qb, first_head, info, q_ref, k_ref, v_ref, ks_ref, vs_ref, own_ref, other_ref, o_ref,
    dq_ref, dk_ref, dv_ref, dks_ref, dvs_ref, d_ref, acc_ref,
):
    length = q_ref.shape[1]
    step = pl.program_id(0)
    head = first_head + step
    pair, parity = head // 2, head % 2
    core = info[0]
    rows = own_ref.shape[2]
    column = aux_column((rows, LANES), parity)
    inside = (column < 0) | (column >= HEAD_DIM)
    for r in range(length // rows):
        low, high = r * rows, (r + 1) * rows
        d = jnp.where(core == r % 2, own_ref[r // 2, pair], other_ref[r // 2, pair]).astype(F32)
        delta = jnp.sum(
            jnp.where(inside, d * o_ref[pair, low:high, :].astype(F32), 0.0), axis=1, keepdims=True
        )
        d_ref[low:high, :] = jnp.where(
            inside, d, put_log(column, -delta, jnp.zeros_like(d))
        ).astype(BF16)
    acc_ref[...] = jnp.zeros_like(acc_ref)

    count = ks_ref.shape[1]
    pieces = [(ks_ref, vs_ref, dks_ref, dvs_ref, 0, count, None)]
    pieces += [(k_ref, v_ref, dk_ref, dv_ref, j, j + kb, j) for j in range(0, length, kb)]
    for keys, values, dk_out, dv_out, start, stop, first in pieces:
        k = keys[step, start:stop, :]
        v = values[step, start:stop, :]
        turned = k.astype(F32).T.astype(BF16)
        dk = jnp.zeros((stop - start, LANES), F32)
        dv = jnp.zeros((stop - start, LANES), F32)
        low = first or 0
        while low < length:
            high = min((low // qb + 1) * qb, length)
            q = q_ref[step, low:high, :]
            d = d_ref[low:high, :]
            scores = dot(k, q, NT)
            share = jnp.exp2(scores * EXP)
            if first is not None and low < stop:
                key = first + lax.broadcasted_iota(jnp.int32, scores.shape, 0)
                position = low + lax.broadcasted_iota(jnp.int32, scores.shape, 1)
                share = jnp.where(key <= position, share, 0.0)
            ds = (share * dot(v, d, NT)).astype(BF16)
            dv = dv + dot(share.astype(BF16), d)
            dk = dk + dot(ds, q)
            acc_ref[:, low:high] += dot(turned, ds)
            low = high
        dk_out[step, start:stop, :] = (dk * SCALE).astype(BF16)
        dv_out[step, start:stop, :] = dv.astype(BF16)
    dq_ref[step] = (acc_ref[...].T * SCALE).astype(BF16)


def of_heads(array, first, heads):
    shape = (heads, *array.shape[1:])
    return array, shape, [((first + j,), (j,)) for j in range(heads)]


def some_heads_kernel(first, need, give, info, *refs):
    step = pl.program_id(0)
    for k in (5, 6, 7):
        need(k)
    for k in range(5):
        for j in range(refs[k].shape[0]):
            need(k, j, j)
    attend_back_kernel(256, 1024, first, info, *refs)
    for k in range(5):
        give(k, step)


def attend_back(info, first, heads, q, k, v, ks, vs, own, other, o):
    _, length, _ = q.shape
    out = ((heads, length, LANES), BF16)
    slot_out = ((heads, ks.shape[1], LANES), BF16)
    arrays = [of_heads(array, first, heads) for array in (q, k, v, ks, vs)]
    return streamed(
        functools.partial(some_heads_kernel, first), "attend_back", info,
        (*arrays, own, other, o), (out, out, out, slot_out, slot_out),
        [pltpu.VMEM((length, LANES), BF16), pltpu.VMEM((LANES, length), F32)], grid=(heads,),
    )


def side_by_side(tiles):
    return jnp.concatenate(tiles, axis=1)


MIDDLE, NORMED_TWO, ACT, SLOPE, RESULT, KEYS, VALUES, AWAY, WQ, SK, SV, STATS = range(12)


def forward_kernel(
    need, give, info, own, other, tokens_ref, gains, packed, memory,
    middle_out, normed_out, act_out, slope_out, result_out, keys_out, values_out, away_out,
    query_out, key_out, value_out, stats,
):
    core, chip = info[0], info[1]
    half = CORE_WIDTH // FIELDS[OUT]
    for k in range(4):
        need(k)
    need(4, OUT)
    w_own = flat_rows(packed[pl.ds(core * half, half), : FIELDS[OUT], :])
    w_other = flat_rows(packed[pl.ds((1 - core) * half, half), : FIELDS[OUT], :])
    step = pl.program_id(0)
    rows = normed_out.shape[1]
    block = 2 * rows // pl.num_programs(0)
    which, at = step // (rows // block), pl.multiple_of(step % (rows // block) * block, block)
    place = (which, pl.ds(at, block))
    tokens = tokens_ref[place]
    start = pl.multiple_of((2 * which + core) * rows + at, block)
    o_own = side_by_side([own[pair, pl.ds(start, block), :] for pair in range(2)])
    o_other = side_by_side([other[which, pair, pl.ds(at, block), :] for pair in range(2)])
    middle = tokens.astype(F32) + (dot(o_own, w_own) + dot(o_other, w_other))
    middle_out[place] = middle
    unit, _ = norm_parts(middle)
    normed = (unit * gains[1:2, :].astype(F32)).astype(BF16)
    normed_out[place] = normed
    width = normed.shape[1]
    need(4, UP)
    for k in range(CHUNKS):
        pre = dot(normed, take_up(packed, k))
        square = pre * pre
        half = 0.5 + 0.5 * jnp.tanh(pre * (GELU_A + (GELU_A * GELU_B) * square))
        turn = (half - half * half) * (2.0 * GELU_A + (6.0 * GELU_A * GELU_B) * square)
        act_out[(k, *place)] = (pre * half).astype(BF16)
        slope_out[(k, *place)] = (half + pre * turn).astype(BF16)
    acts = side_by_side([act_out[(k, *place)] for k in range(CHUNKS)])
    need(4, DOWN)
    low = (middle + dot(acts, take(packed, DOWN))).astype(BF16)
    result_out[place] = low

    @pl.when(which != chip)
    def _():
        away_out[pl.ds(at, block), :] = low
        give(AWAY, pl.ds(at, block))

    need(4, WRITE)
    need(4, VALUE)
    need(5)
    keys_out[place] = dot(low, flat_rows(packed[OWNERS // 2 :, CUTS[WRITE] : CUTS[WRITE + 1], :])).astype(BF16)
    values_out[place] = dot(low, take(packed, VALUE)).astype(BF16)


    for k in (MIDDLE, NORMED_TWO, RESULT, KEYS, VALUES):
        give(k, *place)
    for k in (ACT, SLOPE):
        give(k, slice(None), *place)

    @pl.when(step == pl.num_programs(0) - 1)
    def _():
        write_step(keys_out, values_out, memory, packed, query_out, key_out, value_out, stats)
        for k in (WQ, SK, SV, STATS):
            give(k)


def fields_of(packed):
    pieces = [(slice(None), slice(CUTS[k], CUTS[k + 1])) for k in range(len(FIELDS))]
    return packed, packed.shape, [(piece, piece) for piece in pieces]


def forward(info, tokens, o, other, packed, gains, memory):
    _, rows, width = tokens.shape
    slots = memory.shape[0]
    small = ((2, rows, width), BF16)
    wide = ((CHUNKS, 2, rows, FF // CHUNKS), BF16)
    slot = ((slots, width), BF16)
    return streamed(
        forward_kernel, "feed_forward", info, (o, other, tokens, gains, fields_of(packed), memory),
        (((2, rows, width), F32), small, wide, wide, small, small, small, ((rows, width), BF16),
         slot, slot, slot, ((3, slots, width), F32)),
        grid=(4,),
    )


KEPT, SENT, D_MIDDLE, D_OWN, D_OTHER, G_GAIN, D_MEMORY, NEW_ROWS = range(8)


def backward_kernel(
    need, give, info, stats, stats_other, query, key, value, rows_ref, cot_mine, cot_recv,
    cot_other, keys, values, packed, result, normed, act, slope, middle, own, other, gains,
    kept, away, d_middle_out, d_own, d_other, g_gain, d_memory, new_out,
    d_keys, d_values, d_query, d_self_key, d_self_value, mem_cot,
    d_result_ref, d_update_ref, d_normed_ref,
):
    step = pl.program_id(0)
    core, chip = info[0], info[1]
    count, rows, width = result.shape
    total = count * rows
    half = CORE_WIDTH // FIELDS[OUT]

    @pl.when(step == 0)
    def _():
        for k in range(11):
            need(k)
        write_back_step(
            info, stats, stats_other, query, key, value, rows_ref, cot_mine, cot_recv, cot_other,
            keys, values, new_out, d_keys, d_values, d_query, d_self_key, d_self_value, mem_cot,
        )
        give(NEW_ROWS)
        need(11, WRITE)
        need(11, VALUE)
        need(12)

    @pl.when(step == 0)
    def _():
        dk = d_keys[...].reshape(total, width)
        dv = d_values[...].reshape(total, width)
        w_query = flat_rows(packed[: OWNERS // 2, CUTS[WRITE] : CUTS[WRITE + 1], :])
        w_key = flat_rows(packed[OWNERS // 2 :, CUTS[WRITE] : CUTS[WRITE + 1], :])
        w_value = take(packed, VALUE)
        first, second = cot_mine[:rows, :].astype(F32), cot_recv[:rows, :].astype(F32)
        cot = jnp.concatenate(
            [jnp.where(chip == 0, first, second), jnp.where(chip == 0, second, first)], axis=0
        )
        d_result = cot + (dot(dk, w_key, NT) + dot(dv, w_value, NT))
        d_result_ref[...] = d_result
        d_update_ref[...] = d_result.astype(BF16)
        d_normed_ref[...] = jnp.zeros_like(d_normed_ref)
        out = result[...].reshape(total, width)
        memory = rows_ref[...]
        put(core, kept, away, dot(memory, d_query[...], TN), 0, OWNERS // 2, CUTS[WRITE], FIELDS[WRITE])
        put(
            core, kept, away, dot(out, dk, TN) + dot(memory, d_self_key[...], TN),
            OWNERS // 4, OWNERS // 2, CUTS[WRITE], FIELDS[WRITE],
        )
        put(
            core, kept, away, dot(out, dv, TN) + dot(memory, d_self_value[...], TN),
            0, OWNERS, CUTS[VALUE], FIELDS[VALUE],
        )
        d_memory[...] = mem_cot[...] + (
            dot(d_query[...], w_query, NT)
            + dot(d_self_key[...], w_key, NT)
            + dot(d_self_value[...], w_value, NT)
        )
        give(D_MEMORY)
        need(11, DOWN)
        need(11, UP)
        need(13)

    for j in range(CHUNKS):
        need(14, j, j)
        need(15, j, j)
    d_update = d_update_ref[...]
    d_act = dot(d_update, take_down(packed, step), NT)
    d_hidden = (d_act * slope[step].reshape(total, -1).astype(F32)).astype(BF16)
    g_down = dot(act[step].reshape(total, -1), d_update, TN)
    owners = OWNERS // CHUNKS
    put(core, kept, away, g_down, step * (owners // 2), owners, CUTS[DOWN], FIELDS[DOWN])
    g_up = dot(normed[...].reshape(total, width), d_hidden, TN)
    at = pl.multiple_of(CUTS[UP] + step * PART, PART)
    put(core, kept, away, g_up, 0, OWNERS, at, PART)
    d_normed_ref[...] += dot(d_hidden, take_up(packed, step), NT)

    @pl.when(step == pl.num_programs(0) - 1)
    def _():
        for k in (16, 17, 18, 19):
            need(k, 0, CHUNKS - 1)
        need(11, OUT, CHUNKS - 1)
        gain = gains[1:2, :].astype(F32)
        unit, scale = norm_parts(middle[...].reshape(total, width))
        d_normed = d_normed_ref[...]
        g_gain[...] = jnp.sum(d_normed * unit, axis=0, keepdims=True)
        d_middle = d_result_ref[...] + norm_back(unit, scale, d_normed, gain)
        d_middle_out[...] = d_middle.reshape(count, rows, width)
        give(D_MIDDLE)
        give(G_GAIN)
        d_branch = d_middle.astype(BF16)
        for start, out in ((core * half, d_own), ((1 - core) * half, d_other)):
            weight = flat_rows(packed[pl.ds(start, half), : FIELDS[OUT], :])
            back = dot(d_branch, weight, NT).astype(BF16)
            for k in range(count):
                for pair in range(2):
                    lanes = slice(pair * LANES, (pair + 1) * LANES)
                    out[k, pair] = back[k * rows : (k + 1) * rows, lanes]
        give(D_OWN)
        give(D_OTHER)
        own_rows = jnp.concatenate(
            [
                side_by_side(
                    [
                        own[pair, pl.ds(pl.multiple_of((2 * k + core) * rows, rows), rows), :]
                        for pair in range(2)
                    ]
                )
                for k in range(count)
            ],
            axis=0,
        )
        other_rows = jnp.concatenate([side_by_side([other[k, 0], other[k, 1]]) for k in range(count)], axis=0)
        g_own = dot(own_rows, d_branch, TN)
        g_other = dot(other_rows, d_branch, TN)
        put(core, kept, away, g_own, core * (half // 2), half, 0, FIELDS[OUT])
        put(core, kept, away, g_other, (1 - core) * (half // 2), half, 0, FIELDS[OUT])
        give(SENT)
        give(KEPT)


def by_chunk(array):
    return array, array.shape, [((j,), (j,)) for j in range(CHUNKS)]


def backward(info, stats, stats_other, writer, memory, cots, cot_other, keys, values, packed,
             result, normed, act, slope, middle, o, other, gains):
    _, rows, width = result.shape
    slots = memory.shape[0]
    grads = ((OWNERS // 2, PACKED, width), BF16)
    half = ((2, 2, rows, LANES), BF16)
    slot = pltpu.VMEM((slots, width), BF16)
    return streamed(
        backward_kernel, "feed_forward_back", info,
        (stats, stats_other, *writer, memory, *cots, cot_other, keys, values, fields_of(packed),
         result, normed, by_chunk(act), by_chunk(slope), middle, o, other, gains),
        (grads, grads, ((2, rows, width), F32), half, half, ((1, width), F32),
         ((slots, width), F32), ((slots, width), BF16)),
        [pltpu.VMEM((2, rows, width), BF16), pltpu.VMEM((2, rows, width), BF16), slot, slot, slot,
         pltpu.VMEM((slots, width), F32),
         pltpu.VMEM((2 * rows, width), F32), pltpu.VMEM((2 * rows, width), BF16),
         pltpu.VMEM((2 * rows, width), F32)],
        grid=(CHUNKS,),
    )


def head_mask(shape, head):
    lane = lax.broadcasted_iota(jnp.int32, shape, 1)
    return (lane >= head * HEAD_DIM) & (lane < (head + 1) * HEAD_DIM)


def stacked_heads(values):
    return jnp.concatenate(
        [jnp.where(head_mask(values.shape, h), values, 0.0) for h in range(HEADS)], axis=0
    )


def joined_heads(stacked, slots):
    out = None
    for h in range(HEADS):
        part = stacked[h * slots : (h + 1) * slots, :]
        shape = (slots, HEADS * HEAD_DIM)
        part = jnp.broadcast_to(part, shape)
        out = part if out is None else jnp.where(head_mask(shape, h), part, out)
    return out


def column_of_heads(values):
    return jnp.concatenate(
        [values[:, h * HEAD_DIM : h * HEAD_DIM + 1] for h in range(HEADS)], axis=0
    )


def head_sums(values):
    return jnp.concatenate(
        [
            jnp.sum(jnp.where(head_mask(values.shape, h), values, 0.0), axis=1, keepdims=True)
            for h in range(HEADS)
        ],
        axis=0,
    )


def write_step(keys, values, memory, packed, query_out, key_out, value_out, stats):
    slots = memory.shape[0]
    total = keys.shape[0] * keys.shape[1]
    rows = memory[...]
    w_write = take(packed, WRITE)
    query = dot(rows, w_write[: w_write.shape[0] // 2]).astype(BF16)
    query_out[...] = query
    key_out[...] = dot(rows, w_write[w_write.shape[0] // 2 :]).astype(BF16)
    value_out[...] = dot(rows, take(packed, VALUE)).astype(BF16)
    stacked = stacked_heads(query.astype(F32)).astype(BF16)
    scores = dot(stacked, keys[...].reshape(total, -1), NT)
    top = jnp.max(scores, axis=1, keepdims=True)
    share = jnp.exp2((scores - top) * EXP)
    stats[0] = joined_heads(top, slots)
    stats[1] = joined_heads(jnp.sum(share, axis=1, keepdims=True), slots)
    stats[2] = joined_heads(dot(share.astype(BF16), values[...].reshape(total, -1)), slots)


def write_back_step(
    info, own, other, query, key, value, memory, cot_mine, cot_recv, cot_other, keys, values,
    new_out, d_keys, d_values, d_query, d_key, d_value, cot_out,
):
    core, chip = info[0], info[1]
    slots, width = memory.shape
    part = slots // 4
    rows = keys.shape[1]
    total = keys.shape[0] * rows
    sources = (cot_mine[rows:, :], cot_recv[rows:, :], cot_other[:part, :], cot_other[part:, :])
    cot = jnp.concatenate([choose(k, core, chip, *sources) for k in range(4)], axis=0).astype(F32)
    q = query[...].astype(F32)
    sk = key[...].astype(F32)
    sv = value[...].astype(F32)
    self_column = head_sums(q * sk)
    self_scores = joined_heads(self_column, slots)
    top = jnp.maximum(jnp.maximum(own[0], other[0]), self_scores)
    own_share = jnp.exp2((own[0] - top) * EXP)
    other_share = jnp.exp2((other[0] - top) * EXP)
    self_share = jnp.exp2((self_scores - top) * EXP)
    count = own[1] * own_share + other[1] * other_share + self_share
    written = (
        own[2] * own_share + other[2] * other_share + self_share.astype(BF16).astype(F32) * sv
    ) / count
    new_out[...] = (memory[...].astype(F32) + written).astype(BF16)
    log = top + jnp.log2(count) * (1.0 / EXP)
    log_column = column_of_heads(log)
    delta_column = head_sums(cot * written)
    delta = joined_heads(delta_column, slots)
    stacked = stacked_heads(q).astype(BF16)
    stacked_cot = stacked_heads(cot).astype(BF16)
    flat_keys = keys[...].reshape(total, width)
    share = jnp.exp2((dot(stacked, flat_keys, NT) - log_column) * EXP)
    d_share = dot(stacked_cot, values[...].reshape(total, width), NT)
    d_scores = (share * (d_share - delta_column)).astype(BF16)
    d_values[...] = dot(share.astype(BF16), stacked_cot, TN).astype(BF16).reshape(d_values.shape)
    d_keys[...] = (dot(d_scores, stacked, TN) * SCALE).astype(BF16).reshape(d_keys.shape)
    d_query_part = joined_heads(dot(d_scores, flat_keys), slots) * SCALE
    mine = (lax.broadcasted_iota(jnp.int32, (slots, width), 0) // part) % 2 == core
    self_probs = jnp.exp2((self_scores - log) * EXP)
    self_dp = joined_heads(head_sums(cot * sv), slots)
    self_ds = (self_probs * (self_dp - delta)).astype(BF16).astype(F32) * SCALE
    self_ds = jnp.where(mine, self_ds, 0.0)
    d_query[...] = (d_query_part + self_ds * sk).astype(BF16)
    d_key[...] = (self_ds * q).astype(BF16)
    d_value[...] = jnp.where(mine, self_probs.astype(BF16).astype(F32) * cot, 0.0).astype(BF16)
    cot_out[...] = jnp.where(mine, cot, 0.0)


def merged_heads(heads, place):
    tiles = [ref[k, place, :] for ref in heads for k in range(ref.shape[0])]
    lane = lax.broadcasted_iota(jnp.int32, tiles[0].shape, 1)
    return side_by_side(
        [jnp.where(lane < HEAD_DIM, tiles[2 * p], tiles[2 * p + 1]) for p in range(len(tiles) // 2)]
    )


def inputs_back_step(
    info, dq_parts, dk_parts, dv_parts, packed, normed, scales, gain, d_middle,
    mine_out, away_out, g_gain, merged,
):
    core = info[0]
    rows = mine_out.shape[1]
    weights = [qkv_weight(packed, k) for k in range(3)]
    gain = gain[0:1, :].astype(F32)
    gain_sum = None
    for rank in range(4):
        place = pl.ds(rank * rows, rows)
        total = None
        for k, parts in enumerate((dq_parts, dk_parts, dv_parts)):
            grads = merged_heads(parts, place)
            merged[k, place, :] = grads
            term = dot(grads, weights[k], NT)
            total = term if total is None else total + term
        unit = normed[place, :].astype(F32) * (1.0 / gain)
        part = jnp.sum(total * unit, axis=0, keepdims=True)
        gain_sum = part if gain_sum is None else gain_sum + part
        back = norm_back(unit, scales[place, 0:1], total, gain)

        @pl.when(core == rank % 2)
        def _():
            mine_out[rank // 2] = d_middle[rank // 2] + back

        @pl.when(core != rank % 2)
        def _():
            away_out[rank // 2] = back.astype(BF16)

    g_gain[...] = gain_sum


def weights_back_step(
    info, normed, merged, packed, memory, init, d_memory, dks_parts, dvs_parts,
    g_out, d_init, d_mine, d_away,
):
    source = jnp.concatenate([memory[...], init[...]], axis=0)
    everything = slice(0, source.shape[0])
    dks = merged_heads(dks_parts, everything)
    dvs = merged_heads(dvs_parts, everything)
    d_slots = dot(dks, qkv_weight(packed, 1), NT) + dot(dvs, qkv_weight(packed, 2), NT)
    slots = memory.shape[0]
    part = slots // 4
    d_init[...] = d_slots[slots:]
    total = d_memory[...] + d_slots[:slots]
    for k in range(2):
        even = total[2 * k * part : (2 * k + 1) * part]
        odd = total[(2 * k + 1) * part : (2 * k + 2) * part]
        d_mine[k * part : (k + 1) * part, :] = jnp.where(info[0] == 0, even, odd)
        d_away[k * part : (k + 1) * part, :] = jnp.where(info[0] == 0, odd, even)
    rows = normed[...]
    g_out[0] = dot(rows, merged[0], TN).astype(BF16)
    g_out[1] = (dot(rows, merged[1], TN) + dot(source, dks, TN)).astype(BF16)
    g_out[2] = (dot(rows, merged[2], TN) + dot(source, dvs, TN)).astype(BF16)


def last_heads_kernel(first, need, give, info, *refs):
    heads, refs = refs[:8], refs[8:]
    packed, refs = refs[0], refs[1:]
    earlier, refs = (refs[:5], refs[5:10]), refs[10:]
    normed, scales, gain, d_middle, memory, init, d_memory, refs = *refs[:7], refs[7:]
    d_mine, d_away, g_out, d_init, m_mine, m_away, g_gain, refs = *refs[:7], refs[7:]
    results, merged, scratch = refs[:5], refs[5], refs[6:]
    for k in (5, 6, 7):
        need(k)
    for k in range(5):
        for j in range(heads[k].shape[0]):
            need(k, j, j)
    attend_back_kernel(256, 1024, first, info, *heads, *results, *scratch)

    @pl.when(pl.program_id(0) == pl.num_programs(0) - 1)
    def _():
        for k in range(8, 26):
            need(k, 0, pl.num_programs(0) - 1)
        parts = [(earlier[0][k], earlier[1][k], results[k]) for k in range(5)]
        inputs_back_step(
            info, *parts[:3], packed, normed, scales, gain, d_middle, d_mine, d_away, g_gain, merged
        )
        for k in (0, 1, 6):
            give(k)
        weights_back_step(
            info, normed, merged, packed, memory, init, d_memory, *parts[3:], g_out, d_init,
            m_mine, m_away,
        )
        for k in range(2, 6):
            give(k)


def last_heads(info, first, heads, q, k, v, ks, vs, own, other, o, packed, grads_a, grads_b,
               normed, scales, gains, d_middle, memory, init, d_memory):
    length, width = normed.shape
    slots = memory.shape[0]
    arrays = [of_heads(array, first, heads) for array in (q, k, v, ks, vs)]
    part = (d_middle.shape, F32)
    away = (d_middle.shape, BF16)
    half = ((slots // 2, width), F32)
    out = pltpu.VMEM((heads, length, LANES), BF16)
    slot_out = pltpu.VMEM((heads, ks.shape[1], LANES), BF16)
    return streamed(
        functools.partial(last_heads_kernel, first), "last_heads", info,
        (*arrays, own, other, o, packed, *grads_a, *grads_b, normed, scales, gains, d_middle,
         memory, init, d_memory),
        (part, away, ((3, width, CORE_WIDTH), BF16), ((slots, width), F32), half, half,
         ((1, width), F32)),
        [out, out, out, slot_out, slot_out, pltpu.VMEM((3, length, CORE_WIDTH), BF16),
         pltpu.VMEM((length, LANES), BF16), pltpu.VMEM((LANES, length), F32)],
        grid=(heads,),
    )


def inputs_back_kernel(
    need, give, info, mine, other, mem_mine, mem_other, new_rows, d_out, away_out, mem_out
):
    core, chip = info[0], info[1]
    count, rows, _ = mine.shape
    for k in range(count):
        need(0, k)
        need(1, k)
        back = (mine[k] + other[k].astype(F32)).astype(BF16)
        d_out[k] = back
        give(0, k)

        @pl.when(chip != k)
        def _():
            away_out[:rows, :] = back

    for j in range(2, 5):
        need(j)
    part = mem_mine.shape[0] // 2
    grads = (mem_mine[...] + mem_other[...]).astype(BF16)
    news = [
        jnp.where(
            core == 0,
            new_rows[2 * k * part : (2 * k + 1) * part, :],
            new_rows[(2 * k + 1) * part : (2 * k + 2) * part, :],
        )
        for k in range(2)
    ]
    first, second = grads[:part], grads[part:]
    mem_out[:part, :] = jnp.where(chip == 0, first, second)
    mem_out[part:, :] = jnp.where(chip == 0, news[0], news[1])
    away_out[rows : rows + part, :] = jnp.where(chip == 0, second, first)
    away_out[rows + part :, :] = jnp.where(chip == 0, news[1], news[0])
    for k in (1, 2):
        give(k)


def inputs_back(info, mine, other, mem_mine, mem_other, new_rows):
    _, rows, width = mine.shape
    slots = new_rows.shape[0]
    halves = [(array, array.shape, [((j,), (j,)) for j in range(2)]) for array in (mine, other)]
    return streamed(
        inputs_back_kernel, "inputs_back", info, (*halves, mem_mine, mem_other, new_rows),
        ((mine.shape, BF16), ((rows + slots // 2, width), BF16), ((slots // 2, width), BF16)),
    )


def swap(value, over_batch, over_seq):
    batch, seq = lax.axis_size("batch"), lax.axis_size("seq")
    pairs = [
        (i * seq + j, (i ^ over_batch) * seq + (j ^ over_seq))
        for i in range(batch)
        for j in range(seq)
    ]
    return lax.ppermute(value, ("batch", "seq"), pairs)


def chip_groups():
    batch = lax.axis_index("batch")
    chip = lax.axis_index("seq") // 2
    stages = [(4, 2 * (batch & 1) + chip, lambda k: (k >> 1, 2 * (k & 1)))]
    bits = lax.axis_size("batch").bit_length() - 1
    at = 1
    while at < bits:
        count = min(2, bits - at)
        stages.append(
            (1 << count, (batch >> at) & ((1 << count) - 1), lambda k, at=at: (k << at, 0))
        )
        at += count
    return stages


def in_order(pieces, own):
    bit = 1
    while bit < len(pieces):
        turned = (own & bit) > 0
        pieces = [jnp.where(turned, pieces[k ^ bit], pieces[k]) for k in range(len(pieces))]
        bit *= 2
    return jnp.stack(pieces)


def gather_chips(piece):
    stages = chip_groups()
    shape = piece.shape
    for size, own, peer in reversed(stages):
        piece = in_order([piece] + [swap(piece, *peer(k)) for k in range(1, size)], own)
    count = len(stages)
    piece = piece.transpose(*reversed(range(count)), *range(count, piece.ndim))
    return piece.reshape(-1, *shape)


def spread(pieces, stage):
    size, own, _ = stage
    pieces = pieces.reshape(-1, size, *pieces.shape[-2:])
    return [lax.dynamic_index_in_dim(pieces, own ^ j, 1, keepdims=False) for j in range(size)]


def sent(parts, stage):
    size, _, peer = stage
    return [parts[0]] + [swap(parts[j], *peer(j)) for j in range(1, size)]


def added(parts, kind):
    total = parts[0].astype(F32)
    for part in parts[1:]:
        total = total + part.astype(F32)
    return total.astype(kind)


def split_half(pieces, index):
    return tuple(lax.dynamic_index_in_dim(pieces, k, -3, keepdims=False) for k in (index, 1 - index))


def split_square(pieces, chip):
    half = pieces.shape[1] // 2
    pieces = pieces.reshape(-1, 2, 2, *pieces.shape[1:])
    over_x = split_half(pieces[:, :, :, :half], chip)
    turned = pieces[:, :, :, half:].swapaxes(1, 2)
    return over_x, split_half(turned, lax.axis_index("batch") & 1)


def after(values, *others):
    return lax.optimization_barrier((values, others))[0]


def by_core(core, mine, other, axis=0):
    return jnp.where(
        core == 0,
        jnp.concatenate([mine, other], axis=axis),
        jnp.concatenate([other, mine], axis=axis),
    )


def by_chip(chip, mine, other):
    return jnp.where(chip == 0, jnp.stack([mine, other]), jnp.stack([other, mine]))


def pick(array, index, axis=0):
    return lax.dynamic_index_in_dim(array, index, axis, keepdims=False)


def to_owners(fields, devices):
    many = devices // OWNERS
    out = []
    for k, field in enumerate(fields):
        if many > 1:
            groups = CHUNKS if k == UP else 1
            field = field.reshape(OWNERS, many, groups, -1, field.shape[-1])
            field = field.transpose(0, 2, 1, 3, 4).reshape(OWNERS, -1, field.shape[-1])
        out.append(field)
    return jnp.concatenate(out, axis=1)


def from_owners(packed, devices):
    many = devices // OWNERS
    out = []
    for k in range(len(FIELDS)):
        field = packed[:, CUTS[k] : CUTS[k + 1]]
        groups = CHUNKS if k == UP else 1
        field = field.reshape(OWNERS, groups, many, -1, field.shape[-1])
        out.append(field.transpose(0, 2, 1, 3, 4).reshape(devices, -1, field.shape[-1]))
    return jnp.concatenate(out, axis=1)


def per_device(
    tokens, memory, lengths, resets, attn_in, attn_out, ffn_in, ffn_out, writer_in, writer_value,
    norm_gains, memory_init, out_cotangent, memory_cotangent,
):
    _, rows, width = tokens.shape
    devices = lax.axis_size("batch") * lax.axis_size("seq")
    rank = lax.axis_index("seq")
    chip, core = rank // 2, rank % 2
    slot_part = memory.shape[1]
    slots = 4 * slot_part
    stages = chip_groups()

    ends = jnp.cumsum(pick(lengths, chip))
    info = jnp.concatenate([jnp.stack([core, chip]), ends, pick(resets, chip)]).astype(jnp.int32)

    def to_chip(big, small):
        mine = jnp.concatenate([pick(big, chip), pick(small, chip)], axis=0)
        away = jnp.concatenate([pick(big, 1 - chip), pick(small, 1 - chip)], axis=0)
        return mine, swap(away, 0, 2)

    misc = jnp.concatenate([memory_init, norm_gains])
    misc_rows = -(-misc.shape[0] // CORE_WIDTH)
    misc = jnp.pad(misc, (0, misc_rows * CORE_WIDTH - misc.shape[0])).reshape(misc_rows, CORE_WIDTH)
    attn_rows = attn_in.reshape(-1, 2, CORE_WIDTH)
    own_rows = attn_rows.shape[0]
    mine = jnp.concatenate([pick(attn_rows, core, 1), misc], axis=0)
    theirs = swap(jnp.concatenate([pick(attn_rows, 1 - core, 1), misc], axis=0), 0, 1)
    piece = jnp.concatenate(
        [
            by_core(core, mine[:own_rows], theirs[:own_rows]),
            by_core(core, mine[own_rows:], theirs[own_rows:]),
        ],
        axis=0,
    )
    gathered = gather_chips(piece)
    misc = gathered[:, 2 * own_rows :].reshape(devices, -1)
    init = misc[:, : memory_init.shape[0]].reshape(slots, width)
    gains = misc[:, memory_init.shape[0] :][:, : norm_gains.shape[0]].reshape(2, width)
    w_qkv = gathered
    if devices != OWNERS:
        w_qkv = gathered[:, : 2 * own_rows].reshape(OWNERS // 2, -1, CORE_WIDTH)

    columns = ffn_in.reshape(-1, CHUNKS, width).transpose(1, 0, 2).reshape(-1, width)
    parts = [
        attn_out.reshape(-1, width), writer_value.reshape(-1, width),
        writer_in.reshape(-1, width), columns, ffn_out.reshape(-1, width),
    ]
    sizes = [part.shape[0] for part in parts]
    cuts = [sum(sizes[:k]) for k in range(len(sizes) + 1)]
    packed = lax.all_gather(jnp.concatenate(parts, axis=0), ("batch", "seq"), axis=0)
    if devices != OWNERS:
        packed = to_owners([packed[:, cuts[k] : cuts[k + 1]] for k in range(len(sizes))], devices)

    own, recv = to_chip(tokens, memory)
    sources = (own, recv, swap(own, 0, 1), swap(recv, 0, 1))
    q_log, k, v, ks, vs, normed, own_tokens, mem_rows, o, o_away, scales = read(
        info, sources, w_qkv, init, gains, rows
    )
    out_cotangent, memory_cotangent = after((out_cotangent, memory_cotangent), recv)
    cots = to_chip(out_cotangent, memory_cotangent)
    cot_other = swap(jnp.concatenate([cot[rows:] for cot in after(cots, o)], axis=0), 0, 1)
    o_other = swap(o_away, 0, 1)
    middle, normed_two, act, slope, result, keys, values, result_away, *writer, stats = forward(
        info, own_tokens, o, o_other, packed, gains, mem_rows
    )
    came = swap(result_away, 0, 2)
    stats_other = swap(stats, 0, 1)
    kept, away, d_middle, d_own, d_away, g_gain_two, d_memory, new_rows = backward(
        info, stats, stats_other, writer, mem_rows, cots, cot_other, keys, values, packed, result,
        normed_two, act, slope, middle, o, o_other, gains,
    )
    d_other, came = after((swap(d_away, 0, 1), came), came)
    if devices != OWNERS:
        both = by_core(core, kept[:, None], away[:, None], axis=1).reshape(OWNERS, PACKED, width)
        both = from_owners(both, devices).reshape(devices // 2, 2, -1, width)
        kept, away = pick(both, core, 1), pick(both, 1 - core, 1)
    arrived = swap(after(away, d_other), 0, 1)

    heads = (q_log, k, v, ks, vs)
    grads_a = attend_back(info, 0, 1, *heads, d_own, d_other, o)
    kept, arrived = (split_square(array, chip) for array in after((kept, arrived), grads_a))
    square = [(added((a, b), BF16), added((c, d), BF16)) for (a, c), (b, d) in zip(kept, arrived)]
    d_own_b = after(d_own, square)
    moved = [swap(away, *peer) for (_, away), peer in zip(square, ((0, 2), (1, 0)))]
    grads_b = attend_back(info, 1, 2, *heads, d_own_b, d_other, o)
    moved = after(moved, grads_b)
    square = [split_half(added((own, new), BF16), index) for (own, _), new, index in zip(
        square, moved, (lax.axis_index("batch") & 1, chip))]
    moved = [swap(away, *peer) for (_, away), peer in zip(square, ((1, 0), (0, 2)))]
    grads_b = after(grads_b, [away for _, away in square])
    d_mine, d_away, g_qkv, d_init, mem_mine, mem_away, g_gain_one = last_heads(
        info, 3, 1, *heads, d_own, d_other, o, w_qkv, grads_a, grads_b, normed, scales, gains,
        d_middle, mem_rows, init, d_memory,
    )
    moved = after(moved, g_qkv)
    d_sent = swap(after(d_away, moved), 0, 1)
    m_sent = swap(after(mem_away, moved), 0, 1)

    g_misc = jnp.concatenate(
        [
            d_init.reshape(devices, -1),
            jnp.concatenate([g_gain_one, g_gain_two]).reshape(devices, -1),
        ],
        axis=1,
    )
    g_misc = jnp.pad(g_misc, ((0, 0), (0, misc_rows * CORE_WIDTH - g_misc.shape[1])))
    small = jnp.concatenate(
        [
            g_qkv.reshape(devices // 2, 2 * own_rows, CORE_WIDTH),
            g_misc.reshape(devices // 2, 2 * misc_rows, CORE_WIDTH).astype(BF16),
        ],
        axis=1,
    )
    small_parts = sent(spread(after(small, moved), stages[0]), stages[0])
    parts = [jnp.concatenate([added((own, new), BF16) for (own, _), new in zip(square, moved)], axis=1)]
    for stage in stages[1:]:
        parts = sent(spread(added(parts, BF16), stage), stage)
    d_sent = after(d_sent, parts[0])
    d_tokens, d_tokens_away, mem_out = inputs_back(info, d_mine, d_sent, mem_mine, m_sent, new_rows)
    home = swap(after(d_tokens_away, small_parts), 0, 2)
    parts, small_parts = after(parts, d_tokens), after(small_parts, d_tokens)
    for stage in stages[1:]:
        small_parts = sent(spread(added(small_parts, BF16), stage), stage)
    small_parts = after(small_parts, home)
    summed = added(parts, F32).reshape(-1, width)
    small = added(small_parts, F32).reshape(-1, CORE_WIDTH)
    big = [summed[cuts[k] : cuts[k + 1]] for k in range(len(sizes))]
    big[UP] = big[UP].reshape(CHUNKS, -1, width).transpose(1, 0, 2)
    small_attn = small[: 2 * own_rows].reshape(2, own_rows, CORE_WIDTH)
    small_misc = small[2 * own_rows :].reshape(2, misc_rows, CORE_WIDTH)
    back = swap(
        jnp.concatenate([pick(small_attn, 1 - core), pick(small_misc, 1 - core)], axis=0), 0, 1
    )
    attn_grad = by_core(core, pick(small_attn, core), back[:own_rows], axis=1)
    misc_grad = (pick(small_misc, core) + back[own_rows:]).reshape(-1)

    def at_home(both, new):
        return lax.dynamic_update_index_in_dim(both, new, 1 - chip, 0)

    mem_came = home[rows:]
    return (
        at_home(result, came),
        by_chip(chip, mem_out[slot_part:], mem_came[slot_part:]),
        at_home(d_tokens, home[:rows]),
        by_chip(chip, mem_out[:slot_part], mem_came[:slot_part]),
        attn_grad.reshape(-1),
        *[big[k].reshape(-1) for k in (OUT, UP, DOWN, WRITE, VALUE)],
        misc_grad[memory_init.shape[0] :][: norm_gains.shape[0]],
        misc_grad[: memory_init.shape[0]],
    )


def solution(mesh):
    rows = P("batch", "seq", None)
    table = P("batch", None)
    flat = P(("batch", "seq"))
    return jax.shard_map(
        per_device,
        mesh=mesh,
        in_specs=(rows, rows, table, table, *[flat] * 8, rows, rows),
        out_specs=(rows, rows, rows, rows, *[flat] * 8),
        check_vma=False,
    )
```

time: 342 us -> 251 us (0.73)
  waiting for transfers between devices: 102 us -> 42.4 us
  local copies, waits for them, and re-layouts: 46.4 us -> 22.8 us
  other arithmetic: 12 us -> 7.64 us
  Pallas kernels: 132 us -> 128 us
    ppermute x31 -> x34, waiting for transfers between devices: 102 us -> 33.8 us  [swap(): return lax.ppermute(value, ('batch', 'seq'), pairs)]
    unnamed x85 -> x69, local copies, waits for them, and re-layouts: 17.3 us -> 6.81 us
    slice x10 -> x4, local copies, waits for them, and re-layouts: 12.8 us -> 4.19 us  [the longest x2 4.19 us: split_square(): turned = pieces[:, :, :, half:].swapaxes(1, 2)]
    all_gather x1, waiting for transfers between devices: 0.02 us -> 8.52 us  [per_device(): lax.all_gather(jnp.concatenate(parts, axis=0), ('batch', 'seq'), axis=0)]
    squeeze x14 -> x7, local copies, waits for them, and re-layouts: 5.03 us -> 0.2 us  [pick(): return lax.dynamic_index_in_dim(array, index, axis, keepdims=False)]
    convert_element_type x4 -> x9, other arithmetic: 5.23 us -> 1.74 us  [added(): return total.astype(kind)]
    pallas_call x9 -> x7, Pallas kernels: 132 us -> 128 us  [streamed(): pl.pallas_call(body, grid_spec=pltpu.PrefetchScalarGridSpec(num_scalar_pr...]
    ppermute x31 -> x34, starting transfers between devices: 30.2 us -> 30.2 us  [swap(): return lax.ppermute(value, ('batch', 'seq'), pairs)]
  transfers between devices with their start and end apart: 32 -> 35, of which waited for: 14 -> 14; matrix products, arithmetic and copies ran while one was open for 12% -> 6% of each run, Pallas kernels for 30% -> 52%
where the time goes in v2:
time: 251 us; the launch traced here: 247 us
  Pallas kernels  128 us (51%)
  waiting for transfers between devices  42.4 us (17%)
  starting transfers between devices  30.2 us (12%)
  local copies, waits for them, and re-layouts  22.8 us (9%)
  between operations  15.3 us (6%)
  other arithmetic  7.64 us (3%)
    pallas_call x7, Pallas kernels, streamed(): pl.pallas_call(body, grid_spec=pltpu.PrefetchScalarGridSpec(num_scalar_pr...  128 us
    ppermute x34, waiting for transfers between devices, swap(): return lax.ppermute(value, ('batch', 'seq'), pairs)  33.8 us
    ppermute x34, starting transfers between devices, swap(): return lax.ppermute(value, ('batch', 'seq'), pairs)  30.2 us
    all_gather x1, waiting for transfers between devices, per_device(): lax.all_gather(jnp.concatenate(parts, axis=0), ('batch', 'seq'), axis=0)  8.52 us
    unnamed x69, local copies, waits for them, and re-layouts  6.81 us
  transfers between devices with their start and end apart: 35, of which 14 were waited for; matrix products, arithmetic and copies ran while one was open for 6% of the time, Pallas kernels for 52%

profile of v2, /device:TPU:8, one launch (start us, length us, event | category | flops | bytes accessed | tf_op | source)
XLA Modules:
  0.0 246.8 jit_solution(10060603787002761509)
XLA Ops:
  14.2 1.6 collective-permute-start.7
  16.1 1.6 collective-permute-start.1
  19.0 1.2 collective-permute-start.3
  20.4 1.8 collective-permute-done.1
  23.0 3.3 %collective-permute-done.3 = bf16[106,256]{1,0:T(8,128)(2,1)S(1)} collective-permute-done((bf16[106,256]{1,0:T(8,128)(2,1)S(1)}, bf16[106,256]{1,0:T(8,128)(2,1)S(1)}, u32[]{:S(2)}, u32[]{:S(2)}) %collective-permute-start.3) | collective-permute-done | bytes 54304 | tf_op jit(solution)/shard_map/ppermute | solution.py:946
  26.6 1.5 collective-permute-start.5
  28.1 1.9 collective-permute-start.6
  30.9 5.8 %collective-permute-done.4 = bf16[4,106,256]{2,1,0:T(8,128)(2,1)S(1)} collective-permute-done((bf16[4,106,256]{2,1,0:T(8,128)(2,1)S(1)}, bf16[4,106,256]{2,1,0:T(8,128)(2,1)S(1)}, u32[]{:S(2)}, u32[]{:S(2)}) %collective-permute-start.4) | collective-permute-done | bytes 217120 | tf_op jit(solution)/shard_map/ppermute | solution.py:946
  36.7 1.6 collective-permute-done.5
  38.3 1.9 collective-permute-done.6
  42.2 31.1 %read.1 = (bf16[4,2048,128]{2,1,0:T(8,128)(2,1)}, bf16[4,2048,128]{2,1,0:T(8,128)(2,1)}, bf16[4,2048,128]{2,1,0:T(8,128)(2,1)}, bf16[4,128,128]{2,1,0:T(8,128)(2...) custom-call(s32[14]{0:T(128)} %pad_add_fusion.info, ...), custom_call_target="tpu_custom_call" | custom-call | tf_op jit(solution)/shard_map/read/pallas_call | solution.py:82
  73.5 1.5 collective-permute-start.12
  75.7 8.5 %all-gather.3.cloned.1.call-done = bf16[6144,512]{1,0:T(8,128)(2,1)} async-done(((bf16[192,512]{1,0:T(8,128)(2,1)}), bf16[6144,512]{1,0:T(8,128)(2,1)}) %all-gather.3.cloned.1.call-update) | async-done | bytes 6291472 | tf_op jit(solution)/shard_map/all_gather | solution.py:1105
  84.2 18.3 %feed_forward.1 = (f32[2,512,512]{2,1,0:T(8,128)}, bf16[2,512,512]{2,1,0:T(8,128)(2,1)}, bf16[4,2,512,512]{3,2,1,0:T(8,128)(2,1)}, bf16[4,2,512,512]{3,2,1,0:T(8...) custom-call(s32[14]{0:T(128)} %pad_add_fusion.info, ...), custom_call_target="tpu_custom_call" | custom-call | tf_op jit(solution)/shard_map/feed_forward/pallas_call | solution.py:82
  103.3 1.4 collective-permute-start.15
  105.5 25.3 %feed_forward_back.1 = (bf16[16,192,512]{2,1,0:T(8,128)(2,1)}, bf16[16,192,512]{2,1,0:T(8,128)(2,1)}, f32[2,512,512]{2,1,0:T(8,128)}, bf16[2,2,512,128]{3,2,1,0:...) custom-call(s32[14]{0:T(128)} %pad_add_fusion.info, ...), custom_call_target="tpu_custom_call" | custom-call | tf_op jit(solution)/shard_map/feed_forward_back/pallas_call | solution.py:82
  130.9 2.0 collective-permute-done.14.refs_6_
  133.8 11.5 %attend_back.2 = (bf16[1,2048,128]{2,1,0:T(8,128)(2,1)}, bf16[1,2048,128]{2,1,0:T(8,128)(2,1)}, bf16[1,2048,128]{2,1,0:T(8,128)(2,1)}, bf16[1,128,128]{2,1,0:T(8,128)(2,1)}, bf16[1,128,128]{2,1,0:T(8,128)(2,1)}) custom-call(s32[14]{0:T(128)} %pad_add_fusion.info, bf16[4,2048,128]{2,1,0:T(8,128)(2,1)} %get-tuple-element.121.refs_0_, ...), custom_call_target="tpu_custom_call" | custom-call | tf_op jit(solution)/shard_map/attend_back/pallas_call | solution.py:82
  145.3 2.1 fusion.23
  147.4 2.1 fusion.24
  149.9 1.4 collective-permute-start.18
  153.1 20.2 %attend_back.3 = (bf16[2,2048,128]{2,1,0:T(8,128)(2,1)}, bf16[2,2048,128]{2,1,0:T(8,128)(2,1)}, bf16[2,2048,128]{2,1,0:T(8,128)(2,1)}, bf16[2,128,128]{2,1,0:T(8,128)(2,1)}, bf16[2,128,128]{2,1,0:T(8,128)(2,1)}) custom-call(s32[14]{0:T(128)} %pad_add_fusion.info, bf16[4,2048,128]{2,1,0:T(8,128)(2,1)} %get-tuple-element.121.refs_0_, ...), custom_call_target="tpu_custom_call" | custom-call | tf_op jit(solution)/shard_map/attend_back/pallas_call | solution.py:82
  178.4 18.4 %last_heads.1 = (f32[2,512,512]{2,1,0:T(8,128)}, bf16[2,512,512]{2,1,0:T(8,128)(2,1)}, bf16[3,512,256]{2,1,0:T(8,128)(2,1)}, f32[64,512]{1,0:T(8,128)}, f32[32,5...) custom-call(s32[14]{0:T(128)} %pad_add_fusion.info, bf16[4,2048,128]{2,1,0:T(8,128)(2,1)} %get-tuple-element.121.refs_0_, ...), custom_call_target="tpu_custom_call" | custom-call | tf_op jit(solution)/shard_map/last_heads/pallas_call | solution.py:82
  201.2 1.8 collective-permute-start.32
  204.5 1.3 collective-permute-start.23
  206.9 3.7 %inputs_back.1 = (bf16[2,512,512]{2,1,0:T(8,128)(2,1)}, bf16[544,512]{1,0:T(8,128)(2,1)}, bf16[32,512]{1,0:T(8,128)(2,1)}) custom-call(s32[14]{0:T(128)} %pad_add_fusion.info, f32[2,512,512]{2,1,0:T(8,128)} %get-tuple-element.155.refs_0_, bf16[2,512,512]{2,1,0:T(8,128)(2,1)} %copy-done.9, f32[32,512]{1,0:T(8,128)} %get-tuple-element.162.refs_2_, ...), custom_call_target="tpu_custom_call" | custom-call | tf_op jit(solution)/shard_map/inputs_back/pallas_call | solution.py:82
  210.6 1.4 collective-permute-start.25
  212.1 4.7 %collective-permute-done.32 = bf16[1,192,512]{2,1,0:T(8,128)(2,1)S(1)} collective-permute-done((bf16[1,192,512]{2,1,0:T(8,128)(2,1)S(1)}, bf16[1,192,512]{2,1,0:T(8,128)(2,1)S(1)}, u32[]{:S(2)}, u32[]{:S(2)}) %collective-permute-start.32) | collective-permute-done | bytes 196640 | tf_op jit(solution)/shard_map/ppermute | solution.py:946
  216.8 5.1 %collective-permute-done.33 = bf16[1,192,512]{2,1,0:T(8,128)(2,1)S(1)} collective-permute-done((bf16[1,192,512]{2,1,0:T(8,128)(2,1)S(1)}, bf16[1,192,512]{2,1,0:T(8,128)(2,1)S(1)}, u32[]{:S(2)}, u32[]{:S(2)}) %collective-permute-start.33) | collective-permute-done | bytes 196640 | tf_op jit(solution)/shard_map/ppermute | solution.py:946
  222.0 1.3 collective-permute-start.26
  223.6 2.3 collective-permute-start.28
  231.2 5.1 %collective-permute-done.26 = bf16[544,512]{1,0:T(8,128)(2,1)S(1)} collective-permute-done((bf16[544,512]{1,0:T(8,128)(2,1)}, bf16[544,512]{1,0:T(8,128)(2,1)S(1)}, u32[]{:S(2)}, u32[]{:S(2)}) %collective-permute-start.26) | collective-permute-done | bytes 557088 | tf_op jit(solution)/shard_map/ppermute | solution.py:946
  (205 shorter events, 38.6 us)
Async XLA Ops:
  7.2 77.0 %all-gather.3.cloned.1.call-start = ((), (), s32[]{:S(2)}) async-start(), calls=%async_computation | async-start | bytes 6488064 | tf_op jit(solution)/shard_map/all_gather | solution.py:1105
  13.9 2.1 collective-permute-start
  14.2 16.6 %collective-permute-start.7 = (bf16[528,512]{1,0:T(8,128)(2,1)S(1)}, bf16[528,512]{1,0:T(8,128)(2,1)}, u32[]{:S(2)}, u32[]{:S(2)}) collective-permute-start(bf16[528,512]{1,0:T(8,128)(2,1)S(1)} %pad_maximum_fusion.2), channel_id=1, source_target_pairs={{0,2},{1,3},{2,0},{3,1},{4,6},{5,7},{6,4},{7,5},{8,10},{9,11},{10,... | collective-permute-start | bytes 1622024 | tf_op jit(solution)/shard_map/ppermute | solution.py:946
  15.8 26.3 %collective-permute-start.8 = (bf16[528,512]{1,0:T(8,128)(2,1)S(1)}, bf16[528,512]{1,0:T(8,128)(2,1)}, u32[]{:S(2)}, u32[]{:S(2)}) collective-permute-start(bf16[528,512]{1,0:T(8,128)(2,1)S(1)} %pad_maximum_fusion.1.refs_3_), channel_id=1, source_target_pairs={{0,1},{1,0},{2,3},{3,2},{4,5},{5,4},{6,7},{7,6},{8,9},{9,8},{10,11... | collective-permute-start | bytes 1622024 | tf_op jit(solution)/shard_map/ppermute | solution.py:946
  16.1 6.1 %collective-permute-start.1 = (bf16[106,256]{1,0:T(8,128)(2,1)S(1)}, bf16[106,256]{1,0:T(8,128)(2,1)S(1)}, u32[]{:S(2)}, u32[]{:S(2)}) collective-permute-start(bf16[106,256]{1,0:T(8,128)(2,1)S(1)} %pad_maximum_fusion.6), channel_id=1, source_target_pairs={{0,24},{1,25},{2,26},{3,27},{4,28},{5,29},{6,30},{7,31},{8,16},{9,... | collective-permute-start | bytes 162824 | tf_op jit(solution)/shard_map/ppermute | solution.py:946
  17.8 5.2 %collective-permute-start.2 = (bf16[106,256]{1,0:T(8,128)(2,1)S(1)}, bf16[106,256]{1,0:T(8,128)(2,1)S(1)}, u32[]{:S(2)}, u32[]{:S(2)}) collective-permute-start(bf16[106,256]{1,0:T(8,128)(2,1)S(1)} %pad_maximum_fusion.6), channel_id=1, source_target_pairs={{0,16},{1,17},{2,18},{3,19},{4,20},{5,21},{6,22},{7,23},{8,24},{9,... | collective-permute-start | bytes 162824 | tf_op jit(solution)/shard_map/ppermute | solution.py:946
  19.0 7.3 %collective-permute-start.3 = (bf16[106,256]{1,0:T(8,128)(2,1)S(1)}, bf16[106,256]{1,0:T(8,128)(2,1)S(1)}, u32[]{:S(2)}, u32[]{:S(2)}) collective-permute-start(bf16[106,256]{1,0:T(8,128)(2,1)S(1)} %pad_maximum_fusion.6), channel_id=1, source_target_pairs={{0,8},{1,9},{2,10},{3,11},{4,12},{5,13},{6,14},{7,15},{8,0},{9,1},... | collective-permute-start | bytes 162824 | tf_op jit(solution)/shard_map/ppermute | solution.py:946
  26.4 10.3 %collective-permute-start.4 = (bf16[4,106,256]{2,1,0:T(8,128)(2,1)S(1)}, bf16[4,106,256]{2,1,0:T(8,128)(2,1)S(1)}, u32[]{:S(2)}, u32[]{:S(2)}) collective-permute-start(bf16[4,106,256]{2,1,0:T(8,128)(2,1)S(1)} %pad_maximum_fusion.5), channel_id=1, source_target_pairs={{0,6},{1,7},{2,4},{3,5},{4,2},{5,3},{6,0},{7,1},{8,14},{9,15},{10,... | collective-permute-start | bytes 651272 | tf_op jit(solution)/shard_map/ppermute | solution.py:946
  26.6 11.7 %collective-permute-start.5 = (bf16[4,106,256]{2,1,0:T(8,128)(2,1)S(1)}, bf16[4,106,256]{2,1,0:T(8,128)(2,1)S(1)}, u32[]{:S(2)}, u32[]{:S(2)}) collective-permute-start(bf16[4,106,256]{2,1,0:T(8,128)(2,1)S(1)} %pad_maximum_fusion.5), channel_id=1, source_target_pairs={{0,4},{1,5},{2,6},{3,7},{4,0},{5,1},{6,2},{7,3},{8,12},{9,13},{10,... | collective-permute-start | bytes 651272 | tf_op jit(solution)/shard_map/ppermute | solution.py:946
  28.1 12.1 %collective-permute-start.6 = (bf16[4,106,256]{2,1,0:T(8,128)(2,1)S(1)}, bf16[4,106,256]{2,1,0:T(8,128)(2,1)S(1)}, u32[]{:S(2)}, u32[]{:S(2)}) collective-permute-start(bf16[4,106,256]{2,1,0:T(8,128)(2,1)S(1)} %pad_maximum_fusion.5), channel_id=1, source_target_pairs={{0,2},{1,3},{2,0},{3,1},{4,6},{5,7},{6,4},{7,5},{8,10},{9,11},{10,... | collective-permute-start | bytes 651272 | tf_op jit(solution)/shard_map/ppermute | solution.py:946
  30.8 11.3 %collective-permute-start.9 = (bf16[528,512]{1,0:T(8,128)(2,1)}, bf16[528,512]{1,0:T(8,128)(2,1)}, u32[]{:S(2)}, u32[]{:S(2)}) collective-permute-start(bf16[528,512]{1,0:T(8,128)(2,1)} %collective-permute-done.7.refs_4_), channel_id=1, source_target_pairs={{0,1},{1,0},{2,3},{3,2},{4,5},{5,4},{6,7},{7,6},{8,9},{9,8},{10,11... | collective-permute-start | bytes 1622024 | tf_op jit(solution)/shard_map/ppermute | solution.py:946
  73.3 2.4 collective-permute-start.10
  73.5 29.4 %collective-permute-start.12 = (bf16[528,512]{1,0:T(8,128)(2,1)S(1)}, bf16[528,512]{1,0:T(8,128)(2,1)S(1)}, u32[]{:S(2)}, u32[]{:S(2)}) collective-permute-start(bf16[528,512]{1,0:T(8,128)(2,1)S(1)} %pad_maximum_fusion.4), channel_id=1, source_target_pairs={{0,2},{1,3},{2,0},{3,1},{4,6},{5,7},{6,4},{7,5},{8,10},{9,11},{10,... | collective-permute-start | bytes 1622024 | tf_op jit(solution)/shard_map/ppermute | solution.py:946
  102.5 2.2 collective-permute-start.11
  103.3 27.7 %collective-permute-start.15 = (bf16[512,512]{1,0:T(8,128)(2,1)}, bf16[512,512]{1,0:T(8,128)(2,1)}, u32[]{:S(2)}, u32[]{:S(2)}) collective-permute-start(bf16[512,512]{1,0:T(8,128)(2,1)} %get-tuple-element.119), channel_id=1, source_target_pairs={{0,2},{1,3},{2,0},{3,1},{4,6},{5,7},{6,4},{7,5},{8,10},{9,11},{10,... | collective-permute-start | bytes 1572872 | tf_op jit(solution)/shard_map/ppermute | solution.py:946
  130.8 2.2 collective-permute-start.14
  133.0 12.3 %collective-permute-start.16 = (bf16[16,192,512]{2,1,0:T(8,128)(2,1)}, bf16[16,192,512]{2,1,0:T(8,128)(2,1)}, u32[]{:S(2)}, u32[]{:S(2)}) collective-permute-start(bf16[16,192,512]{2,1,0:T(8,128)(2,1)} %get-tuple-element.135), channel_id=1, source_target_pairs={{0,1},{1,0},{2,3},{3,2},{4,5},{5,4},{6,7},{7,6},{8,9},{9,8},{10,11... | collective-permute-start | bytes 9437192 | tf_op jit(solution)/shard_map/ppermute | solution.py:946
  149.9 23.4 %collective-permute-start.18 = (bf16[4,2,96,512]{3,2,0,1:T(8,128)(2,1)S(1)}, bf16[4,2,96,512]{3,2,0,1:T(8,128)(2,1)S(1)}, u32[]{:S(2)}, u32[]{:S(2)}) collective-permute-start(bf16[4,2,96,512]{3,2,0,1:T(8,128)(2,1)S(1)} %fusion.3), channel_id=1, source_target_pairs={{0,4},{1,5},{2,6},{3,7},{4,0},{5,1},{6,2},{7,3},{8,12},{9,13},{10,... | collective-permute-start | bytes 2359304 | tf_op jit(solution)/shard_map/ppermute | solution.py:946
  151.8 21.5 %collective-permute-start.17 = (bf16[4,2,96,512]{3,2,0,1:T(8,128)(2,1)S(1)}, bf16[4,2,96,512]{3,2,0,1:T(8,128)(2,1)S(1)}, u32[]{:S(2)}, u32[]{:S(2)}) collective-permute-start(bf16[4,2,96,512]{3,2,0,1:T(8,128)(2,1)S(1)} %fusion.1), channel_id=1, source_target_pairs={{0,2},{1,3},{2,0},{3,1},{4,6},{5,7},{6,4},{7,5},{8,10},{9,11},{10,... | collective-permute-start | bytes 2359304 | tf_op jit(solution)/shard_map/ppermute | solution.py:946
  175.4 23.2 %collective-permute-start.20 = (bf16[4,96,512]{2,1,0:T(8,128)(2,1)}, bf16[4,96,512]{2,1,0:T(8,128)(2,1)S(1)}, u32[]{:S(2)}, u32[]{:S(2)}) collective-permute-start(bf16[4,96,512]{2,1,0:T(8,128)(2,1)} %dynamic-slice_bitcast_fusion.4), channel_id=1, source_target_pairs={{0,2},{1,3},{2,0},{3,1},{4,6},{5,7},{6,4},{7,5},{8,10},{9,11},{10,... | collective-permute-start | bytes 1179656 | tf_op jit(solution)/shard_map/ppermute | solution.py:946
  176.6 22.0 %collective-permute-start.19 = (bf16[4,96,512]{2,1,0:T(8,128)(2,1)}, bf16[4,96,512]{2,1,0:T(8,128)(2,1)S(1)}, u32[]{:S(2)}, u32[]{:S(2)}) collective-permute-start(bf16[4,96,512]{2,1,0:T(8,128)(2,1)} %dynamic-slice_bitcast_fusion.5), channel_id=1, source_target_pairs={{0,4},{1,5},{2,6},{3,7},{4,0},{5,1},{6,2},{7,3},{8,12},{9,13},{10,... | collective-permute-start | bytes 1179656 | tf_op jit(solution)/shard_map/ppermute | solution.py:946
  198.6 5.8 %collective-permute-start.21 = (bf16[2,512,512]{2,1,0:T(8,128)(2,1)}, bf16[2,512,512]{2,1,0:T(8,128)(2,1)S(1)}, u32[]{:S(2)}, u32[]{:S(2)}) collective-permute-start(bf16[2,512,512]{2,1,0:T(8,128)(2,1)} %get-tuple-element.160), channel_id=1, source_target_pairs={{0,1},{1,0},{2,3},{3,2},{4,5},{5,4},{6,7},{7,6},{8,9},{9,8},{10,11... | collective-permute-start | bytes 3145736 | tf_op jit(solution)/shard_map/ppermute | solution.py:946
  200.6 10.0 %collective-permute-start.31 = (bf16[1,192,512]{2,1,0:T(8,128)(2,1)S(1)}, bf16[1,192,512]{2,1,0:T(8,128)(2,1)S(1)}, u32[]{:S(2)}, u32[]{:S(2)}) collective-permute-start(bf16[1,192,512]{2,1,0:T(8,128)(2,1)S(1)} %get-tuple-element.211), channel_id=1, source_target_pairs={{0,8},{1,9},{2,10},{3,11},{4,12},{5,13},{6,14},{7,15},{8,0},{9,1},... | collective-permute-start | bytes 589832 | tf_op jit(solution)/shard_map/ppermute | solution.py:946
  201.2 15.5 %collective-permute-start.32 = (bf16[1,192,512]{2,1,0:T(8,128)(2,1)S(1)}, bf16[1,192,512]{2,1,0:T(8,128)(2,1)S(1)}, u32[]{:S(2)}, u32[]{:S(2)}) collective-permute-start(bf16[1,192,512]{2,1,0:T(8,128)(2,1)S(1)} %get-tuple-element.212), channel_id=1, source_target_pairs={{0,16},{1,17},{2,18},{3,19},{4,20},{5,21},{6,22},{7,23},{8,24},{9,... | collective-permute-start | bytes 589832 | tf_op jit(solution)/shard_map/ppermute | solution.py:946
  203.0 18.9 %collective-permute-start.33 = (bf16[1,192,512]{2,1,0:T(8,128)(2,1)S(1)}, bf16[1,192,512]{2,1,0:T(8,128)(2,1)S(1)}, u32[]{:S(2)}, u32[]{:S(2)}) collective-permute-start(bf16[1,192,512]{2,1,0:T(8,128)(2,1)S(1)} %get-tuple-element.209), channel_id=1, source_target_pairs={{0,24},{1,25},{2,26},{3,27},{4,28},{5,29},{6,30},{7,31},{8,16},{9,... | collective-permute-start | bytes 589832 | tf_op jit(solution)/shard_map/ppermute | solution.py:946
  204.5 17.6 %collective-permute-start.23 = (bf16[4,106,256]{2,1,0:T(8,128)(2,1)S(1)}, bf16[4,106,256]{2,1,0:T(8,128)(2,1)S(1)}, u32[]{:S(2)}, u32[]{:S(2)}) collective-permute-start(bf16[4,106,256]{2,1,0:T(8,128)(2,1)S(1)} %get-tuple-element.204), channel_id=1, source_target_pairs={{0,2},{1,3},{2,0},{3,1},{4,6},{5,7},{6,4},{7,5},{8,10},{9,11},{10,... | collective-permute-start | bytes 651272 | tf_op jit(solution)/shard_map/ppermute | solution.py:946
  205.8 16.3 %collective-permute-start.24 = (bf16[4,106,256]{2,1,0:T(8,128)(2,1)S(1)}, bf16[4,106,256]{2,1,0:T(8,128)(2,1)S(1)}, u32[]{:S(2)}, u32[]{:S(2)}) collective-permute-start(bf16[4,106,256]{2,1,0:T(8,128)(2,1)S(1)} %get-tuple-element.203), channel_id=1, source_target_pairs={{0,4},{1,5},{2,6},{3,7},{4,0},{5,1},{6,2},{7,3},{8,12},{9,13},{10,... | collective-permute-start | bytes 651272 | tf_op jit(solution)/shard_map/ppermute | solution.py:946
  210.6 11.4 %collective-permute-start.25 = (bf16[4,106,256]{2,1,0:T(8,128)(2,1)S(1)}, bf16[4,106,256]{2,1,0:T(8,128)(2,1)S(1)}, u32[]{:S(2)}, u32[]{:S(2)}) collective-permute-start(bf16[4,106,256]{2,1,0:T(8,128)(2,1)S(1)} %get-tuple-element.202), channel_id=1, source_target_pairs={{0,6},{1,7},{2,4},{3,5},{4,2},{5,3},{6,0},{7,1},{8,14},{9,15},{10,... | collective-permute-start | bytes 651272 | tf_op jit(solution)/shard_map/ppermute | solution.py:946
  222.0 14.2 %collective-permute-start.26 = (bf16[544,512]{1,0:T(8,128)(2,1)}, bf16[544,512]{1,0:T(8,128)(2,1)S(1)}, u32[]{:S(2)}, u32[]{:S(2)}) collective-permute-start(bf16[544,512]{1,0:T(8,128)(2,1)} %get-tuple-element.172), channel_id=1, source_target_pairs={{0,2},{1,3},{2,0},{3,1},{4,6},{5,7},{6,4},{7,5},{8,10},{9,11},{10,... | collective-permute-start | bytes 1671176 | tf_op jit(solution)/shard_map/ppermute | solution.py:946
  223.5 7.0 %collective-permute-start.27 = (bf16[1,106,256]{2,1,0:T(8,128)(2,1)S(1)}, bf16[1,106,256]{2,1,0:T(8,128)(2,1)S(1)}, u32[]{:S(2)}, u32[]{:S(2)}) collective-permute-start(bf16[1,106,256]{2,1,0:T(8,128)(2,1)S(1)} %get-tuple-element.221), channel_id=1, source_target_pairs={{0,8},{1,9},{2,10},{3,11},{4,12},{5,13},{6,14},{7,15},{8,0},{9,1},... | collective-permute-start | bytes 162824 | tf_op jit(solution)/shard_map/ppermute | solution.py:946
  223.6 6.9 %collective-permute-start.28 = (bf16[1,106,256]{2,1,0:T(8,128)(2,1)S(1)}, bf16[1,106,256]{2,1,0:T(8,128)(2,1)S(1)}, u32[]{:S(2)}, u32[]{:S(2)}) collective-permute-start(bf16[1,106,256]{2,1,0:T(8,128)(2,1)S(1)} %get-tuple-element.220), channel_id=1, source_target_pairs={{0,16},{1,17},{2,18},{3,19},{4,20},{5,21},{6,22},{7,23},{8,24},{9,... | collective-permute-start | bytes 162824 | tf_op jit(solution)/shard_map/ppermute | solution.py:946
  225.9 5.3 %collective-permute-start.29 = (bf16[1,106,256]{2,1,0:T(8,128)(2,1)S(1)}, bf16[1,106,256]{2,1,0:T(8,128)(2,1)S(1)}, u32[]{:S(2)}, u32[]{:S(2)}) collective-permute-start(bf16[1,106,256]{2,1,0:T(8,128)(2,1)S(1)} %get-tuple-element.219), channel_id=1, source_target_pairs={{0,24},{1,25},{2,26},{3,27},{4,28},{5,29},{6,30},{7,31},{8,16},{9,... | collective-permute-start | bytes 162824 | tf_op jit(solution)/shard_map/ppermute | solution.py:946
  (29 other events, 189.9 us)
Sparse Core Ops, SparseCore 0:
  12.3 71.8 all-gather.2
